TPU v7x, 768 devices: a whole 4x8x12 slice. The times are simulated.
768 devices in a mesh: dp: 12 (over z), fsdp: 64 (over x, y, core).
Axes of the slice: x: 4, y: 8, z: 12, core: 2. Of those that a mesh axis runs over, the one named last changes fastest.
Arguments:
- item_hidden: bfloat16 [49152, 2048], P(('dp', 'fsdp')), may hold values from -400 to 400
- item_gain: float32 [2048], replicated, may hold values from 0.25 to 1.75
- history: int32 [98304], P(('dp', 'fsdp')), may hold values from 0 to 767, as said below
- owner_map: int32 [64, 768], P('fsdp'), may hold values from 0 to 767, as said below
- user_gain: float32 [2048], replicated, may hold values from 0.25 to 1.75
- value_weight: bfloat16 [2048, 2048], P('fsdp'), may hold values from -0.125 to 0.125
- value_grad: bfloat16 [98304, 2048], P(('dp', 'fsdp')), may hold values from -6 to 6
Outputs:
- values: bfloat16 [98304, 2048], P(('dp', 'fsdp'))
- item_grad: float32 [49152, 2048], P(('dp', 'fsdp'))
Inputs may be any that keep to these rules, and one draw needn't show every extreme that they name: `history`: storage row s of catalog c is row s % 64 of the items on dp index s // 64 and fsdp index c. In each aligned block of 128 positions, the positions name at most 8 distinct items stored on any one dp index, and exactly 8 for some dp index. `owner_map`: each row is a permutation.
All inputs are finite; a program needn't handle non-finite values.
Results may differ from a plain program's by a relative error of at most 0.0057.
Values may be sent and summed in bfloat16 or wider, within the bound.
No kernel may reach another device: no remote copies, remote signals or barrier semaphores. Data moves between devices by JAX's collectives and lax.ppermute only.
A program may use at most 32 MiB of HBM per device.

v0:
```python
import jax
import jax.numpy as jnp
from jax import lax
from jax.sharding import PartitionSpec as P

CAP = 8


eps = 1e-06


def norm_rows(values, gain):
    scale = lax.rsqrt(jnp.mean(values * values, axis=1, keepdims=True) + eps)
    return (values * scale * gain, scale)


def norm_back(values, gain, scale, upstream):
    unit = values * scale
    scaled = upstream * gain
    return scale * (scaled - unit * jnp.mean(scaled * unit, axis=1, keepdims=True))


def locate(owner_row, items):
    matches = items[:, None] == lax.broadcasted_iota(
        jnp.int32, (items.shape[0], owner_row.shape[0]), 1
    )
    return jnp.sum(jnp.where(matches, owner_row[None, :], 0), axis=1)


def local(item_hidden, item_gain, history, owner_map, user_gain, value_weight, value_grad):
    groups = lax.axis_size("dp")
    here = lax.axis_index("dp")
    item_rows = item_hidden.shape[0]
    hist_rows = history.shape[0]
    width = item_hidden.shape[1]
    owner_row = owner_map[0]
    pool = owner_row.shape[0]
    hidden = item_hidden.astype(jnp.float32)
    item_emb, item_scale = norm_rows(hidden, item_gain)
    item_emb = item_emb.astype(jnp.bfloat16)
    all_history = lax.all_gather(history, "dp", axis=0, tiled=True)
    stored_all = locate(owner_row, all_history).reshape(groups, hist_rows)
    local_rows = lax.broadcasted_iota(jnp.int32, (groups, hist_rows, item_rows), 2)
    wanted = jnp.any(stored_all[:, :, None] == here * item_rows + local_rows, axis=1)
    slot = jnp.cumsum(wanted.astype(jnp.int32), axis=1) - 1
    slot_ids = lax.broadcasted_iota(jnp.int32, (groups, CAP, item_rows), 1)
    select = (wanted[:, None, :] & (slot[:, None, :] == slot_ids)).astype(jnp.bfloat16)
    outgoing = jnp.einsum(
        "dcr,rk->dck", select, item_emb, preferred_element_type=jnp.float32
    ).astype(jnp.bfloat16)
    incoming = lax.all_to_all(outgoing, "dp", split_axis=0, concat_axis=0, tiled=True)
    stored = locate(owner_row, history)
    pick = stored[:, None] == lax.broadcasted_iota(jnp.int32, (hist_rows, pool), 1)
    own_wanted = jnp.any(pick, axis=0).reshape(groups, item_rows)
    own_slot = (jnp.cumsum(own_wanted.astype(jnp.int32), axis=1) - 1).reshape(pool)
    slot_pos = jnp.sum(jnp.where(pick, own_slot[None, :], 0), axis=1)
    buffer_row = stored // item_rows * CAP + slot_pos
    x = jnp.take(incoming.reshape(groups * CAP, width), buffer_row, axis=0).astype(jnp.float32)
    normed, scale = norm_rows(x, user_gain)
    normed = normed.astype(jnp.bfloat16)
    whole = lax.all_gather(value_weight, "fsdp", axis=0, tiled=True)
    values = jnp.dot(normed, whole, preferred_element_type=jnp.float32)
    upstream = lax.dot_general(
        value_grad, whole, (((1,), (1,)), ((), ())), preferred_element_type=jnp.float32
    )
    values = values.astype(jnp.bfloat16)
    dx = norm_back(x, user_gain, scale, upstream)
    one_hot = (
        buffer_row[:, None] == lax.broadcasted_iota(jnp.int32, (hist_rows, groups * CAP), 1)
    ).astype(jnp.float32)
    summed = lax.dot_general(
        one_hot,
        dx,
        (((0,), (0,)), ((), ())),
        precision=lax.Precision.HIGHEST,
        preferred_element_type=jnp.float32,
    )
    returned = lax.all_to_all(
        summed.astype(jnp.bfloat16).reshape(groups, CAP, width),
        "dp",
        split_axis=0,
        concat_axis=0,
        tiled=True,
    )
    emb_grad = jnp.einsum("dcr,dck->rk", select, returned, preferred_element_type=jnp.float32)
    item_grad = norm_back(hidden, item_gain, item_scale, emb_grad)
    return (values, item_grad)


def solution(mesh):
    in_specs = (
        P(("dp", "fsdp"), None),
        P(),
        P(("dp", "fsdp")),
        P("fsdp", None),
        P(),
        P("fsdp", None),
        P(("dp", "fsdp"), None),
    )
    out_specs = (P(("dp", "fsdp"), None), P(("dp", "fsdp"), None))
    return jax.shard_map(local, mesh=mesh, in_specs=in_specs, out_specs=out_specs, check_vma=False)
```

profile of v0, /device:TPU:1, one launch (start us, length us, event | category | flops | bytes accessed | tf_op | source)
XLA Modules:
  0.0 158.2 jit_solution(1456072756796206151)
XLA Ops:
  7.2 0.0 copy-start
  7.2 0.0 all-gather.3.cloned.1.call-start
  7.2 0.7 all-gather.3.cloned.1.call-update
  7.9 0.7 reduce
  8.6 27.6 %all-gather = s32[12,1,128]{2,1,0:T(1,128)S(1)} all-gather(s32[1,1,128]{2,1,0:T(1,128)} %bitcast.35), channel_id=1, replica_groups=mesh['dp'=12,'fsdp'=64] {'dp'}, dimensions={0}, use_global_device_ids=true | all-gather | bytes 6656 | tf_op jit(solution)/shard_map/all_gather | solution.py:41
  36.3 0.8 select_reduce_fusion
  37.1 0.4 compare_reduce_fusion
  37.5 0.2 reduce_window_sum.18
  37.7 1.1 fusion.18
  38.9 2.0 %convolution_convert_fusion.2 = bf16[12,8,2048]{2,1,0:T(8,128)(2,1)} fusion(bf16[64,2048]{1,0:T(8,128)(2,1)} %param.7, f32[2048]{0:T(1024)} %param.8, f32[64]{0:T(128)S(1)} %add_rsqrt_fusion.1, pred[12,8,64]{2,0,1:T(8,128)(4,1)S(1)} %fusion.30), kind=kOutput, calls=%fused_computation.6 | convolution fusion | flops 25886720 | bytes 669952 | tf_op jit(solution)/shard_map/dcr,rk->dck/dot_general | solution.py:48
  40.9 3.6 %all-to-all-start = ((bf16[12,8,2048]{2,1,0:T(8,128)(2,1)}), bf16[12,8,2048]{2,1,0:T(8,128)(2,1)S(1)}, u32[]{:S(2)}, u32[]{:S(2)}) async-start(bf16[12,8,2048]{2,1,0:T(8,128)(2,1)} %convolution_convert_fusion.2), calls=%async_computation | async-start | bytes 786432 | tf_op jit(solution)/shard_map/all_to_all | solution.py:51
  44.5 0.8 select_reduce_fusion.2
  45.3 0.1 fusion.25
  45.5 0.1 reshape.140
  45.6 0.2 reduce_window_sum.17
  45.8 0.1 sub.24
  45.9 0.2 select_reduce_fusion.1
  46.1 13.5 %all-to-all-done = bf16[12,8,2048]{2,1,0:T(8,128)(2,1)S(1)} async-done(((bf16[12,8,2048]{2,1,0:T(8,128)(2,1)}), bf16[12,8,2048]{2,1,0:T(8,128)(2,1)S(1)}, u32[]{:S(2)}, u32[]{:S(2)}) %all-to-all-start) | async-done | bytes 393248 | tf_op jit(solution)/shard_map/all_to_all | solution.py:51
  59.6 0.9 gather_fusion
  60.6 0.3 fusion.10
  60.9 52.8 %all-gather.3.cloned.1.call-done = bf16[2048,2048]{1,0:T(8,128)(2,1)} async-done(((bf16[32,2048]{1,0:T(8,128)(2,1)}), bf16[2048,2048]{1,0:T(8,128)(2,1)}) %all-gather.3.cloned.1.call-update) | async-done | bytes 8388624 | tf_op jit(solution)/shard_map/all_gather | solution.py:61
  113.7 0.0 copy-done
  113.7 6.4 %fusion.6 = (f32[128]{0:T(128)S(1)}, f32[128,2048]{1,0:T(8,128)S(1)}) fusion(f32[128]{0:T(128)S(1)} %add_rsqrt_fusion, bf16[128,2048]{1,0:T(8,128)(2,1)S(1)} %gather_fusion, pred[128]{0:T(512)(128)(4,1)S(1)} %get-tuple-element.2, f32[2048]{0:T(1024)} %param.11, bf16[128,2048]{1,0:T(8,128)(2,1)S(1)} %copy-done, ...), kind=kOutput, calls=%fused_computation.16 | convolution fusion | flops 1075314560 | bytes 10495104 | tf_op jit(solution)/shard_map/dot_general | solution.py:63
  120.0 1.6 %fusion.1 = bf16[12,8,2048]{2,1,0:T(8,128)(2,1)} fusion(f32[128,2048]{1,0:T(8,128)S(1)} %get-tuple-element.5, f32[128]{0:T(128)S(1)} %broadcast_multiply_fusion, f32[128]{0:T(128)S(1)} %add_rsqrt_fusion, s32[128]{0:T(128)S(1)} %get-tuple-element.3, bf16[128,2048]{1,0:T(8,128)(2,1)S(1)} %gather_fusion, pred[128]{0:T(512)(128)(4,1)S(1)} %get-tuple-element.2), kind=kOutput, calls=%fused_computation.9 | convolution fusion | flops 303771648 | bytes 1967744 | tf_op jit(solution)/shard_map/dot_general | solution.py:71
  121.7 9.9 %all-to-all-start.1 = ((bf16[12,8,2048]{2,1,0:T(8,128)(2,1)}), bf16[12,8,2048]{2,1,0:T(8,128)(2,1)S(1)}, u32[]{:S(2)}, u32[]{:S(2)}) async-start(bf16[12,8,2048]{2,1,0:T(8,128)(2,1)} %fusion.1), calls=%async_computation.1 | async-start | bytes 786432 | tf_op jit(solution)/shard_map/all_to_all | solution.py:78
  131.6 0.0 copy-start.1
  131.6 0.0 copy-start.2
  131.6 5.5 %convolution_convert_fusion = bf16[128,2048]{1,0:T(8,128)(2,1)} fusion(bf16[2048,2048]{1,0:T(8,128)(2,1)} %all-gather.3.cloned.1.call-done, f32[2048]{0:T(1024)S(1)} %copy-done.3, f32[128]{0:T(128)S(1)} %add_rsqrt_fusion, bf16[128,2048]{1,0:T(8,128)(2,1)S(1)} %gather_fusion, pred[128]{0:T(512)(128)(4,1)S(1)} %get-tuple-element.2), kind=kOutput, calls=%fused_computation.4 | convolution fusion | flops 1075314688 | bytes 9446016 | tf_op jit(solution)/shard_map/dot_general | solution.py:62
  137.1 12.8 %all-to-all-done.1 = bf16[12,8,2048]{2,1,0:T(8,128)(2,1)S(1)} async-done(((bf16[12,8,2048]{2,1,0:T(8,128)(2,1)}), bf16[12,8,2048]{2,1,0:T(8,128)(2,1)S(1)}, u32[]{:S(2)}, u32[]{:S(2)}) %all-to-all-start.1) | async-done | bytes 393248 | tf_op jit(solution)/shard_map/all_to_all | solution.py:78
  149.9 0.0 copy-done.1
  149.9 0.5 fusion.15
  150.4 1.0 fusion.17
  (17 shorter events, 0.1 us)
Async XLA Ops:
  7.2 106.5 %copy-start = (bf16[128,2048]{1,0:T(8,128)(2,1)S(1)}, bf16[128,2048]{1,0:T(8,128)(2,1)}, u32[]{:S(2)}) copy-start(bf16[128,2048]{1,0:T(8,128)(2,1)} %param.13) | copy-start | bytes 1572868
  7.2 106.5 %all-gather.3.cloned.1.call-start = ((), (), s32[]{:S(2)}) async-start(), calls=%async_computation.2 | async-start | bytes 8519680 | tf_op jit(solution)/shard_map/all_gather | solution.py:61
  40.9 18.7 %all-to-all-start = ((bf16[12,8,2048]{2,1,0:T(8,128)(2,1)}), bf16[12,8,2048]{2,1,0:T(8,128)(2,1)S(1)}, u32[]{:S(2)}, u32[]{:S(2)}) async-start(bf16[12,8,2048]{2,1,0:T(8,128)(2,1)} %convolution_convert_fusion.2), calls=%async_computation | async-start | bytes 786432 | tf_op jit(solution)/shard_map/all_to_all | solution.py:51
  59.6 71.9 %copy-start.3 = (f32[2048]{0:T(1024)S(1)}, f32[2048]{0:T(1024)}, u32[]{:S(2)}) copy-start(f32[2048]{0:T(1024)} %param.11) | copy-start | bytes 24580
  121.7 28.3 %all-to-all-start.1 = ((bf16[12,8,2048]{2,1,0:T(8,128)(2,1)}), bf16[12,8,2048]{2,1,0:T(8,128)(2,1)S(1)}, u32[]{:S(2)}, u32[]{:S(2)}) async-start(bf16[12,8,2048]{2,1,0:T(8,128)(2,1)} %fusion.1), calls=%async_computation.1 | async-start | bytes 786432 | tf_op jit(solution)/shard_map/all_to_all | solution.py:78
  131.6 18.3 %copy-start.1 = (bf16[64,2048]{1,0:T(8,128)(2,1)S(1)}, bf16[64,2048]{1,0:T(8,128)(2,1)}, u32[]{:S(2)}) copy-start(bf16[64,2048]{1,0:T(8,128)(2,1)} %param.7) | copy-start | bytes 786436
  131.6 18.3 %copy-start.2 = (f32[2048]{0:T(1024)S(1)}, f32[2048]{0:T(1024)}, u32[]{:S(2)}) copy-start(f32[2048]{0:T(1024)} %param.8) | copy-start | bytes 24580
Sparse Core Ops, SparseCore 0:
  12.0 101.6 all-gather.2
where the time goes:
time: 160 us; the launch traced here: 158 us
  waiting for transfers between devices  79.8 us (50%)
  blocking collectives  27.6 us (17%)
  matrix products  16 us (10%)
  between operations  14.2 us (9%)
  starting transfers between devices  13.5 us (8%)
  other arithmetic  5.99 us (4%)
    all_gather x1, waiting for transfers between devices, local(): whole = lax.all_gather(value_weight, 'fsdp', axis=0, tiled=True)  52.8 us
    all_gather x1, blocking collectives, local(): all_history = lax.all_gather(history, 'dp', axis=0, tiled=True)  27.6 us
    all_to_all x1, waiting for transfers between devices, local(): lax.all_to_all(outgoing, 'dp', split_axis=0, concat_axis=0, tiled=True)  13.5 us
    all_to_all x1, waiting for transfers between devices, local(): lax.all_to_all(summed.astype(jnp.bfloat16).reshape(groups, CAP, width), '...  12.8 us
    all_to_all x1, starting transfers between devices, local(): lax.all_to_all(summed.astype(jnp.bfloat16).reshape(groups, CAP, width), '...  9.9 us
    dot_general x1, matrix products, local(): lax.dot_general(value_grad, whole, (((1,), (1,)), ((), ())), preferred_el...  6.36 us
    dot_general x1, matrix products, local(): values = jnp.dot(normed, whole, preferred_element_type=jnp.float32)  5.52 us
    all_to_all x1, starting transfers between devices, local(): lax.all_to_all(outgoing, 'dp', split_axis=0, concat_axis=0, tiled=True)  3.57 us
  transfers between devices with their start and end apart: 3, of which 3 were waited for; matrix products, arithmetic and copies ran while one was open for 9% of the time, Pallas kernels for 0%

commit v1 on v0

v1 whole, which is shorter than its diff:
```python
import jax
import jax.numpy as jnp
from jax import lax
from jax.sharding import PartitionSpec as P

CAP = 8


eps = 1e-06


def norm_rows(values, gain):
    scale = lax.rsqrt(jnp.mean(values * values, axis=1, keepdims=True) + eps)
    return (values * scale * gain, scale)


def norm_back(values, gain, scale, upstream):
    unit = values * scale
    scaled = upstream * gain
    return scale * (scaled - unit * jnp.mean(scaled * unit, axis=1, keepdims=True))


def locate(owner_row, items):
    matches = items[:, None] == lax.broadcasted_iota(
        jnp.int32, (items.shape[0], owner_row.shape[0]), 1
    )
    return jnp.sum(jnp.where(matches, owner_row[None, :], 0), axis=1)


def local(item_hidden, item_gain, history, owner_map, user_gain, value_weight, value_grad):
    groups = lax.axis_size("dp")
    here = lax.axis_index("dp")
    item_rows = item_hidden.shape[0]
    hist_rows = history.shape[0]
    width = item_hidden.shape[1]
    owner_row = owner_map[0]
    pool = owner_row.shape[0]
    whole = lax.all_gather(value_weight, "fsdp", axis=0, tiled=True)
    all_history = lax.all_gather(history, "dp", axis=0, tiled=True)
    hidden = item_hidden.astype(jnp.float32)
    item_emb, item_scale = norm_rows(hidden, item_gain)
    item_emb = item_emb.astype(jnp.bfloat16)
    stored = locate(owner_row, history)
    pick = stored[:, None] == lax.broadcasted_iota(jnp.int32, (hist_rows, pool), 1)
    own_wanted = jnp.any(pick, axis=0).reshape(groups, item_rows)
    own_slot = (jnp.cumsum(own_wanted.astype(jnp.int32), axis=1) - 1).reshape(pool)
    slot_pos = jnp.sum(jnp.where(pick, own_slot[None, :], 0), axis=1)
    buffer_row = stored // item_rows * CAP + slot_pos
    one_hot = (
        buffer_row[:, None] == lax.broadcasted_iota(jnp.int32, (hist_rows, groups * CAP), 1)
    ).astype(jnp.bfloat16)
    grad_sums = lax.dot_general(
        one_hot, value_grad, (((0,), (0,)), ((), ())), preferred_element_type=jnp.float32
    ).astype(jnp.bfloat16).reshape(groups, CAP, width)
    stored_all = locate(owner_row, all_history).reshape(groups, hist_rows)
    local_rows = lax.broadcasted_iota(jnp.int32, (groups, hist_rows, item_rows), 2)
    wanted = jnp.any(stored_all[:, :, None] == here * item_rows + local_rows, axis=1)
    slot = jnp.cumsum(wanted.astype(jnp.int32), axis=1) - 1
    slot_ids = lax.broadcasted_iota(jnp.int32, (groups, CAP, item_rows), 1)
    select = (wanted[:, None, :] & (slot[:, None, :] == slot_ids)).astype(jnp.bfloat16)
    outgoing = jnp.einsum(
        "dcr,rk->dck", select, item_emb, preferred_element_type=jnp.float32
    ).astype(jnp.bfloat16)
    arrived = lax.all_to_all(
        jnp.concatenate([outgoing, grad_sums], axis=1), "dp", split_axis=0, concat_axis=0, tiled=True
    )
    incoming = arrived[:, :CAP].reshape(groups * CAP, width)
    returned = arrived[:, CAP:]
    normed, _ = norm_rows(incoming.astype(jnp.float32), user_gain)
    normed = jnp.dot(
        one_hot, normed.astype(jnp.bfloat16), preferred_element_type=jnp.float32
    ).astype(jnp.bfloat16)
    total = jnp.einsum("dcr,dck->rk", select, returned, preferred_element_type=jnp.float32)
    high = lax.reduce_precision(total, 8, 7)
    both = jnp.concatenate([high, total - high], axis=0).astype(jnp.bfloat16)
    normed, both = lax.optimization_barrier((normed, both))
    values = jnp.dot(normed, whole, preferred_element_type=jnp.float32).astype(jnp.bfloat16)
    upstream = lax.dot_general(
        both, whole, (((1,), (1,)), ((), ())), preferred_element_type=jnp.float32
    )
    upstream = upstream[:item_rows] + upstream[item_rows:]
    x = item_emb.astype(jnp.float32)
    scale = lax.rsqrt(jnp.mean(x * x, axis=1, keepdims=True) + eps)
    emb_grad = norm_back(x, user_gain, scale, upstream)
    item_grad = norm_back(hidden, item_gain, item_scale, emb_grad)
    return (values, item_grad)


def solution(mesh):
    in_specs = (
        P(("dp", "fsdp"), None),
        P(),
        P(("dp", "fsdp")),
        P("fsdp", None),
        P(),
        P("fsdp", None),
        P(("dp", "fsdp"), None),
    )
    out_specs = (P(("dp", "fsdp"), None), P(("dp", "fsdp"), None))
    return jax.shard_map(local, mesh=mesh, in_specs=in_specs, out_specs=out_specs, check_vma=False)
```

time: 160 us -> 131 us (0.82)
  waiting for transfers between devices: 79.8 us -> 66.1 us
  starting transfers between devices: 13.5 us -> 3.69 us
  matrix products: 16 us -> 11 us
  other arithmetic: 5.99 us -> 7.92 us
    all_gather x1, waiting for transfers between devices: 52.8 us -> 42.6 us  [local(): whole = lax.all_gather(value_weight, 'fsdp', axis=0, tiled=True)]
    all_to_all x2 -> x1, starting transfers between devices: 13.5 us -> 3.65 us  [local(): lax.all_to_all(jnp.concatenate([outgoing, grad_sums], axis=1), 'dp', spli...]
    dot_general x3 -> x4, matrix products: 13.5 us -> 9.27 us  [the longest x1 6.4 us: local(): lax.dot_general(both, whole, (((1,), (1,)), ((), ())), preferred_element_...]
    all_to_all x2 -> x1, waiting for transfers between devices: 26.3 us -> 22.8 us  [local(): lax.all_to_all(jnp.concatenate([outgoing, grad_sums], axis=1), 'dp', spli...]
  transfers between devices with their start and end apart: 3 -> 2, of which waited for: 3 -> 2; matrix products, arithmetic and copies ran while one was open for 9% -> 7% of each run, Pallas kernels for 0% -> 0%
where the time goes in v1:
time: 131 us
  waiting for transfers between devices  66.1 us (50%)
  blocking collectives  27.6 us (21%)
  between operations  14.2 us (11%)
  matrix products  11 us (8%)
  other arithmetic  7.92 us (6%)
  starting transfers between devices  3.69 us (3%)
    all_gather x1, waiting for transfers between devices, local(): whole = lax.all_gather(value_weight, 'fsdp', axis=0, tiled=True)  42.6 us
    all_gather x1, blocking collectives, local(): all_history = lax.all_gather(history, 'dp', axis=0, tiled=True)  27.6 us
    all_to_all x1, waiting for transfers between devices, local(): lax.all_to_all(jnp.concatenate([outgoing, grad_sums], axis=1), 'dp', spli...  22.8 us
    dot_general x1, matrix products, local(): lax.dot_general(both, whole, (((1,), (1,)), ((), ())), preferred_element_...  6.4 us
    all_to_all x1, starting transfers between devices, local(): lax.all_to_all(jnp.concatenate([outgoing, grad_sums], axis=1), 'dp', spli...  3.65 us
  transfers between devices with their start and end apart: 2, of which 2 were waited for; matrix products, arithmetic and copies ran while one was open for 7% of the time, Pallas kernels for 0%

profile of v1, /device:TPU:1, one launch (start us, length us, event | category | flops | bytes accessed | tf_op | source)
XLA Modules:
  0.0 130.8 jit_solution(8346504820184171047)
XLA Ops:
  7.2 0.0 copy-start
  7.2 0.0 copy-start.3
  7.2 0.0 all-gather.3.cloned.1.call-start
  7.3 0.7 all-gather.3.cloned.1.call-update
  8.0 0.7 reduce.1
  8.7 0.8 select_reduce_fusion.2
  9.5 0.1 fusion.26
  9.7 0.1 reshape.99
  9.7 0.2 reduce_window_sum.17
  10.0 0.1 sub.25
  10.0 27.6 %all-gather = s32[12,1,128]{2,1,0:T(1,128)S(1)} all-gather(s32[1,1,128]{2,1,0:T(1,128)} %bitcast.26), channel_id=1, replica_groups=mesh['dp'=12,'fsdp'=64] {'dp'}, dimensions={0}, use_global_device_ids=true | all-gather | bytes 6656 | tf_op jit(solution)/shard_map/all_gather | solution.py:39
  37.7 0.8 select_reduce_fusion
  38.5 0.4 compare_reduce_fusion
  38.9 0.2 reduce_window_sum.18
  39.1 0.2 select_reduce_fusion.1
  39.3 1.1 fusion.18
  40.4 0.4 fusion
  40.9 1.3 convolution_convert_fusion.3
  42.2 1.0 pad_maximum_fusion
  43.2 3.6 %all-to-all-start = ((bf16[12,16,2048]{2,1,0:T(8,128)(2,1)}), bf16[12,16,2048]{2,1,0:T(8,128)(2,1)S(1)}, u32[]{:S(2)}, u32[]{:S(2)}) async-start(bf16[12,16,2048]{2,1,0:T(8,128)(2,1)} %pad_maximum_fusion), calls=%async_computation | async-start | bytes 1572864 | tf_op jit(solution)/shard_map/all_to_all | solution.py:64
  46.9 0.3 fusion.19
  47.1 22.8 %all-to-all-done = bf16[12,16,2048]{2,1,0:T(8,128)(2,1)S(1)} async-done(((bf16[12,16,2048]{2,1,0:T(8,128)(2,1)}), bf16[12,16,2048]{2,1,0:T(8,128)(2,1)S(1)}, u32[]{:S(2)}, u32[]{:S(2)}) %all-to-all-start) | async-done | bytes 786464 | tf_op jit(solution)/shard_map/all_to_all | solution.py:64
  69.9 0.2 fusion.4
  70.1 0.1 rsqrt.29
  70.2 0.4 reduce-precision_convert_fusion
  70.7 0.4 convolution_convert_fusion.1
  71.1 42.6 %all-gather.3.cloned.1.call-done = bf16[2048,2048]{1,0:T(8,128)(2,1)} async-done(((bf16[32,2048]{1,0:T(8,128)(2,1)}), bf16[2048,2048]{1,0:T(8,128)(2,1)}) %all-gather.3.cloned.1.call-update) | async-done | bytes 8388624 | tf_op jit(solution)/shard_map/all_gather | solution.py:38
  113.7 6.4 %fusion.36 = f32[128,2048]{1,0:T(8,128)S(1)} fusion(bf16[128,2048]{1,0:T(8,128)(2,1)S(1)} %pad_maximum_fusion.1, bf16[2048,2048]{1,0:T(8,128)(2,1)} %all-gather.3.cloned.1.call-done), kind=kOutput, calls=%fused_computation.70 | convolution fusion | flops 1073741824 | bytes 9961472 | tf_op jit(solution)/shard_map/dot_general | solution.py:78
  120.1 0.3 fusion.10
  120.4 0.3 fusion.15
  120.7 1.1 fusion.17
  121.8 2.1 %convolution_convert_fusion = bf16[128,2048]{1,0:T(8,128)(2,1)} fusion(bf16[128,2048]{1,0:T(8,128)(2,1)S(1)} %convolution_convert_fusion.1, bf16[2048,2048]{1,0:T(8,128)(2,1)S(1)} %copy-done.1), kind=kOutput, calls=%fused_computation.2 | convolution fusion | flops 1074003968 | bytes 9437184 | tf_op jit(solution)/shard_map/dot_general | solution.py:77
  (23 shorter events, 0.2 us)
Async XLA Ops:
  7.2 33.3 %copy-start = (bf16[128,2048]{1,0:T(8,128)(2,1)S(1)}, bf16[128,2048]{1,0:T(8,128)(2,1)}, u32[]{:S(2)}) copy-start(bf16[128,2048]{1,0:T(8,128)(2,1)} %param.13) | copy-start | bytes 1572868
  7.2 39.7 %copy-start.2 = (bf16[64,2048]{1,0:T(8,128)(2,1)S(1)}, bf16[64,2048]{1,0:T(8,128)(2,1)}, u32[]{:S(2)}) copy-start(bf16[64,2048]{1,0:T(8,128)(2,1)} %param.7) | copy-start | bytes 786436
  7.2 39.7 %copy-start.3 = (f32[2048]{0:T(1024)S(1)}, f32[2048]{0:T(1024)}, u32[]{:S(2)}) copy-start(f32[2048]{0:T(1024)} %param.8) | copy-start | bytes 24580
  7.2 63.5 %copy-start.4 = (f32[2048]{0:T(1024)S(1)}, f32[2048]{0:T(1024)}, u32[]{:S(2)}) copy-start(f32[2048]{0:T(1024)} %param.11) | copy-start | bytes 24580
  7.2 106.5 %all-gather.3.cloned.1.call-start = ((), (), s32[]{:S(2)}) async-start(), calls=%async_computation.1 | async-start | bytes 8519680 | tf_op jit(solution)/shard_map/all_gather | solution.py:38
  43.2 26.7 %all-to-all-start = ((bf16[12,16,2048]{2,1,0:T(8,128)(2,1)}), bf16[12,16,2048]{2,1,0:T(8,128)(2,1)S(1)}, u32[]{:S(2)}, u32[]{:S(2)}) async-start(bf16[12,16,2048]{2,1,0:T(8,128)(2,1)} %pad_maximum_fusion), calls=%async_computation | async-start | bytes 1572864 | tf_op jit(solution)/shard_map/all_to_all | solution.py:64
  113.7 8.1 %copy-start.1 = (bf16[2048,2048]{1,0:T(8,128)(2,1)S(1)}, bf16[2048,2048]{1,0:T(8,128)(2,1)}, u32[]{:S(2)}) copy-start(bf16[2048,2048]{1,0:T(8,128)(2,1)} %all-gather.3.cloned.1.call-done) | copy-start | bytes 25165828
Sparse Core Ops, SparseCore 0:
  12.0 101.6 all-gather.2

commit v2 on v1

v2 whole, which is shorter than its diff:
```python
import jax
import jax.numpy as jnp
from jax import lax
from jax.sharding import Mesh, PartitionSpec as P

CAP = 8
NX, NY, NCORE = 4, 8, 2
ROW = ("x", "y", "core")


eps = 1e-06


def norm_rows(values, gain):
    scale = lax.rsqrt(jnp.mean(values * values, axis=1, keepdims=True) + eps)
    return (values * scale * gain, scale)


def norm_back(values, gain, scale, upstream):
    unit = values * scale
    scaled = upstream * gain
    return scale * (scaled - unit * jnp.mean(scaled * unit, axis=1, keepdims=True))


def locate(owner_row, items):
    matches = items[:, None] == lax.broadcasted_iota(
        jnp.int32, (items.shape[0], owner_row.shape[0]), 1
    )
    return jnp.sum(jnp.where(matches, owner_row[None, :], 0), axis=1)


def dot(a, b, da=1, db=0):
    return lax.dot_general(a, b, (((da,), (db,)), ((), ())), preferred_element_type=jnp.float32)


def shift(a, axis, step):
    n = lax.axis_size(axis)
    return lax.ppermute(a, axis, [((i + step) % n, i) for i in range(n)])


def turned(a, start):
    twice = jnp.concatenate([a, a], axis=1)
    return lax.dynamic_slice_in_dim(twice, start, a.shape[1], axis=1)


def local(item_hidden, item_gain, history, owner_map, user_gain, value_weight, value_grad):
    groups = lax.axis_size("dp")
    item_rows, width = item_hidden.shape
    hist_rows = history.shape[0]
    half = width // 2
    block = width // NX
    core = lax.axis_index("core")
    color = (lax.axis_index("x") + 2 * (lax.axis_index("dp") % 2)) % NX

    seed = lax.ppermute(
        value_weight,
        ("dp", "x"),
        [(z * NX + (x + 2 * (z % 2)) % NX, z * NX + x) for z in range(groups) for x in range(NX)],
    )
    owner_row = owner_map[0]
    pool = owner_row.shape[0]
    stored = locate(owner_row, history)
    pick = stored[:, None] == lax.broadcasted_iota(jnp.int32, (hist_rows, pool), 1)
    wanted = jnp.any(pick, axis=0).reshape(groups, item_rows)
    slot = jnp.cumsum(wanted.astype(jnp.int32), axis=1) - 1
    slot_pos = jnp.sum(jnp.where(pick, slot.reshape(1, pool), 0), axis=1)
    buffer_row = stored // item_rows * CAP + slot_pos
    one_hot = (
        buffer_row[:, None] == lax.broadcasted_iota(jnp.int32, (hist_rows, groups * CAP), 1)
    ).astype(jnp.bfloat16)
    grad_sums = dot(one_hot, value_grad, 0, 0).astype(jnp.bfloat16).reshape(groups, CAP, width)
    slot_ids = lax.broadcasted_iota(jnp.int32, (groups, CAP, item_rows), 1)
    asked = (wanted[:, None, :] & (slot[:, None, :] == slot_ids)).astype(jnp.bfloat16)
    asked = jnp.pad(asked, ((0, 0), (0, 0), (0, -item_rows % 128)))
    sent, seed = lax.optimization_barrier((jnp.concatenate([grad_sums, asked], axis=2), seed))
    arrived = lax.all_to_all(sent, "dp", split_axis=0, concat_axis=0, tiled=True)
    arrived = arrived.reshape(groups * CAP, -1)
    column = lax.all_gather(seed, ("y", "core"), axis=0, tiled=True)
    select = arrived[:, width : width + item_rows]

    hidden = item_hidden.astype(jnp.float32)
    item_emb, item_scale = norm_rows(hidden, item_gain)
    item_emb = item_emb.astype(jnp.bfloat16)
    outgoing = dot(select, item_emb).astype(jnp.bfloat16).reshape(groups, CAP, width)
    incoming = lax.all_to_all(outgoing, "dp", split_axis=0, concat_axis=0, tiled=True)

    mine = lax.dynamic_slice(column, (0, core * half), (block, half))
    rows = block // 2
    one_a, one_b = shift(mine[:rows], "x", 1), shift(mine[rows:], "x", 1)
    three_a, three_b = shift(mine[:rows], "x", -1), shift(mine[rows:], "x", -1)
    two_a = shift(mine[:rows], "dp", 1)
    two_b = shift(mine[rows:], "dp", -1)
    incoming, one_a, three_a, two_a, two_b = lax.optimization_barrier(
        (incoming, one_a, three_a, two_a, two_b)
    )

    total = dot(select, arrived[:, :width], 0, 0)
    high = lax.reduce_precision(total, 8, 7)
    both = jnp.concatenate([high, total - high], axis=0).astype(jnp.bfloat16)
    low_half, high_half = both[:, :half], both[:, half:]
    own = jnp.where(core == 0, low_half, high_half)
    swap = [(0, 1), (1, 0)]
    other = lax.ppermute(jnp.where(core == 0, high_half, low_half), "core", swap)
    grads = jnp.concatenate([own, other], axis=0)

    normed, _ = norm_rows(incoming.reshape(groups * CAP, width).astype(jnp.float32), user_gain)
    normed = dot(one_hot, normed.astype(jnp.bfloat16)).astype(jnp.bfloat16)
    normed = turned(normed, color * block)
    normed = jnp.concatenate([normed, lax.ppermute(normed, "core", swap)], axis=0)

    pieces = [
        (0, mine),
        (2 * block, two_a),
        (2 * block + rows, two_b),
        (block, one_a),
        (3 * block, three_a),
        (block + rows, one_b),
        (3 * block + rows, three_b),
    ]
    values = sum(dot(normed[:, at : at + p.shape[0]], p) for at, p in pieces)
    upstream = {at: dot(grads, p, 1, 1) for at, p in pieces}
    upstream = jnp.concatenate([upstream[at] for at in sorted(upstream)], axis=1)
    upstream = upstream.reshape(2, 2, item_rows, width)
    upstream = upstream[:, 0] + upstream[:, 1]
    values = values.astype(jnp.bfloat16).reshape(2, hist_rows, half)
    upstream = upstream[0] + lax.ppermute(upstream[1], "core", swap)
    theirs = lax.ppermute(values[1], "core", swap)
    values = jnp.where(
        core == 0,
        jnp.concatenate([values[0], theirs], axis=1),
        jnp.concatenate([theirs, values[0]], axis=1),
    )

    upstream = turned(upstream, (NX - color) % NX * block)
    x = item_emb.astype(jnp.float32)
    scale = lax.rsqrt(jnp.mean(x * x, axis=1, keepdims=True) + eps)
    emb_grad = norm_back(x, user_gain, scale, upstream)
    item_grad = norm_back(hidden, item_gain, item_scale, emb_grad)
    return (values, item_grad)


def solution(mesh):
    groups = mesh.shape["dp"]
    mesh = Mesh(mesh.devices.reshape(groups, NX, NY, NCORE), ("dp",) + ROW)
    everywhere = ("dp",) + ROW
    in_specs = (
        P(everywhere, None),
        P(),
        P(everywhere),
        P(ROW, None),
        P(),
        P(ROW, None),
        P(everywhere, None),
    )
    out_specs = (P(everywhere, None), P(everywhere, None))
    return jax.shard_map(local, mesh=mesh, in_specs=in_specs, out_specs=out_specs, check_vma=False)
```

time: 131 us -> 145 us (1.11)
  starting transfers between devices: 3.69 us -> 57.9 us
  waiting for transfers between devices: 66.1 us -> 32.9 us
  blocking collectives: 27.6 us -> 0 us
  matrix products: 11 us -> 25.1 us
  local copies, waits for them, and re-layouts: 0.28 us -> 4.18 us
    all_gather x1, waiting for transfers between devices: 42.6 us -> 8.53 us  [local(): column = lax.all_gather(seed, ('y', 'core'), axis=0, tiled=True)]
    ppermute x0 -> x11, starting transfers between devices: none -> 33.1 us  [the longest x6 20.9 us: shift(): return lax.ppermute(a, axis, [((i + step) % n, i) for i in range(n)])]
    all_gather x1 -> x0, blocking collectives: 27.6 us -> none  [local(): all_history = lax.all_gather(history, 'dp', axis=0, tiled=True)]
    all_to_all x1 -> x2, starting transfers between devices: 3.65 us -> 24.7 us  [the longest x1 18.8 us: local(): lax.all_to_all(sent, 'dp', split_axis=0, concat_axis=0, tiled=True)]
    dot_general x6 -> x18, matrix products: 11 us -> 25.1 us  [dot(): lax.dot_general(a, b, (((da,), (db,)), ((), ())), preferred_element_type=...]
    ppermute x0 -> x11, waiting for transfers between devices: none -> 6.41 us  [the longest x6 4.99 us: shift(): return lax.ppermute(a, axis, [((i + step) % n, i) for i in range(n)])]
    all_to_all x1 -> x2, waiting for transfers between devices: 22.8 us -> 18 us  [the longest x1 18 us: local(): lax.all_to_all(sent, 'dp', split_axis=0, concat_axis=0, tiled=True)]
    slice x1 -> x2, local copies, waits for them, and re-layouts: 0.03 us -> 2.42 us  [the longest x1 2.38 us: local(): one_a, one_b = (shift(mine[:rows], 'x', 1), shift(mine[rows:], 'x', 1))]
  transfers between devices with their start and end apart: 2 -> 14, of which waited for: 2 -> 5; matrix products, arithmetic and copies ran while one was open for 7% -> 17% of each run, Pallas kernels for 0% -> 0%
where the time goes in v2:
time: 145 us; the launch traced here: 144 us
  starting transfers between devices  57.9 us (40%)
  waiting for transfers between devices  32.9 us (23%)
  matrix products  25.1 us (17%)
  between operations  14.5 us (10%)
  other arithmetic  9.05 us (6%)
  local copies, waits for them, and re-layouts  4.18 us (3%)
    dot_general x18, matrix products, dot(): lax.dot_general(a, b, (((da,), (db,)), ((), ())), preferred_element_type=...  25.1 us
    ppermute x6, starting transfers between devices, shift(): return lax.ppermute(a, axis, [((i + step) % n, i) for i in range(n)])  20.9 us
    all_to_all x1, starting transfers between devices, local(): lax.all_to_all(sent, 'dp', split_axis=0, concat_axis=0, tiled=True)  18.8 us
    all_to_all x1, waiting for transfers between devices, local(): lax.all_to_all(sent, 'dp', split_axis=0, concat_axis=0, tiled=True)  18 us
    all_gather x1, waiting for transfers between devices, local(): column = lax.all_gather(seed, ('y', 'core'), axis=0, tiled=True)  8.53 us
    all_to_all x1, starting transfers between devices, local(): lax.all_to_all(outgoing, 'dp', split_axis=0, concat_axis=0, tiled=True)  5.9 us
    ppermute x6, waiting for transfers between devices, shift(): return lax.ppermute(a, axis, [((i + step) % n, i) for i in range(n)])  4.99 us
    ppermute x1, starting transfers between devices, local(): upstream = upstream[0] + lax.ppermute(upstream[1], 'core', swap)  3.61 us
  transfers between devices with their start and end apart: 14, of which 5 were waited for; matrix products, arithmetic and copies ran while one was open for 17% of the time, Pallas kernels for 0%

profile of v2, /device:TPU:1, one launch (start us, length us, event | category | flops | bytes accessed | tf_op | source)
XLA Modules:
  0.0 143.6 jit_solution(17741780149530891754)
XLA Ops:
  7.2 1.7 %collective-permute-start = (bf16[32,2048]{1,0:T(8,128)(2,1)}, bf16[32,2048]{1,0:T(8,128)(2,1)S(1)}, u32[]{:S(2)}, u32[]{:S(2)}) collective-permute-start(bf16[32,2048]{1,0:T(8,128)(2,1)} %param.12), channel_id=1, source_target_pairs={{0,0},{16,16},{32,32},{48,48},{96,64},{112,80},{64,96},{80,112},{1... | collective-permute-start | bytes 393224 | tf_op jit(solution)/shard_map/ppermute | solution.py:55
  13.2 18.8 %all-to-all-start = ((bf16[12,8,2176]{2,1,0:T(8,128)(2,1)}), bf16[12,8,2176]{2,1,0:T(8,128)(2,1)S(1)}, u32[]{:S(2)}, u32[]{:S(2)}) async-start(bf16[12,8,2176]{2,1,0:T(8,128)(2,1)} %pad_maximum_fusion.1), calls=%async_computation | async-start | bytes 835584 | tf_op jit(solution)/shard_map/all_to_all | solution.py:76
  32.2 18.0 %all-to-all-done = bf16[12,8,2176]{2,1,0:T(8,128)(2,1)S(1)} async-done(((bf16[12,8,2176]{2,1,0:T(8,128)(2,1)}), bf16[12,8,2176]{2,1,0:T(8,128)(2,1)S(1)}, u32[]{:S(2)}, u32[]{:S(2)}) %all-to-all-start) | async-done | bytes 417824 | tf_op jit(solution)/shard_map/all_to_all | solution.py:76
  50.1 1.1 fusion.1
  51.2 5.9 %all-to-all-start.1 = ((bf16[12,8,2048]{2,1,0:T(8,128)(2,1)}), bf16[12,8,2048]{2,1,0:T(8,128)(2,1)S(1)}, u32[]{:S(2)}, u32[]{:S(2)}) async-start(bf16[12,8,2048]{2,1,0:T(8,128)(2,1)} %fusion.1), calls=%async_computation.1 | async-start | bytes 786432 | tf_op jit(solution)/shard_map/all_to_all | solution.py:85
  58.2 2.9 %collective-permute-start.9 = (bf16[128,1024]{1,0:T(8,128)(2,1)}, bf16[128,1024]{1,0:T(8,128)(2,1)}, u32[]{:S(2)}, u32[]{:S(2)}) collective-permute-start(bf16[128,1024]{1,0:T(8,128)(2,1)} %get-tuple-element.21), channel_id=1, source_target_pairs={{0,1},{1,0},{2,3},{3,2},{4,5},{5,4},{6,7},{7,6},{8,9},{9,8},{10,11... | collective-permute-start | bytes 786440 | tf_op jit(solution)/shard_map/ppermute | solution.py:103
  61.1 8.5 %all-gather.2.cloned.1.call-done = bf16[512,2048]{1,0:T(8,128)(2,1)} async-done(((bf16[32,2048]{1,0:T(8,128)(2,1)}), bf16[512,2048]{1,0:T(8,128)(2,1)}) %all-gather.2.cloned.1.call-update) | async-done | bytes 2097168 | tf_op jit(solution)/shard_map/all_gather | solution.py:78
  69.7 2.4 %constant_dynamic-slice_fusion = (bf16[256,1024]{1,0:T(8,128)(2,1)}, bf16[256,1024]{1,0:T(8,128)(2,1)}) fusion(bf16[512,2048]{1,0:T(8,128)(2,1)} %all-gather.2.cloned.1.call-done, s32[]{:T(128)S(6)} %select_n.64, s32[]{:T(128)S(6)} %add.118), kind=kLoop, calls=%fused_computation.115 | loop fusion | bytes 2097160 | tf_op jit(solution)/shard_map/slice | solution.py:89
  72.1 4.3 %collective-permute-start.1 = (bf16[256,1024]{1,0:T(8,128)(2,1)}, bf16[256,1024]{1,0:T(8,128)(2,1)}, u32[]{:S(2)}, u32[]{:S(2)}) collective-permute-start(bf16[256,1024]{1,0:T(8,128)(2,1)} %get-tuple-element.18), channel_id=1, source_target_pairs={{16,0},{32,16},{48,32},{0,48},{17,1},{33,17},{49,33},{1,49},{18,2}... | collective-permute-start | bytes 1572872 | tf_op jit(solution)/shard_map/ppermute | solution.py:38
  76.4 1.9 %collective-permute-start.2 = (bf16[256,1024]{1,0:T(8,128)(2,1)}, bf16[256,1024]{1,0:T(8,128)(2,1)}, u32[]{:S(2)}, u32[]{:S(2)}) collective-permute-start(bf16[256,1024]{1,0:T(8,128)(2,1)} %get-tuple-element.18), channel_id=1, source_target_pairs={{48,0},{0,16},{16,32},{32,48},{49,1},{1,17},{17,33},{33,49},{50,2}... | collective-permute-start | bytes 1572872 | tf_op jit(solution)/shard_map/ppermute | solution.py:38
  78.3 6.3 %collective-permute-start.3 = (bf16[256,1024]{1,0:T(8,128)(2,1)}, bf16[256,1024]{1,0:T(8,128)(2,1)}, u32[]{:S(2)}, u32[]{:S(2)}) collective-permute-start(bf16[256,1024]{1,0:T(8,128)(2,1)} %get-tuple-element.18), channel_id=1, source_target_pairs={{64,0},{128,64},{192,128},{256,192},{320,256},{384,320},{448,384},... | collective-permute-start | bytes 1572872 | tf_op jit(solution)/shard_map/ppermute | solution.py:38
  84.6 1.9 %collective-permute-start.4 = (bf16[256,1024]{1,0:T(8,128)(2,1)}, bf16[256,1024]{1,0:T(8,128)(2,1)}, u32[]{:S(2)}, u32[]{:S(2)}) collective-permute-start(bf16[256,1024]{1,0:T(8,128)(2,1)} %get-tuple-element.19), channel_id=1, source_target_pairs={{704,0},{0,64},{64,128},{128,192},{192,256},{256,320},{320,384},{3... | collective-permute-start | bytes 1572872 | tf_op jit(solution)/shard_map/ppermute | solution.py:38
  86.8 4.6 %collective-permute-start.6 = (bf16[256,1024]{1,0:T(8,128)(2,1)}, bf16[256,1024]{1,0:T(8,128)(2,1)}, u32[]{:S(2)}, u32[]{:S(2)}) collective-permute-start(bf16[256,1024]{1,0:T(8,128)(2,1)} %get-tuple-element.19), channel_id=1, source_target_pairs={{16,0},{32,16},{48,32},{0,48},{17,1},{33,17},{49,33},{1,49},{18,2}... | collective-permute-start | bytes 1572872 | tf_op jit(solution)/shard_map/ppermute | solution.py:38
  91.5 2.3 %convolution_dynamic-update-slice_fusion = f32[256,2048]{1,0:T(8,128)} fusion(bf16[512,2048]{1,0:T(8,128)(2,1)S(1)} %copy-done.2, s32[]{:T(128)S(6)} %select_n.64, bf16[128,1024]{1,0:T(8,128)(2,1)} %collective-permute-done.9, bf16[128,1024]{1,0:T(8,128)(2,1)S(1)} %get-tuple-element.20), kind=kOutput, calls=%fused_computation.24 | convolution fusion | flops 269484032 | bytes 2097156 | tf_op jit(solution)/shard_map/dot_general | solution.py:33
  93.7 1.9 %collective-permute-start.7 = (bf16[256,1024]{1,0:T(8,128)(2,1)}, bf16[256,1024]{1,0:T(8,128)(2,1)S(1)}, u32[]{:S(2)}, u32[]{:S(2)}) collective-permute-start(bf16[256,1024]{1,0:T(8,128)(2,1)} %get-tuple-element.19), channel_id=1, source_target_pairs={{48,0},{0,16},{16,32},{32,48},{49,1},{1,17},{17,33},{33,49},{50,2}... | collective-permute-start | bytes 1572872 | tf_op jit(solution)/shard_map/ppermute | solution.py:38
  95.7 5.0 %collective-permute-done.4 = bf16[256,1024]{1,0:T(8,128)(2,1)} collective-permute-done((bf16[256,1024]{1,0:T(8,128)(2,1)}, bf16[256,1024]{1,0:T(8,128)(2,1)}, u32[]{:S(2)}, u32[]{:S(2)}) %collective-permute-start.4) | collective-permute-done | bytes 524320 | tf_op jit(solution)/shard_map/ppermute | solution.py:38
  100.6 2.2 %convolution_dynamic-update-slice_fusion.6 = f32[256,2048]{1,0:T(8,128)} fusion(f32[256,2048]{1,0:T(8,128)} %convolution_dynamic-update-slice_fusion, bf16[256,1024]{1,0:T(8,128)(2,1)} %collective-permute-done.1, bf16[128,1024]{1,0:T(8,128)(2,1)} %collective-permute-done.9, bf16[128,1024]{1,0:T(8,128)(2,1)S(1)} %get-tuple-element.20), kind=kOutput, calls=%fused_computation.30 | convolution fusion | flops 135266304 | bytes 1310720 | tf_op jit(solution)/shard_map/dot_general | solution.py:33
  102.9 2.2 %convolution_dynamic-update-slice_fusion.5 = f32[256,2048]{1,0:T(8,128)} fusion(f32[256,2048]{1,0:T(8,128)} %convolution_dynamic-update-slice_fusion.6, bf16[256,1024]{1,0:T(8,128)(2,1)} %collective-permute-done.6, bf16[128,1024]{1,0:T(8,128)(2,1)} %collective-permute-done.9, bf16[128,1024]{1,0:T(8,128)(2,1)S(1)} %get-tuple-element.20), kind=kOutput, calls=%fused_computation.29 | convolution fusion | flops 135266304 | bytes 1310720 | tf_op jit(solution)/shard_map/dot_general | solution.py:33
  105.1 2.2 %convolution_dynamic-update-slice_fusion.4 = f32[256,2048]{1,0:T(8,128)} fusion(f32[256,2048]{1,0:T(8,128)} %convolution_dynamic-update-slice_fusion.5, bf16[256,1024]{1,0:T(8,128)(2,1)} %collective-permute-done.3, bf16[128,1024]{1,0:T(8,128)(2,1)} %collective-permute-done.9, bf16[128,1024]{1,0:T(8,128)(2,1)S(1)} %get-tuple-element.20), kind=kOutput, calls=%fused_computation.28 | convolution fusion | flops 135266304 | bytes 1310720 | tf_op jit(solution)/shard_map/dot_general | solution.py:33
  107.3 2.2 %convolution_dynamic-update-slice_fusion.3 = f32[256,2048]{1,0:T(8,128)} fusion(f32[256,2048]{1,0:T(8,128)} %convolution_dynamic-update-slice_fusion.4, bf16[256,1024]{1,0:T(8,128)(2,1)} %collective-permute-done.4, bf16[128,1024]{1,0:T(8,128)(2,1)} %collective-permute-done.9, bf16[128,1024]{1,0:T(8,128)(2,1)S(1)} %get-tuple-element.20), kind=kOutput, calls=%fused_computation.27 | convolution fusion | flops 135266304 | bytes 1310720 | tf_op jit(solution)/shard_map/dot_general | solution.py:33
  109.5 2.2 %convolution_dynamic-update-slice_fusion.2 = f32[256,2048]{1,0:T(8,128)} fusion(f32[256,2048]{1,0:T(8,128)} %convolution_dynamic-update-slice_fusion.3, bf16[256,1024]{1,0:T(8,128)(2,1)} %collective-permute-done.2, bf16[128,1024]{1,0:T(8,128)(2,1)} %collective-permute-done.9, bf16[128,1024]{1,0:T(8,128)(2,1)S(1)} %get-tuple-element.20), kind=kOutput, calls=%fused_computation.26 | convolution fusion | flops 135266304 | bytes 1310720 | tf_op jit(solution)/shard_map/dot_general | solution.py:33
  111.7 2.0 %convolution_dynamic-update-slice_fusion.1 = f32[256,2048]{1,0:T(8,128)} fusion(f32[256,2048]{1,0:T(8,128)} %convolution_dynamic-update-slice_fusion.2, bf16[256,1024]{1,0:T(8,128)(2,1)S(1)} %collective-permute-done.7, bf16[128,1024]{1,0:T(8,128)(2,1)} %collective-permute-done.9, bf16[128,1024]{1,0:T(8,128)(2,1)S(1)} %get-tuple-element.20), kind=kOutput, calls=%fused_computation.25 | convolution fusion | flops 135266304 | bytes 1310720 | tf_op jit(solution)/shard_map/dot_general | solution.py:33
  113.7 1.7 %slice_add_fusion = f32[2,1,64,2048]{3,2,1,0:T(8,128)S(1)} fusion(f32[2,2,64,2048]{3,2,1,0:T(8,128)} %bitcast.34), kind=kLoop, calls=%fused_computation.31 | loop fusion | flops 262144 | bytes 3145728 | tf_op jit(solution)/shard_map/add | solution.py:124
  116.2 3.6 %collective-permute-start.10 = (f32[64,2048]{1,0:T(8,128)}, f32[64,2048]{1,0:T(8,128)S(1)}, u32[]{:S(2)}, u32[]{:S(2)}) collective-permute-start(f32[64,2048]{1,0:T(8,128)} %slice_bitcast_fusion), channel_id=1, source_target_pairs={{0,1},{1,0},{2,3},{3,2},{4,5},{5,4},{6,7},{7,6},{8,9},{9,8},{10,11... | collective-permute-start | bytes 1572872 | tf_op jit(solution)/shard_map/ppermute | solution.py:126
  120.8 1.9 %collective-permute-start.5 = (bf16[128,2048]{1,0:T(8,128)(2,1)S(1)}, bf16[128,2048]{1,0:T(8,128)(2,1)S(1)}, u32[]{:S(2)}, u32[]{:S(2)}) collective-permute-start(bf16[128,2048]{1,0:T(8,128)(2,1)S(1)} %fusion.32), channel_id=1, source_target_pairs={{0,1},{1,0},{2,3},{3,2},{4,5},{5,4},{6,7},{7,6},{8,9},{9,8},{10,11... | collective-permute-start | bytes 1572872 | tf_op jit(solution)/shard_map/ppermute | solution.py:109
  123.5 1.1 collective-permute-done.5
  124.6 1.3 fusion.50
  125.9 1.3 fusion.52
  127.3 1.3 fusion.54
  128.6 1.3 fusion.56
  130.0 1.5 %fusion.48 = f32[256,1024]{1,0:T(8,128)S(1)} fusion(bf16[256,1024]{1,0:T(8,128)(2,1)} %collective-permute-done.6, bf16[128,2048]{1,0:T(8,128)(2,1)S(1)} %fusion.32, bf16[128,2048]{1,0:T(8,128)(2,1)S(1)} %collective-permute-done.5), kind=kOutput, calls=%fused_computation.96 | convolution fusion | flops 134479872 | bytes 2621440 | tf_op jit(solution)/shard_map/dot_general | solution.py:33
  132.4 2.0 %collective-permute-start.8 = (bf16[128,1024]{1,0:T(8,128)(2,1)S(1)}, bf16[128,1024]{1,0:T(8,128)(2,1)S(1)}, u32[]{:S(2)}, u32[]{:S(2)}) collective-permute-start(bf16[128,1024]{1,0:T(8,128)(2,1)S(1)} %get-tuple-element.25), channel_id=1, source_target_pairs={{0,1},{1,0},{2,3},{3,2},{4,5},{5,4},{6,7},{7,6},{8,9},{9,8},{10,11... | collective-permute-start | bytes 786440 | tf_op jit(solution)/shard_map/ppermute | solution.py:127
  (66 shorter events, 11.4 us)
Async XLA Ops:
  7.2 4.1 %copy-start = (bf16[128,2048]{1,0:T(8,128)(2,1)S(1)}, bf16[128,2048]{1,0:T(8,128)(2,1)}, u32[]{:S(2)}) copy-start(bf16[128,2048]{1,0:T(8,128)(2,1)} %param.13) | copy-start | bytes 1572868
  7.2 24.8 %copy-start.1 = (bf16[64,2048]{1,0:T(8,128)(2,1)S(1)}, bf16[64,2048]{1,0:T(8,128)(2,1)}, u32[]{:S(2)}) copy-start(bf16[64,2048]{1,0:T(8,128)(2,1)} %param.7) | copy-start | bytes 786436
  7.2 42.9 %copy-start.4 = (f32[2048]{0:T(1024)S(1)}, f32[2048]{0:T(1024)}, u32[]{:S(2)}) copy-start(f32[2048]{0:T(1024)} %param.8) | copy-start | bytes 24580
  7.2 62.5 %all-gather.2.cloned.1.call-start = ((), (), s32[]{:S(2)}) async-start(), calls=%async_computation.2 | async-start | bytes 2228224 | tf_op jit(solution)/shard_map/all_gather | solution.py:78
  7.2 5.2 %collective-permute-start = (bf16[32,2048]{1,0:T(8,128)(2,1)}, bf16[32,2048]{1,0:T(8,128)(2,1)S(1)}, u32[]{:S(2)}, u32[]{:S(2)}) collective-permute-start(bf16[32,2048]{1,0:T(8,128)(2,1)} %param.12), channel_id=1, source_target_pairs={{0,0},{16,16},{32,32},{48,48},{96,64},{112,80},{64,96},{80,112},{1... | collective-permute-start | bytes 393224 | tf_op jit(solution)/shard_map/ppermute | solution.py:55
  11.3 40.0 %copy-start.7 = (s32[128]{0:T(128)}, s32[128]{0:T(128)S(1)}, u32[]{:S(2)}) copy-start(s32[128]{0:T(128)S(1)} %multiply_add_fusion) | copy-start | bytes 1540
  12.5 0.7 copy-start.5
  13.2 37.0 %all-to-all-start = ((bf16[12,8,2176]{2,1,0:T(8,128)(2,1)}), bf16[12,8,2176]{2,1,0:T(8,128)(2,1)S(1)}, u32[]{:S(2)}, u32[]{:S(2)}) async-start(bf16[12,8,2176]{2,1,0:T(8,128)(2,1)} %pad_maximum_fusion.1), calls=%async_computation | async-start | bytes 835584 | tf_op jit(solution)/shard_map/all_to_all | solution.py:76
  51.2 44.4 %all-to-all-start.1 = ((bf16[12,8,2048]{2,1,0:T(8,128)(2,1)}), bf16[12,8,2048]{2,1,0:T(8,128)(2,1)S(1)}, u32[]{:S(2)}, u32[]{:S(2)}) async-start(bf16[12,8,2048]{2,1,0:T(8,128)(2,1)} %fusion.1), calls=%async_computation.1 | async-start | bytes 786432 | tf_op jit(solution)/shard_map/all_to_all | solution.py:85
  58.2 28.6 %collective-permute-start.9 = (bf16[128,1024]{1,0:T(8,128)(2,1)}, bf16[128,1024]{1,0:T(8,128)(2,1)}, u32[]{:S(2)}, u32[]{:S(2)}) collective-permute-start(bf16[128,1024]{1,0:T(8,128)(2,1)} %get-tuple-element.21), channel_id=1, source_target_pairs={{0,1},{1,0},{2,3},{3,2},{4,5},{5,4},{6,7},{7,6},{8,9},{9,8},{10,11... | collective-permute-start | bytes 786440 | tf_op jit(solution)/shard_map/ppermute | solution.py:103
  69.7 21.8 %copy-start.2 = (bf16[512,2048]{1,0:T(8,128)(2,1)S(1)}, bf16[512,2048]{1,0:T(8,128)(2,1)}, u32[]{:S(2)}) copy-start(bf16[512,2048]{1,0:T(8,128)(2,1)} %all-gather.2.cloned.1.call-done) | copy-start | bytes 6291460
  72.1 21.7 %collective-permute-start.1 = (bf16[256,1024]{1,0:T(8,128)(2,1)}, bf16[256,1024]{1,0:T(8,128)(2,1)}, u32[]{:S(2)}, u32[]{:S(2)}) collective-permute-start(bf16[256,1024]{1,0:T(8,128)(2,1)} %get-tuple-element.18), channel_id=1, source_target_pairs={{16,0},{32,16},{48,32},{0,48},{17,1},{33,17},{49,33},{1,49},{18,2}... | collective-permute-start | bytes 1572872 | tf_op jit(solution)/shard_map/ppermute | solution.py:38
  76.4 19.3 %collective-permute-start.2 = (bf16[256,1024]{1,0:T(8,128)(2,1)}, bf16[256,1024]{1,0:T(8,128)(2,1)}, u32[]{:S(2)}, u32[]{:S(2)}) collective-permute-start(bf16[256,1024]{1,0:T(8,128)(2,1)} %get-tuple-element.18), channel_id=1, source_target_pairs={{48,0},{0,16},{16,32},{32,48},{49,1},{1,17},{17,33},{33,49},{50,2}... | collective-permute-start | bytes 1572872 | tf_op jit(solution)/shard_map/ppermute | solution.py:38
  78.3 17.3 %collective-permute-start.3 = (bf16[256,1024]{1,0:T(8,128)(2,1)}, bf16[256,1024]{1,0:T(8,128)(2,1)}, u32[]{:S(2)}, u32[]{:S(2)}) collective-permute-start(bf16[256,1024]{1,0:T(8,128)(2,1)} %get-tuple-element.18), channel_id=1, source_target_pairs={{64,0},{128,64},{192,128},{256,192},{320,256},{384,320},{448,384},... | collective-permute-start | bytes 1572872 | tf_op jit(solution)/shard_map/ppermute | solution.py:38
  84.6 16.0 %collective-permute-start.4 = (bf16[256,1024]{1,0:T(8,128)(2,1)}, bf16[256,1024]{1,0:T(8,128)(2,1)}, u32[]{:S(2)}, u32[]{:S(2)}) collective-permute-start(bf16[256,1024]{1,0:T(8,128)(2,1)} %get-tuple-element.19), channel_id=1, source_target_pairs={{704,0},{0,64},{64,128},{128,192},{192,256},{256,320},{320,384},{3... | collective-permute-start | bytes 1572872 | tf_op jit(solution)/shard_map/ppermute | solution.py:38
  86.8 16.0 %collective-permute-start.6 = (bf16[256,1024]{1,0:T(8,128)(2,1)}, bf16[256,1024]{1,0:T(8,128)(2,1)}, u32[]{:S(2)}, u32[]{:S(2)}) collective-permute-start(bf16[256,1024]{1,0:T(8,128)(2,1)} %get-tuple-element.19), channel_id=1, source_target_pairs={{16,0},{32,16},{48,32},{0,48},{17,1},{33,17},{49,33},{1,49},{18,2}... | collective-permute-start | bytes 1572872 | tf_op jit(solution)/shard_map/ppermute | solution.py:38
  93.7 18.0 %collective-permute-start.7 = (bf16[256,1024]{1,0:T(8,128)(2,1)}, bf16[256,1024]{1,0:T(8,128)(2,1)S(1)}, u32[]{:S(2)}, u32[]{:S(2)}) collective-permute-start(bf16[256,1024]{1,0:T(8,128)(2,1)} %get-tuple-element.19), channel_id=1, source_target_pairs={{48,0},{0,16},{16,32},{32,48},{49,1},{1,17},{17,33},{33,49},{50,2}... | collective-permute-start | bytes 1572872 | tf_op jit(solution)/shard_map/ppermute | solution.py:38
  113.7 6.4 %copy-start.6 = (f32[2048]{0:T(1024)S(1)}, f32[2048]{0:T(1024)}, u32[]{:S(2)}) copy-start(f32[2048]{0:T(1024)} %param.11) | copy-start | bytes 24580
  113.7 6.4 %copy-start.8 = (s32[128]{0:T(128)S(1)}, s32[128]{0:T(128)}, u32[]{:S(2)}) copy-start(s32[128]{0:T(128)} %copy-done.7) | copy-start | bytes 1540
  116.2 6.5 %collective-permute-start.10 = (f32[64,2048]{1,0:T(8,128)}, f32[64,2048]{1,0:T(8,128)S(1)}, u32[]{:S(2)}, u32[]{:S(2)}) collective-permute-start(f32[64,2048]{1,0:T(8,128)} %slice_bitcast_fusion), channel_id=1, source_target_pairs={{0,1},{1,0},{2,3},{3,2},{4,5},{5,4},{6,7},{7,6},{8,9},{9,8},{10,11... | collective-permute-start | bytes 1572872 | tf_op jit(solution)/shard_map/ppermute | solution.py:126
  120.8 3.8 %collective-permute-start.5 = (bf16[128,2048]{1,0:T(8,128)(2,1)S(1)}, bf16[128,2048]{1,0:T(8,128)(2,1)S(1)}, u32[]{:S(2)}, u32[]{:S(2)}) collective-permute-start(bf16[128,2048]{1,0:T(8,128)(2,1)S(1)} %fusion.32), channel_id=1, source_target_pairs={{0,1},{1,0},{2,3},{3,2},{4,5},{5,4},{6,7},{7,6},{8,9},{9,8},{10,11... | collective-permute-start | bytes 1572872 | tf_op jit(solution)/shard_map/ppermute | solution.py:109
  130.0 1.8 %copy-start.3 = (bf16[512,2048]{1,0:T(8,128)(2,1)S(1)}, bf16[512,2048]{1,0:T(8,128)(2,1)}, u32[]{:S(2)}) copy-start(bf16[512,2048]{1,0:T(8,128)(2,1)} %all-gather.2.cloned.1.call-done) | copy-start | bytes 6291460
  132.4 3.4 %collective-permute-start.8 = (bf16[128,1024]{1,0:T(8,128)(2,1)S(1)}, bf16[128,1024]{1,0:T(8,128)(2,1)S(1)}, u32[]{:S(2)}, u32[]{:S(2)}) collective-permute-start(bf16[128,1024]{1,0:T(8,128)(2,1)S(1)} %get-tuple-element.25), channel_id=1, source_target_pairs={{0,1},{1,0},{2,3},{3,2},{4,5},{5,4},{6,7},{7,6},{8,9},{9,8},{10,11... | collective-permute-start | bytes 786440 | tf_op jit(solution)/shard_map/ppermute | solution.py:127
Sparse Core Ops, SparseCore 0:
  13.3 56.3 all-gather.1

commit v3 on v2

v3 whole, which is shorter than its diff:
```python
import itertools

import jax
import jax.numpy as jnp
from jax import lax
from jax.experimental import pallas as pl
from jax.experimental.pallas import tpu as pltpu
from jax.sharding import Mesh, PartitionSpec as P

CAP = 8
NX, NY, NCORE = 4, 8, 2
ROW = ("x", "y", "core")


eps = 1e-06


def norm_rows(values, gain):
    scale = lax.rsqrt(jnp.mean(values * values, axis=1, keepdims=True) + eps)
    return (values * scale * gain, scale)


def norm_back(values, gain, scale, upstream):
    unit = values * scale
    scaled = upstream * gain
    return scale * (scaled - unit * jnp.mean(scaled * unit, axis=1, keepdims=True))


def locate(owner_row, items):
    matches = items[:, None] == lax.broadcasted_iota(
        jnp.int32, (items.shape[0], owner_row.shape[0]), 1
    )
    return jnp.sum(jnp.where(matches, owner_row[None, :], 0), axis=1)


def dot(a, b, da=1, db=0):
    return lax.dot_general(a, b, (((da,), (db,)), ((), ())), preferred_element_type=jnp.float32)


def nt(a, b):
    return dot(a, b, 1, 1)


def turned(a, start):
    twice = jnp.concatenate([a, a], axis=1)
    return lax.dynamic_slice_in_dim(twice, start, a.shape[1], axis=1)


def route(a, axes, sizes, source):
    pairs = []
    for to in itertools.product(*[range(n) for n in sizes]):
        flat = 0
        for n, i in zip(sizes, source(*to)):
            flat = flat * n + i % n
        mine = 0
        for n, i in zip(sizes, to):
            mine = mine * n + i
        pairs.append((flat, mine))
    return lax.ppermute(a, axes, pairs)


def products(act, act_other, grads, grads_other, weight):
    rows = grads.shape[0] // 2
    forward = dot(jnp.concatenate([act, act_other], axis=0), weight)
    back = nt(jnp.concatenate([grads, grads_other], axis=0), weight)
    return (
        forward,
        back[:rows] + back[rows : 2 * rows],
        back[2 * rows : 3 * rows] + back[3 * rows :],
    )


def first_kernel(act, act_other, grads, grads_other, weight, acc, up, up_other):
    acc[...], up[...], up_other[...] = products(
        act[...], act_other[...], grads[...], grads_other[...], weight[...]
    )


def second_kernel(act, act_other, grads, grads_other, a, b, c, d, acc, up, up_other, keep, send):
    rows, width = act.shape[0], a.shape[1]
    weight = jnp.concatenate([a[...], b[...], c[...], d[...]], axis=0)
    forward, back, back_other = products(
        act[...], act_other[...], grads[...], grads_other[...], weight
    )
    items = back.shape[0]
    keep[:, :width] = acc[:rows] + forward[:rows]
    send[:, :width] = acc[rows:] + forward[rows:]
    keep[:items, width:] = up[...]
    keep[items:, width:] = back
    send[:items, width:] = up_other[...]
    send[items:, width:] = back_other


def last_kernel(place, keep, got, hidden, item_emb, item_gain, user_gain, values, item_grad, upstream):
    width = values.shape[1]
    items = hidden.shape[0]
    block = keep.shape[1] - width
    values[...] = (keep[:, :width] + got[:, :width]).astype(jnp.bfloat16)
    for step, ref in ((0, keep), (2, got)):
        for part in range(2):
            at = lax.rem(place[0] + step + part, NX) * block
            upstream[:, pl.ds(pl.multiple_of(at, block), block)] = ref[
                part * items : (part + 1) * items, width:
            ]
    x = item_emb[...].astype(jnp.float32)
    scale = lax.rsqrt(jnp.mean(x * x, axis=1, keepdims=True) + eps)
    emb_grad = norm_back(x, user_gain[...], scale, upstream[...])
    hid = hidden[...].astype(jnp.float32)
    scale = lax.rsqrt(jnp.mean(hid * hid, axis=1, keepdims=True) + eps)
    item_grad[...] = norm_back(hid, item_gain[...], scale, emb_grad)


def on_chip(kernel, shapes, *args, scratch=(), cost=None, smem=0):
    vmem = pl.BlockSpec(memory_space=pltpu.VMEM)
    return pl.pallas_call(
        kernel,
        out_shape=[jax.ShapeDtypeStruct(s, t) for s, t in shapes],
        in_specs=[pl.BlockSpec(memory_space=pltpu.SMEM)] * smem + [vmem] * (len(args) - smem),
        out_specs=[vmem] * len(shapes),
        scratch_shapes=list(scratch),
        cost_estimate=cost,
        compiler_params=pltpu.CompilerParams(vmem_limit_bytes=32 << 20),
    )(*args)


def local(item_hidden, item_gain, history, owner_map, user_gain, value_weight, value_grad):
    groups = lax.axis_size("dp")
    item_rows, width = item_hidden.shape
    hist_rows = history.shape[0]
    block = width // NX
    core = lax.axis_index("core")
    color = (lax.axis_index("x") + lax.axis_index("dp") % 2 + 2 * core) % NX
    axes, sizes = ("dp", "x", "core"), (groups, NX, NCORE)
    f32, bf16 = jnp.float32, jnp.bfloat16

    shard_a = route(value_weight, axes, sizes, lambda z, x, c: (z, x + z % 2 + 2 * c, 1 - c))
    shard_b = route(value_weight, axes, sizes, lambda z, x, c: (z, x + z % 2 + 2 * c, c))
    seed = jnp.where(
        core == 0,
        jnp.concatenate([shard_b, shard_a], axis=0),
        jnp.concatenate([shard_a, shard_b], axis=0),
    )

    owner_row = owner_map[0]
    pool = owner_row.shape[0]
    stored = locate(owner_row, history)
    pick = stored[:, None] == lax.broadcasted_iota(jnp.int32, (hist_rows, pool), 1)
    wanted = jnp.any(pick, axis=0).reshape(groups, item_rows)
    slot = jnp.cumsum(wanted.astype(jnp.int32), axis=1) - 1
    slot_pos = jnp.sum(jnp.where(pick, slot.reshape(1, pool), 0), axis=1)
    buffer_row = stored // item_rows * CAP + slot_pos
    one_hot = (
        buffer_row[:, None] == lax.broadcasted_iota(jnp.int32, (hist_rows, groups * CAP), 1)
    ).astype(bf16)
    grad_sums = dot(one_hot, value_grad, 0, 0).astype(bf16).reshape(groups, CAP, width)
    slot_ids = lax.broadcasted_iota(jnp.int32, (groups, CAP, item_rows), 1)
    asked = (wanted[:, None, :] & (slot[:, None, :] == slot_ids)).astype(bf16)
    asked = jnp.pad(asked, ((0, 0), (0, 0), (0, -item_rows % 128)))
    sent, seed = lax.optimization_barrier((jnp.concatenate([grad_sums, asked], axis=2), seed))
    arrived = lax.all_to_all(sent, "dp", split_axis=0, concat_axis=0, tiled=True)
    arrived = arrived.reshape(groups * CAP, -1)
    mine = lax.all_gather(seed, "y", axis=0, tiled=True)
    select = arrived[:, width : width + item_rows]

    item_emb, _ = norm_rows(item_hidden.astype(f32), item_gain)
    item_emb = item_emb.astype(bf16)
    outgoing = dot(select, item_emb).astype(bf16).reshape(groups, CAP, width)
    incoming = lax.all_to_all(outgoing, "dp", split_axis=0, concat_axis=0, tiled=True)

    quarter = block // 4
    cuts = [mine[i * quarter : (i + 1) * quarter] for i in range(4)]
    cross = lambda z, c: 1 - c if z % 2 else c
    pieces = [
        route(cuts[0], axes, sizes, lambda z, x, c: (z, x + 1, c)),
        route(cuts[1], axes, sizes, lambda z, x, c: (z, x - 1, 1 - c)),
        route(cuts[2], axes, sizes, lambda z, x, c: (z + 1, x, cross(z, c))),
        route(cuts[3], axes, sizes, lambda z, x, c: (z - 1, x, cross(z, c))),
    ]

    incoming, pieces[0] = lax.optimization_barrier((incoming, pieces[0]))

    swap = [(0, 1), (1, 0)]
    total = dot(select, arrived[:, :width], 0, 0)
    high = lax.reduce_precision(total, 8, 7)
    grads = jnp.concatenate([high, total - high], axis=0).astype(bf16)
    grads_other = lax.ppermute(grads, "core", swap)
    normed, _ = norm_rows(incoming.reshape(groups * CAP, width).astype(f32), user_gain)
    normed = dot(one_hot, normed.astype(bf16)).astype(bf16)
    normed = turned(normed, color * block)
    act = normed[:, : 2 * block]
    act_other = lax.ppermute(normed[:, 2 * block :], "core", swap)

    both = 2 * hist_rows
    cost = pl.CostEstimate(flops=0, bytes_accessed=0, transcendentals=0)
    acc, up, up_other = on_chip(
        first_kernel,
        [((both, width), f32), ((item_rows, block), f32), ((item_rows, block), f32)],
        act[:, :block], act_other[:, :block], grads, grads_other, mine,
        cost=cost,
    )
    keep, send = on_chip(
        second_kernel,
        [((hist_rows, width + block), f32)] * 2,
        act[:, block:], act_other[:, block:], grads, grads_other, *pieces, acc, up, up_other,
        cost=cost,
    )
    got = lax.ppermute(send, "core", swap)
    values, item_grad = on_chip(
        last_kernel,
        [((hist_rows, width), bf16), ((item_rows, width), f32)],
        color.reshape(1).astype(jnp.int32), keep, got, item_hidden, item_emb,
        item_gain.reshape(1, width), user_gain.reshape(1, width),
        scratch=[pltpu.VMEM((item_rows, width), f32)],
        smem=1,
    )
    return (values, item_grad)


def solution(mesh):
    groups = mesh.shape["dp"]
    mesh = Mesh(mesh.devices.reshape(groups, NX, NY, NCORE), ("dp",) + ROW)
    everywhere = ("dp",) + ROW
    in_specs = (
        P(everywhere, None),
        P(),
        P(everywhere),
        P(ROW, None),
        P(),
        P(ROW, None),
        P(everywhere, None),
    )
    out_specs = (P(everywhere, None), P(everywhere, None))
    return jax.shard_map(local, mesh=mesh, in_specs=in_specs, out_specs=out_specs, check_vma=False)
```

time: 145 us -> 126 us (0.87)
  matrix products: 25.1 us -> 3.01 us
  Pallas kernels: 0 us -> 6.74 us
  waiting for transfers between devices: 32.9 us -> 39.4 us
  starting transfers between devices: 57.9 us -> 52.8 us
  other arithmetic: 9.05 us -> 5.47 us
    dot_general x18 -> x4, matrix products: 25.1 us -> 3.01 us  [dot(): lax.dot_general(a, b, (((da,), (db,)), ((), ())), preferred_element_type=...]
    all_to_all x1, starting transfers between devices: 18.8 us -> 7.95 us  [local(): lax.all_to_all(sent, 'dp', split_axis=0, concat_axis=0, tiled=True)]
    ppermute x11 -> x9, starting transfers between devices: 33.1 us -> 40.6 us  [the longest x6 29.1 us: route(): return lax.ppermute(a, axes, pairs)]
    pallas_call x0 -> x3, Pallas kernels: none -> 6.74 us  [on_chip(): pl.pallas_call(kernel, out_shape=[jax.ShapeDtypeStruct(s, t) for s, t in...]
    ppermute x11 -> x9, waiting for transfers between devices: 6.41 us -> 12.5 us  [the longest x6 8.71 us: route(): return lax.ppermute(a, axes, pairs)]
    add x2 -> x0, other arithmetic: 1.73 us -> none  [the longest x1 1.67 us: local(): upstream = upstream[:, 0] + upstream[:, 1]]
    all_to_all x1, starting transfers between devices: 5.9 us -> 4.23 us  [local(): lax.all_to_all(outgoing, 'dp', split_axis=0, concat_axis=0, tiled=True)]
    slice x2 -> x4, local copies, waits for them, and re-layouts: 2.42 us -> 2.97 us  [the longest x1 2.91 us: local(): cuts = [mine[i * quarter:(i + 1) * quarter] for i in range(4)]]
  transfers between devices with their start and end apart: 14 -> 12, of which waited for: 5 -> 7; matrix products, arithmetic and copies ran while one was open for 17% -> 9% of each run, Pallas kernels for 0% -> 2%
where the time goes in v3:
time: 126 us; the launch traced here: 125 us
  starting transfers between devices  52.8 us (42%)
  waiting for transfers between devices  39.4 us (31%)
  between operations  14.4 us (11%)
  Pallas kernels  6.74 us (5%)
  other arithmetic  5.47 us (4%)
  local copies, waits for them, and re-layouts  3.24 us (3%)
  matrix products  3.01 us (2%)
    ppermute x6, starting transfers between devices, route(): return lax.ppermute(a, axes, pairs)  29.1 us
    all_to_all x1, waiting for transfers between devices, local(): lax.all_to_all(sent, 'dp', split_axis=0, concat_axis=0, tiled=True)  19.1 us
    ppermute x6, waiting for transfers between devices, route(): return lax.ppermute(a, axes, pairs)  8.71 us
    all_to_all x1, starting transfers between devices, local(): lax.all_to_all(sent, 'dp', split_axis=0, concat_axis=0, tiled=True)  7.95 us
    all_gather x1, waiting for transfers between devices, local(): mine = lax.all_gather(seed, 'y', axis=0, tiled=True)  7.85 us
    ppermute x1, starting transfers between devices, local(): grads_other = lax.ppermute(grads, 'core', swap)  6.8 us
    pallas_call x3, Pallas kernels, on_chip(): pl.pallas_call(kernel, out_shape=[jax.ShapeDtypeStruct(s, t) for s, t in...  6.74 us
    all_to_all x1, starting transfers between devices, local(): lax.all_to_all(outgoing, 'dp', split_axis=0, concat_axis=0, tiled=True)  4.23 us
  transfers between devices with their start and end apart: 12, of which 7 were waited for; matrix products, arithmetic and copies ran while one was open for 9% of the time, Pallas kernels for 2%

profile of v3, /device:TPU:1, one launch (start us, length us, event | category | flops | bytes accessed | tf_op | source)
XLA Modules:
  0.0 125.0 jit_solution(3939518477296125462)
XLA Ops:
  7.2 12.6 %collective-permute-start.1 = (bf16[32,2048]{1,0:T(8,128)(2,1)}, bf16[32,2048]{1,0:T(8,128)(2,1)S(1)}, u32[]{:S(2)}, u32[]{:S(2)}) collective-permute-start(bf16[32,2048]{1,0:T(8,128)(2,1)} %param.12), channel_id=1, source_target_pairs={{1,0},{32,1},{17,16},{48,17},{33,32},{0,33},{49,48},{16,49},{81,64... | collective-permute-start | bytes 393224 | tf_op jit(solution)/shard_map/ppermute | solution.py:59
  19.8 1.9 %collective-permute-start = (bf16[32,2048]{1,0:T(8,128)(2,1)}, bf16[32,2048]{1,0:T(8,128)(2,1)S(1)}, u32[]{:S(2)}, u32[]{:S(2)}) collective-permute-start(bf16[32,2048]{1,0:T(8,128)(2,1)} %param.12), channel_id=1, source_target_pairs={{0,0},{33,1},{16,16},{49,17},{32,32},{1,33},{48,48},{17,49},{80,64... | collective-permute-start | bytes 393224 | tf_op jit(solution)/shard_map/ppermute | solution.py:59
  21.7 0.7 reduce.1
  22.4 0.8 select_reduce_fusion.1
  24.1 0.4 fusion
  24.5 0.8 pad_maximum_fusion.1
  25.3 2.0 %collective-permute-done = bf16[32,2048]{1,0:T(8,128)(2,1)S(1)} collective-permute-done((bf16[32,2048]{1,0:T(8,128)(2,1)}, bf16[32,2048]{1,0:T(8,128)(2,1)S(1)}, u32[]{:S(2)}, u32[]{:S(2)}) %collective-permute-start) | collective-permute-done | bytes 131104 | tf_op jit(solution)/shard_map/ppermute | solution.py:59
  27.2 0.8 maximum_select_fusion
  28.0 7.9 %all-to-all-start = ((bf16[12,8,2176]{2,1,0:T(8,128)(2,1)}), bf16[12,8,2176]{2,1,0:T(8,128)(2,1)S(1)}, u32[]{:S(2)}, u32[]{:S(2)}) async-start(bf16[12,8,2176]{2,1,0:T(8,128)(2,1)} %pad_maximum_fusion.1), calls=%async_computation | async-start | bytes 835584 | tf_op jit(solution)/shard_map/all_to_all | solution.py:160
  36.3 19.1 %all-to-all-done = bf16[12,8,2176]{2,1,0:T(8,128)(2,1)S(1)} async-done(((bf16[12,8,2176]{2,1,0:T(8,128)(2,1)}), bf16[12,8,2176]{2,1,0:T(8,128)(2,1)S(1)}, u32[]{:S(2)}, u32[]{:S(2)}) %all-to-all-start) | async-done | bytes 417824 | tf_op jit(solution)/shard_map/all_to_all | solution.py:160
  55.4 1.0 fusion.1
  56.4 4.2 %all-to-all-start.1 = ((bf16[12,8,2048]{2,1,0:T(8,128)(2,1)}), bf16[12,8,2048]{2,1,0:T(8,128)(2,1)}, u32[]{:S(2)}, u32[]{:S(2)}) async-start(bf16[12,8,2048]{2,1,0:T(8,128)(2,1)} %fusion.1), calls=%async_computation.1 | async-start | bytes 786432 | tf_op jit(solution)/shard_map/all_to_all | solution.py:168
  60.6 7.8 %all-gather.2.cloned.1.call-done.weight = bf16[512,2048]{1,0:T(8,128)(2,1)} async-done(((bf16[64,2048]{1,0:T(8,128)(2,1)}), bf16[512,2048]{1,0:T(8,128)(2,1)}) %all-gather.2.cloned.1.call-update) | async-done | bytes 2097168 | tf_op jit(solution)/shard_map/all_gather | solution.py:162
  68.5 2.9 %fusion.22 = (bf16[128,2048]{1,0:T(8,128)(2,1)}, bf16[128,2048]{1,0:T(8,128)(2,1)}, bf16[128,2048]{1,0:T(8,128)(2,1)}, bf16[128,2048]{1,0:T(8,128)(2,1)}) fusion(bf16[512,2048]{1,0:T(8,128)(2,1)} %all-gather.2.cloned.1.call-done.weight), kind=kLoop, calls=%fused_computation.50 | loop fusion | bytes 4194304 | tf_op jit(solution)/shard_map/slice | solution.py:171
  71.4 4.4 %collective-permute-start.2 = (bf16[128,2048]{1,0:T(8,128)(2,1)}, bf16[128,2048]{1,0:T(8,128)(2,1)}, u32[]{:S(2)}, u32[]{:S(2)}) collective-permute-start(bf16[128,2048]{1,0:T(8,128)(2,1)} %get-tuple-element.23), channel_id=1, source_target_pairs={{16,0},{17,1},{32,16},{33,17},{48,32},{49,33},{0,48},{1,49},{80,64... | collective-permute-start | bytes 1572872 | tf_op jit(solution)/shard_map/ppermute | solution.py:59
  75.9 0.3 reduce-precision_convert_fusion
  76.2 6.8 %collective-permute-start.4 = (bf16[128,2048]{1,0:T(8,128)(2,1)S(1)}, bf16[128,2048]{1,0:T(8,128)(2,1)}, u32[]{:S(2)}, u32[]{:S(2)}) collective-permute-start(bf16[128,2048]{1,0:T(8,128)(2,1)S(1)} %pad_maximum_fusion.grads), channel_id=1, source_target_pairs={{0,1},{1,0},{2,3},{3,2},{4,5},{5,4},{6,7},{7,6},{8,9},{9,8},{10,11... | collective-permute-start | bytes 1572872 | tf_op jit(solution)/shard_map/ppermute | solution.py:186
  83.0 3.3 %collective-permute-start.7 = (bf16[128,2048]{1,0:T(8,128)(2,1)}, bf16[128,2048]{1,0:T(8,128)(2,1)}, u32[]{:S(2)}, u32[]{:S(2)}) collective-permute-start(bf16[128,2048]{1,0:T(8,128)(2,1)} %get-tuple-element.20), channel_id=1, source_target_pairs={{704,0},{705,1},{720,16},{721,17},{736,32},{737,33},{752,48},{753,... | collective-permute-start | bytes 1572872 | tf_op jit(solution)/shard_map/ppermute | solution.py:59
  86.2 5.0 %collective-permute-start.6 = (bf16[128,2048]{1,0:T(8,128)(2,1)}, bf16[128,2048]{1,0:T(8,128)(2,1)}, u32[]{:S(2)}, u32[]{:S(2)}) collective-permute-start(bf16[128,2048]{1,0:T(8,128)(2,1)} %get-tuple-element.21), channel_id=1, source_target_pairs={{64,0},{65,1},{80,16},{81,17},{96,32},{97,33},{112,48},{113,49},{1... | collective-permute-start | bytes 1572872 | tf_op jit(solution)/shard_map/ppermute | solution.py:59
  91.2 1.9 %collective-permute-start.5 = (bf16[128,2048]{1,0:T(8,128)(2,1)}, bf16[128,2048]{1,0:T(8,128)(2,1)}, u32[]{:S(2)}, u32[]{:S(2)}) collective-permute-start(bf16[128,2048]{1,0:T(8,128)(2,1)} %get-tuple-element.22), channel_id=1, source_target_pairs={{49,0},{48,1},{1,16},{0,17},{17,32},{16,33},{33,48},{32,49},{113,6... | collective-permute-start | bytes 1572872 | tf_op jit(solution)/shard_map/ppermute | solution.py:59
  93.2 1.2 fusion.5
  94.4 1.4 %convolution_convert_fusion = bf16[128,2048]{1,0:T(8,128)(2,1)S(1)} fusion(bf16[12,8,2048]{2,1,0:T(8,128)(2,1)} %all-to-all-done.1, f32[2048]{0:T(1024)S(1)} %copy-done.6, f32[96]{0:T(128)S(1)} %rsqrt.21, s32[128]{0:T(128)S(1)} %multiply_add_fusion), kind=kOutput, calls=%fused_computation | convolution fusion | flops 51392512 | bytes 926592 | tf_op jit(solution)/shard_map/dot_general | solution.py:37
  95.8 0.3 fusion.10
  96.1 2.4 %collective-permute-start.3 = (bf16[128,1024]{1,0:T(8,128)(2,1)S(1)}, bf16[128,1024]{1,0:T(8,128)(2,1)S(1)}, u32[]{:S(2)}, u32[]{:S(2)}) collective-permute-start(bf16[128,1024]{1,0:T(8,128)(2,1)S(1)} %slice.50), channel_id=1, source_target_pairs={{0,1},{1,0},{2,3},{3,2},{4,5},{5,4},{6,7},{7,6},{8,9},{9,8},{10,11... | collective-permute-start | bytes 786440 | tf_op jit(solution)/shard_map/ppermute | solution.py:191
  98.6 1.1 collective-permute-done.3
  99.7 2.3 %shard_map.86 = (f32[256,2048]{1,0:T(8,128)S(1)}, f32[64,512]{1,0:T(8,128)S(1)}, f32[64,512]{1,0:T(8,128)S(1)}) custom-call(bf16[128,512]{1,0:T(8,128)(2,1)S(1)} %get-tuple-element.24.act, bf16[128,512]{1,0:T(8,128)(2,1)S(1)} %get-tuple-element.28.act_other, bf16[128,2048]{1,0:T(8,128)(2,1)S(1)} %pad_maximum_fusion.grads, ...), custom_call_target="tpu_custom_call" | custom-call | tf_op jit(solution)/shard_map/pallas_call | solution.py:115
  102.0 0.6 collective-permute-done.6.c
  102.6 6.1 %collective-permute-done.5.b = bf16[128,2048]{1,0:T(8,128)(2,1)} collective-permute-done((bf16[128,2048]{1,0:T(8,128)(2,1)}, bf16[128,2048]{1,0:T(8,128)(2,1)}, u32[]{:S(2)}, u32[]{:S(2)}) %collective-permute-start.5) | collective-permute-done | bytes 524320 | tf_op jit(solution)/shard_map/ppermute | solution.py:59
  108.8 3.0 %shard_map.87 = (f32[128,2560]{1,0:T(8,128)S(1)}, f32[128,2560]{1,0:T(8,128)S(1)}) custom-call(bf16[128,512]{1,0:T(8,128)(2,1)S(1)} %get-tuple-element.25.act, bf16[128,512]{1,0:T(8,128)(2,1)S(1)} %get-tuple-element.29.act_other, bf16[128,2048]{1,0:T(8,128)(2,1)S(1)} %pad_maximum_fusion.grads, bf16[128,2048]{1,0:T(8,128)(2,1)} %collective-permute-done.4.grads_other, ...), custom_call_target="tpu_custom_call" | custom-call | tf_op jit(solution)/shard_map/pallas_call | solution.py:115
  111.8 2.3 %collective-permute-start.8 = (f32[128,2560]{1,0:T(8,128)S(1)}, f32[128,2560]{1,0:T(8,128)S(1)}, u32[]{:S(2)}, u32[]{:S(2)}) collective-permute-start(f32[128,2560]{1,0:T(8,128)S(1)} %get-tuple-element.19), channel_id=1, source_target_pairs={{0,1},{1,0},{2,3},{3,2},{4,5},{5,4},{6,7},{7,6},{8,9},{9,8},{10,11... | collective-permute-start | bytes 3932168 | tf_op jit(solution)/shard_map/ppermute | solution.py:207
  114.1 2.6 %collective-permute-done.8.got = f32[128,2560]{1,0:T(8,128)S(1)} collective-permute-done((f32[128,2560]{1,0:T(8,128)S(1)}, f32[128,2560]{1,0:T(8,128)S(1)}, u32[]{:S(2)}, u32[]{:S(2)}) %collective-permute-start.8) | collective-permute-done | bytes 1310752 | tf_op jit(solution)/shard_map/ppermute | solution.py:207
  116.7 1.5 %shard_map.88 = (bf16[128,2048]{1,0:T(8,128)(2,1)}, f32[64,2048]{1,0:T(8,128)}) custom-call(s32[1]{0:T(128)} %bitcast.place, f32[128,2560]{1,0:T(8,128)S(1)} %get-tuple-element.18.keep, f32[128,2560]{1,0:T(8,128)S(1)} %collective-permute-done.8.got, bf16[64,2048]{1,0:T(8,128)(2,1)S(1)} %copy-done.2, bf16[64,2048]{1,0:T(8,128)(2,1)S(1)} %copy-done.4, ...), custom_call_target="tpu_custom_call" | custom-call | tf_op jit(solution)/shard_map/pallas_call | solution.py:115
  (40 shorter events, 1.3 us)
Async XLA Ops:
  7.2 16.9 %copy-start = (bf16[128,2048]{1,0:T(8,128)(2,1)S(1)}, bf16[128,2048]{1,0:T(8,128)(2,1)}, u32[]{:S(2)}) copy-start(bf16[128,2048]{1,0:T(8,128)(2,1)} %param.13) | copy-start | bytes 1572868
  7.2 28.8 %copy-start.2 = (bf16[64,2048]{1,0:T(8,128)(2,1)S(1)}, bf16[64,2048]{1,0:T(8,128)(2,1)}, u32[]{:S(2)}) copy-start(bf16[64,2048]{1,0:T(8,128)(2,1)} %hidden.1) | copy-start | bytes 786436
  7.2 29.0 %copy-start.5 = (f32[2048]{0:T(1024)S(1)}, f32[2048]{0:T(1024)}, u32[]{:S(2)}) copy-start(f32[2048]{0:T(1024)} %param.8) | copy-start | bytes 24580
  7.2 61.3 %all-gather.2.cloned.1.call-start = ((), (), s32[]{:S(2)}) async-start(), calls=%async_computation.2 | async-start | bytes 2359296 | tf_op jit(solution)/shard_map/all_gather | solution.py:162
  7.2 18.0 %collective-permute-start.1 = (bf16[32,2048]{1,0:T(8,128)(2,1)}, bf16[32,2048]{1,0:T(8,128)(2,1)S(1)}, u32[]{:S(2)}, u32[]{:S(2)}) collective-permute-start(bf16[32,2048]{1,0:T(8,128)(2,1)} %param.12), channel_id=1, source_target_pairs={{1,0},{32,1},{17,16},{48,17},{33,32},{0,33},{49,48},{16,49},{81,64... | collective-permute-start | bytes 393224 | tf_op jit(solution)/shard_map/ppermute | solution.py:59
  19.8 7.4 %collective-permute-start = (bf16[32,2048]{1,0:T(8,128)(2,1)}, bf16[32,2048]{1,0:T(8,128)(2,1)S(1)}, u32[]{:S(2)}, u32[]{:S(2)}) collective-permute-start(bf16[32,2048]{1,0:T(8,128)(2,1)} %param.12), channel_id=1, source_target_pairs={{0,0},{33,1},{16,16},{49,17},{32,32},{1,33},{48,48},{17,49},{80,64... | collective-permute-start | bytes 393224 | tf_op jit(solution)/shard_map/ppermute | solution.py:59
  28.0 27.4 %all-to-all-start = ((bf16[12,8,2176]{2,1,0:T(8,128)(2,1)}), bf16[12,8,2176]{2,1,0:T(8,128)(2,1)S(1)}, u32[]{:S(2)}, u32[]{:S(2)}) async-start(bf16[12,8,2176]{2,1,0:T(8,128)(2,1)} %pad_maximum_fusion.1), calls=%async_computation | async-start | bytes 835584 | tf_op jit(solution)/shard_map/all_to_all | solution.py:160
  36.3 35.1 %copy-start.3 = (bf16[64,2048]{1,0:T(8,128)(2,1)}, bf16[64,2048]{1,0:T(8,128)(2,1)S(1)}, u32[]{:S(2)}) copy-start(bf16[64,2048]{1,0:T(8,128)(2,1)S(1)} %fusion.8.item_emb) | copy-start | bytes 786436
  56.4 36.8 %all-to-all-start.1 = ((bf16[12,8,2048]{2,1,0:T(8,128)(2,1)}), bf16[12,8,2048]{2,1,0:T(8,128)(2,1)}, u32[]{:S(2)}, u32[]{:S(2)}) async-start(bf16[12,8,2048]{2,1,0:T(8,128)(2,1)} %fusion.1), calls=%async_computation.1 | async-start | bytes 786432 | tf_op jit(solution)/shard_map/all_to_all | solution.py:168
  71.4 23.1 %copy-start.6 = (f32[2048]{0:T(1024)S(1)}, f32[2048]{0:T(1024)}, u32[]{:S(2)}) copy-start(f32[2048]{0:T(1024)} %param.11) | copy-start | bytes 24580
  71.4 21.8 %collective-permute-start.2 = (bf16[128,2048]{1,0:T(8,128)(2,1)}, bf16[128,2048]{1,0:T(8,128)(2,1)}, u32[]{:S(2)}, u32[]{:S(2)}) collective-permute-start(bf16[128,2048]{1,0:T(8,128)(2,1)} %get-tuple-element.23), channel_id=1, source_target_pairs={{16,0},{17,1},{32,16},{33,17},{48,32},{49,33},{0,48},{1,49},{80,64... | collective-permute-start | bytes 1572872 | tf_op jit(solution)/shard_map/ppermute | solution.py:59
  76.2 23.6 %copy-start.1 = (bf16[512,2048]{1,0:T(8,128)(2,1)S(1)}, bf16[512,2048]{1,0:T(8,128)(2,1)}, u32[]{:S(2)}) copy-start(bf16[512,2048]{1,0:T(8,128)(2,1)} %all-gather.2.cloned.1.call-done.weight) | copy-start | bytes 6291460
  76.2 23.5 %collective-permute-start.4 = (bf16[128,2048]{1,0:T(8,128)(2,1)S(1)}, bf16[128,2048]{1,0:T(8,128)(2,1)}, u32[]{:S(2)}, u32[]{:S(2)}) collective-permute-start(bf16[128,2048]{1,0:T(8,128)(2,1)S(1)} %pad_maximum_fusion.grads), channel_id=1, source_target_pairs={{0,1},{1,0},{2,3},{3,2},{4,5},{5,4},{6,7},{7,6},{8,9},{9,8},{10,11... | collective-permute-start | bytes 1572872 | tf_op jit(solution)/shard_map/ppermute | solution.py:186
  83.0 19.0 %collective-permute-start.7 = (bf16[128,2048]{1,0:T(8,128)(2,1)}, bf16[128,2048]{1,0:T(8,128)(2,1)}, u32[]{:S(2)}, u32[]{:S(2)}) collective-permute-start(bf16[128,2048]{1,0:T(8,128)(2,1)} %get-tuple-element.20), channel_id=1, source_target_pairs={{704,0},{705,1},{720,16},{721,17},{736,32},{737,33},{752,48},{753,... | collective-permute-start | bytes 1572872 | tf_op jit(solution)/shard_map/ppermute | solution.py:59
  86.2 16.4 %collective-permute-start.6 = (bf16[128,2048]{1,0:T(8,128)(2,1)}, bf16[128,2048]{1,0:T(8,128)(2,1)}, u32[]{:S(2)}, u32[]{:S(2)}) collective-permute-start(bf16[128,2048]{1,0:T(8,128)(2,1)} %get-tuple-element.21), channel_id=1, source_target_pairs={{64,0},{65,1},{80,16},{81,17},{96,32},{97,33},{112,48},{113,49},{1... | collective-permute-start | bytes 1572872 | tf_op jit(solution)/shard_map/ppermute | solution.py:59
  91.2 17.6 %collective-permute-start.5 = (bf16[128,2048]{1,0:T(8,128)(2,1)}, bf16[128,2048]{1,0:T(8,128)(2,1)}, u32[]{:S(2)}, u32[]{:S(2)}) collective-permute-start(bf16[128,2048]{1,0:T(8,128)(2,1)} %get-tuple-element.22), channel_id=1, source_target_pairs={{49,0},{48,1},{1,16},{0,17},{17,32},{16,33},{33,48},{32,49},{113,6... | collective-permute-start | bytes 1572872 | tf_op jit(solution)/shard_map/ppermute | solution.py:59
  96.1 3.6 %collective-permute-start.3 = (bf16[128,1024]{1,0:T(8,128)(2,1)S(1)}, bf16[128,1024]{1,0:T(8,128)(2,1)S(1)}, u32[]{:S(2)}, u32[]{:S(2)}) collective-permute-start(bf16[128,1024]{1,0:T(8,128)(2,1)S(1)} %slice.50), channel_id=1, source_target_pairs={{0,1},{1,0},{2,3},{3,2},{4,5},{5,4},{6,7},{7,6},{8,9},{9,8},{10,11... | collective-permute-start | bytes 786440 | tf_op jit(solution)/shard_map/ppermute | solution.py:191
  108.8 7.9 %copy-start.4 = (bf16[64,2048]{1,0:T(8,128)(2,1)S(1)}, bf16[64,2048]{1,0:T(8,128)(2,1)}, u32[]{:S(2)}) copy-start(bf16[64,2048]{1,0:T(8,128)(2,1)} %copy-done.3) | copy-start | bytes 786436
  111.8 4.9 %collective-permute-start.8 = (f32[128,2560]{1,0:T(8,128)S(1)}, f32[128,2560]{1,0:T(8,128)S(1)}, u32[]{:S(2)}, u32[]{:S(2)}) collective-permute-start(f32[128,2560]{1,0:T(8,128)S(1)} %get-tuple-element.19), channel_id=1, source_target_pairs={{0,1},{1,0},{2,3},{3,2},{4,5},{5,4},{6,7},{7,6},{8,9},{9,8},{10,11... | collective-permute-start | bytes 3932168 | tf_op jit(solution)/shard_map/ppermute | solution.py:207
Sparse Core Ops, SparseCore 0:
  28.1 40.2 all-gather.1

commit v4 on v2

v4 whole, which is shorter than its diff:
```python
import jax
import jax.numpy as jnp
from jax import lax
from jax.experimental import pallas as pl
from jax.experimental.pallas import tpu as pltpu
from jax.sharding import Mesh, PartitionSpec as P

CAP = 8
NX, NY, NCORE = 4, 8, 2
ROW = ("x", "y", "core")


eps = 1e-06


def norm_rows(values, gain):
    scale = lax.rsqrt(jnp.mean(values * values, axis=1, keepdims=True) + eps)
    return (values * scale * gain, scale)


def norm_back(values, gain, scale, upstream):
    unit = values * scale
    scaled = upstream * gain
    return scale * (scaled - unit * jnp.mean(scaled * unit, axis=1, keepdims=True))


def locate(owner_row, items):
    matches = items[:, None] == lax.broadcasted_iota(
        jnp.int32, (items.shape[0], owner_row.shape[0]), 1
    )
    return jnp.sum(jnp.where(matches, owner_row[None, :], 0), axis=1)


def dot(a, b, da=1, db=0):
    return lax.dot_general(a, b, (((da,), (db,)), ((), ())), preferred_element_type=jnp.float32)


def split(a):
    part = a.shape[1] // (NX * NY * NCORE)
    a = a.reshape(a.shape[0], NX, NY, NCORE, part).transpose(0, 3, 2, 1, 4)
    return a.reshape(a.shape[0], -1)


def products(act, act_other, grads, grads_other, weight, acc, up, up_other):
    forward = dot(jnp.concatenate([act[...], act_other[...]], axis=0), weight[...])
    back = dot(jnp.concatenate([grads[...], grads_other[...]], axis=0), weight[...], 1, 1)

    @pl.when(pl.program_id(0) == 0)
    def _():
        acc[...] = forward

    @pl.when(pl.program_id(0) > 0)
    def _():
        acc[...] += forward

    rows = up.shape[0]
    up[...] = back[:rows] + back[rows : 2 * rows]
    up_other[...] = back[2 * rows : 3 * rows] + back[3 * rows :]


def products_kernel(act, act_other, grads, grads_other, weight, keep, send, acc, up, up_other):
    step, steps = pl.program_id(0), pl.num_programs(0)
    block, width = weight.shape
    items = up.shape[0]
    at = pl.ds(pl.multiple_of(step * block, block), block)
    products(
        act, act_other, grads, grads_other, weight, acc, up.at[:, at], up_other.at[:, at]
    )

    @pl.when(step == steps - 1)
    def _():
        rows = act.shape[0]
        half = up.shape[1] // 2
        keep[:, :width] = acc[:rows]
        send[:, :width] = acc[rows:]
        for ref, sums in ((keep, up), (send, up_other)):
            ref[:items, width:] = sums[:, :half]
            ref[items:, width:] = sums[:, half:]


def last_kernel(core, keep, got, hidden, item_emb, item_gain, user_gain, values, item_grad, up):
    width = values.shape[1]
    items = hidden.shape[0]
    block = keep.shape[1] - width
    part = width // (NX * NY * NCORE)
    tile = part * NX
    values[...] = (keep[:, :width] + got[:, :width]).astype(jnp.bfloat16)
    for side, ref in ((core[0], keep), (1 - core[0], got)):
        for piece in range(2):
            at = pl.multiple_of((2 * side + piece) * block, block)
            up[:, pl.ds(at, block)] = ref[piece * items : (piece + 1) * items, width:]
    x = item_emb[...].astype(jnp.float32)
    scale = lax.rsqrt(jnp.mean(x * x, axis=1, keepdims=True) + eps)
    emb_grad = norm_back(x, user_gain[...], scale, up[...])
    hid = hidden[...].astype(jnp.float32)
    scale = lax.rsqrt(jnp.mean(hid * hid, axis=1, keepdims=True) + eps)
    up[...] = norm_back(hid, item_gain[...], scale, emb_grad)
    group = lax.broadcasted_iota(jnp.int32, (items, tile), 1) // part
    for out in range(width // tile):
        at_x, y = out // (NY // 2), 2 * (out % (NY // 2))
        total = None
        for to, (side, at_y) in enumerate(((0, y), (1, y), (0, y + 1), (1, y + 1))):
            piece = up[:, (side * NY + at_y) * tile : (side * NY + at_y + 1) * tile]
            piece = pltpu.roll(piece, (to - at_x) % NX * part, 1)
            total = piece if total is None else jnp.where(group == to, piece, total)
        item_grad[:, out * tile : (out + 1) * tile] = total


def local(item_hidden, item_gain, history, owner_map, user_gain, value_weight, value_grad):
    groups = lax.axis_size("dp")
    item_rows, width = item_hidden.shape
    hist_rows = history.shape[0]
    shard = value_weight.shape[0]
    half = width // 2
    core = lax.axis_index("core")
    f32, bf16 = jnp.float32, jnp.bfloat16

    near = [value_weight]
    for step in range(1, NX):
        pairs = [((x + step) % NX, x) for x in range(NX)]
        near.append(lax.ppermute(value_weight, "x", pairs))
    seed = lax.dynamic_slice_in_dim(
        jnp.concatenate(near + near, axis=0),
        (NX - lax.axis_index("x")) % NX * shard,
        NX * shard,
        axis=0,
    )

    owner_row = owner_map[0]
    pool = owner_row.shape[0]
    stored = locate(owner_row, history)
    pick = stored[:, None] == lax.broadcasted_iota(jnp.int32, (hist_rows, pool), 1)
    wanted = jnp.any(pick, axis=0).reshape(groups, item_rows)
    slot = jnp.cumsum(wanted.astype(jnp.int32), axis=1) - 1
    slot_pos = jnp.sum(jnp.where(pick, slot.reshape(1, pool), 0), axis=1)
    buffer_row = stored // item_rows * CAP + slot_pos
    one_hot = (
        buffer_row[:, None] == lax.broadcasted_iota(jnp.int32, (hist_rows, groups * CAP), 1)
    ).astype(bf16)
    grad_sums = dot(one_hot, value_grad, 0, 0).astype(bf16).reshape(groups, CAP, width)
    slot_ids = lax.broadcasted_iota(jnp.int32, (groups, CAP, item_rows), 1)
    asked = (wanted[:, None, :] & (slot[:, None, :] == slot_ids)).astype(bf16)
    asked = jnp.pad(asked, ((0, 0), (0, 0), (0, -item_rows % 128)))
    sent, seed = lax.optimization_barrier((jnp.concatenate([grad_sums, asked], axis=2), seed))
    weight = lax.all_gather(seed, "y", axis=0, tiled=True)
    arrived = lax.all_to_all(sent, "dp", split_axis=0, concat_axis=0, tiled=True)
    arrived = arrived.reshape(groups * CAP, -1)
    select = arrived[:, width : width + item_rows]

    hidden = split(item_hidden)
    item_gain, user_gain = split(item_gain.reshape(1, width)), split(user_gain.reshape(1, width))
    item_emb, _ = norm_rows(hidden.astype(f32), item_gain)
    item_emb = item_emb.astype(bf16)
    outgoing = dot(select, item_emb).astype(bf16).reshape(groups, CAP, width)
    incoming = lax.all_to_all(outgoing, "dp", split_axis=0, concat_axis=0, tiled=True)

    swap = [(0, 1), (1, 0)]
    total = dot(select, arrived[:, :width], 0, 0)
    high = lax.reduce_precision(total, 8, 7)
    grads = jnp.concatenate([high, total - high], axis=0).astype(bf16)
    grads_other = lax.ppermute(grads, "core", swap)
    normed, _ = norm_rows(incoming.reshape(groups * CAP, width).astype(f32), user_gain)
    normed = dot(one_hot, normed.astype(bf16)).astype(bf16)
    low, high = normed[:, :half], normed[:, half:]
    act = jnp.where(core == 0, low, high)
    act_other = lax.ppermute(jnp.where(core == 0, high, low), "core", swap)

    steps = 4
    block = half // steps
    piece = pl.BlockSpec((hist_rows, block), lambda i: (0, i))
    once = pl.BlockSpec((2 * item_rows, width), lambda i: (0, 0))
    result = jax.ShapeDtypeStruct((hist_rows, width + half * item_rows // hist_rows), f32)
    keep, send = pl.pallas_call(
        products_kernel,
        grid=(steps,),
        out_shape=[result, result],
        in_specs=[piece, piece, once, once, pl.BlockSpec((block, width), lambda i: (i, 0))],
        out_specs=[pl.BlockSpec(result.shape, lambda i: (0, 0))] * 2,
        scratch_shapes=[
            pltpu.VMEM((2 * hist_rows, width), f32),
            pltpu.VMEM((item_rows, half), f32),
            pltpu.VMEM((item_rows, half), f32),
        ],
        cost_estimate=pl.CostEstimate(
            flops=8 * hist_rows * half * width, bytes_accessed=10 << 20, transcendentals=0
        ),
        compiler_params=pltpu.CompilerParams(vmem_limit_bytes=32 << 20),
    )(act, act_other, grads, grads_other, weight)
    got = lax.ppermute(send, "core", swap)

    vmem = pl.BlockSpec(memory_space=pltpu.VMEM)
    values, item_grad = pl.pallas_call(
        last_kernel,
        out_shape=[
            jax.ShapeDtypeStruct((hist_rows, width), bf16),
            jax.ShapeDtypeStruct((item_rows, width), f32),
        ],
        in_specs=[pl.BlockSpec(memory_space=pltpu.SMEM)] + [vmem] * 6,
        out_specs=[vmem] * 2,
        scratch_shapes=[pltpu.VMEM((item_rows, width), f32)],
        compiler_params=pltpu.CompilerParams(vmem_limit_bytes=32 << 20),
    )(core.reshape(1).astype(jnp.int32), keep, got, hidden, item_emb, item_gain, user_gain)
    return (values, item_grad)


def solution(mesh):
    groups = mesh.shape["dp"]
    mesh = Mesh(mesh.devices.reshape(groups, NX, NY, NCORE), ("dp",) + ROW)
    everywhere = ("dp",) + ROW
    in_specs = (
        P(everywhere, None),
        P(),
        P(everywhere),
        P(ROW, None),
        P(),
        P(ROW, None),
        P(everywhere, None),
    )
    out_specs = (P(everywhere, None), P(everywhere, None))
    return jax.shard_map(local, mesh=mesh, in_specs=in_specs, out_specs=out_specs, check_vma=False)
```

time: 145 us -> 114 us (0.79)
  matrix products: 25.1 us -> 2.01 us
  starting transfers between devices: 57.9 us -> 42.9 us
  Pallas kernels: 0 us -> 8.28 us
  other arithmetic: 9.05 us -> 3.61 us
  waiting for transfers between devices: 32.9 us -> 36.1 us
  local copies, waits for them, and re-layouts: 4.18 us -> 6.29 us
    dot_general x18 -> x4, matrix products: 25.1 us -> 2.01 us  [dot(): lax.dot_general(a, b, (((da,), (db,)), ((), ())), preferred_element_type=...]
    all_to_all x1, waiting for transfers between devices: 0.01 us -> 15.2 us  [local(): lax.all_to_all(outgoing, 'dp', split_axis=0, concat_axis=0, tiled=True)]
    ppermute x11 -> x6, starting transfers between devices: 33.1 us -> 20.3 us  [the longest x3 10.9 us: local(): near.append(lax.ppermute(value_weight, 'x', pairs))]
    pallas_call x0 -> x2, Pallas kernels: none -> 8.28 us  [the longest x1 5.04 us: local(): pl.pallas_call(products_kernel, grid=(steps,), out_shape=[result, result]...]
    all_gather x1, waiting for transfers between devices: 8.53 us -> 1.67 us  [local(): weight = lax.all_gather(seed, 'y', axis=0, tiled=True)]
    all_to_all x1, starting transfers between devices: 18.8 us -> 14.9 us  [local(): lax.all_to_all(sent, 'dp', split_axis=0, concat_axis=0, tiled=True)]
    unnamed x18 -> x24, local copies, waits for them, and re-layouts: 0.69 us -> 4.4 us
    all_to_all x1, waiting for transfers between devices: 18 us -> 15 us  [local(): lax.all_to_all(sent, 'dp', split_axis=0, concat_axis=0, tiled=True)]
  transfers between devices with their start and end apart: 14 -> 9, of which waited for: 5 -> 6; matrix products, arithmetic and copies ran while one was open for 17% -> 6% of each run, Pallas kernels for 0% -> 0%
where the time goes in v4:
time: 114 us
  starting transfers between devices  42.9 us (38%)
  waiting for transfers between devices  36.1 us (32%)
  between operations  14.4 us (13%)
  Pallas kernels  8.28 us (7%)
  local copies, waits for them, and re-layouts  6.29 us (6%)
  other arithmetic  3.61 us (3%)
  matrix products  2.01 us (2%)
    all_to_all x1, waiting for transfers between devices, local(): lax.all_to_all(outgoing, 'dp', split_axis=0, concat_axis=0, tiled=True)  15.2 us
    all_to_all x1, waiting for transfers between devices, local(): lax.all_to_all(sent, 'dp', split_axis=0, concat_axis=0, tiled=True)  15 us
    all_to_all x1, starting transfers between devices, local(): lax.all_to_all(sent, 'dp', split_axis=0, concat_axis=0, tiled=True)  14.9 us
    ppermute x3, starting transfers between devices, local(): near.append(lax.ppermute(value_weight, 'x', pairs))  10.9 us
    all_to_all x1, starting transfers between devices, local(): lax.all_to_all(outgoing, 'dp', split_axis=0, concat_axis=0, tiled=True)  7.71 us
    pallas_call x1, Pallas kernels, local(): pl.pallas_call(products_kernel, grid=(steps,), out_shape=[result, result]...  5.04 us
    unnamed x24, local copies, waits for them, and re-layouts  4.4 us
    ppermute x1, starting transfers between devices, local(): act_other = lax.ppermute(jnp.where(core == 0, high, low), 'core', swap)  3.73 us
  transfers between devices with their start and end apart: 9, of which 6 were waited for; matrix products, arithmetic and copies ran while one was open for 6% of the time, Pallas kernels for 0%

profile of v4, /device:TPU:1, one launch (start us, length us, event | category | flops | bytes accessed | tf_op | source)
XLA Modules:
  0.0 113.6 jit_solution(13331321959187974391)
XLA Ops:
  7.2 5.6 %collective-permute-start.1 = (bf16[32,2048]{1,0:T(8,128)(2,1)}, bf16[32,2048]{1,0:T(8,128)(2,1)S(1)}, u32[]{:S(2)}, u32[]{:S(2)}) collective-permute-start(bf16[32,2048]{1,0:T(8,128)(2,1)} %param.12), channel_id=1, source_target_pairs={{32,0},{48,16},{0,32},{16,48},{33,1},{49,17},{1,33},{17,49},{34,2}... | collective-permute-start | bytes 393224 | tf_op jit(solution)/shard_map/ppermute | solution.py:121
  12.9 2.8 %collective-permute-start = (bf16[32,2048]{1,0:T(8,128)(2,1)}, bf16[32,2048]{1,0:T(8,128)(2,1)S(1)}, u32[]{:S(2)}, u32[]{:S(2)}) collective-permute-start(bf16[32,2048]{1,0:T(8,128)(2,1)} %param.12), channel_id=1, source_target_pairs={{16,0},{32,16},{48,32},{0,48},{17,1},{33,17},{49,33},{1,49},{18,2}... | collective-permute-start | bytes 393224 | tf_op jit(solution)/shard_map/ppermute | solution.py:121
  15.6 2.5 %collective-permute-start.2 = (bf16[32,2048]{1,0:T(8,128)(2,1)}, bf16[32,2048]{1,0:T(8,128)(2,1)S(1)}, u32[]{:S(2)}, u32[]{:S(2)}) collective-permute-start(bf16[32,2048]{1,0:T(8,128)(2,1)} %param.12), channel_id=1, source_target_pairs={{48,0},{0,16},{16,32},{32,48},{49,1},{1,17},{17,33},{33,49},{50,2}... | collective-permute-start | bytes 393224 | tf_op jit(solution)/shard_map/ppermute | solution.py:121
  18.2 0.7 reduce.2
  18.9 0.8 select_reduce_fusion.1
  19.9 0.2 reduce_window_sum.11
  20.3 0.2 select_reduce_fusion
  20.5 0.4 fusion
  20.9 0.8 pad_maximum_fusion.1
  21.8 1.0 collective-permute-done.2
  22.9 0.8 constant_dynamic-slice_fusion
  23.7 14.9 %all-to-all-start = ((bf16[12,8,2176]{2,1,0:T(8,128)(2,1)}), bf16[12,8,2176]{2,1,0:T(8,128)(2,1)S(1)}, u32[]{:S(2)}, u32[]{:S(2)}) async-start(bf16[12,8,2176]{2,1,0:T(8,128)(2,1)} %pad_maximum_fusion.1), calls=%async_computation | async-start | bytes 835584 | tf_op jit(solution)/shard_map/all_to_all | solution.py:146
  38.8 0.3 copy.24
  39.2 0.2 copy.26.hidden
  39.4 0.3 multiply_reduce_fusion
  39.8 15.0 %all-to-all-done = bf16[12,8,2176]{2,1,0:T(8,128)(2,1)S(1)} async-done(((bf16[12,8,2176]{2,1,0:T(8,128)(2,1)}), bf16[12,8,2176]{2,1,0:T(8,128)(2,1)S(1)}, u32[]{:S(2)}, u32[]{:S(2)}) %all-to-all-start) | async-done | bytes 417824 | tf_op jit(solution)/shard_map/all_to_all | solution.py:146
  54.9 1.0 fusion.1
  55.9 7.7 %all-to-all-start.1 = ((bf16[12,8,2048]{2,1,0:T(8,128)(2,1)}), bf16[12,8,2048]{2,1,0:T(8,128)(2,1)S(1)}, u32[]{:S(2)}, u32[]{:S(2)}) async-start(bf16[12,8,2048]{2,1,0:T(8,128)(2,1)} %fusion.1), calls=%async_computation.1 | async-start | bytes 786432 | tf_op jit(solution)/shard_map/all_to_all | solution.py:155
  63.8 0.3 reduce-precision_convert_fusion
  64.1 3.1 %collective-permute-start.4 = (bf16[128,2048]{1,0:T(8,128)(2,1)S(1)}, bf16[128,2048]{1,0:T(8,128)(2,1)S(1)}, u32[]{:S(2)}, u32[]{:S(2)}) collective-permute-start(bf16[128,2048]{1,0:T(8,128)(2,1)S(1)} %pad_maximum_fusion.grads), channel_id=1, source_target_pairs={{0,1},{1,0},{2,3},{3,2},{4,5},{5,4},{6,7},{7,6},{8,9},{9,8},{10,11... | collective-permute-start | bytes 1572872 | tf_op jit(solution)/shard_map/ppermute | solution.py:161
  67.2 15.2 %all-to-all-done.1 = bf16[12,8,2048]{2,1,0:T(8,128)(2,1)S(1)} async-done(((bf16[12,8,2048]{2,1,0:T(8,128)(2,1)}), bf16[12,8,2048]{2,1,0:T(8,128)(2,1)S(1)}, u32[]{:S(2)}, u32[]{:S(2)}) %all-to-all-start.1) | async-done | bytes 393248 | tf_op jit(solution)/shard_map/all_to_all | solution.py:155
  82.7 0.4 convolution_convert_fusion
  83.2 3.7 %collective-permute-start.3 = (bf16[128,1024]{1,0:T(8,128)(2,1)S(1)}, bf16[128,1024]{1,0:T(8,128)(2,1)S(1)}, u32[]{:S(2)}, u32[]{:S(2)}) collective-permute-start(bf16[128,1024]{1,0:T(8,128)(2,1)S(1)} %get-tuple-element.12), channel_id=1, source_target_pairs={{0,1},{1,0},{2,3},{3,2},{4,5},{5,4},{6,7},{7,6},{8,9},{9,8},{10,11... | collective-permute-start | bytes 786440 | tf_op jit(solution)/shard_map/ppermute | solution.py:166
  87.0 0.8 copy-done.2
  87.7 0.3 collective-permute-done.3.act_other
  88.1 1.7 %all-gather.2.cloned.1.call-done.weight = bf16[1024,2048]{1,0:T(8,128)(2,1)} async-done(((bf16[128,2048]{1,0:T(8,128)(2,1)}), bf16[1024,2048]{1,0:T(8,128)(2,1)}) %all-gather.2.cloned.1.call-update) | async-done | bytes 4194320 | tf_op jit(solution)/shard_map/all_gather | solution.py:145
  89.7 2.2 %copy-done.1 = bf16[1024,2048]{1,0:T(8,128)(2,1)S(1)} copy-done((bf16[1024,2048]{1,0:T(8,128)(2,1)S(1)}, bf16[1024,2048]{1,0:T(8,128)(2,1)}, u32[]{:S(2)}) %copy-start.1) | copy-done | bytes 4194328
  91.9 1.0 copy-done.3
  93.0 5.0 %shard_map.86 = (f32[128,2560]{1,0:T(8,128)S(1)}, f32[128,2560]{1,0:T(8,128)}) custom-call(bf16[128,1024]{1,0:T(8,128)(2,1)S(1)} %get-tuple-element.13.act, bf16[128,1024]{1,0:T(8,128)(2,1)S(1)} %collective-permute-done.3.act_other, bf16[128,2048]{1,0:T(8,128)(2,1)S(1)} %pad_maximum_fusion.grads, bf16[128,2048]{1,0:T(8,128)(2,1)S(1)} %copy-done.3, ...), custom_call_target="tpu_custom_call" | custom-call | flops 2147483648 | bytes 10485760 | tf_op jit(solution)/shard_map/pallas_call | solution.py:173
  98.0 2.6 %collective-permute-start.5 = (f32[128,2560]{1,0:T(8,128)}, f32[128,2560]{1,0:T(8,128)}, u32[]{:S(2)}, u32[]{:S(2)}) collective-permute-start(f32[128,2560]{1,0:T(8,128)} %get-tuple-element.9), channel_id=1, source_target_pairs={{0,1},{1,0},{2,3},{3,2},{4,5},{5,4},{6,7},{7,6},{8,9},{9,8},{10,11... | collective-permute-start | bytes 3932168 | tf_op jit(solution)/shard_map/ppermute | solution.py:189
  100.8 2.8 %collective-permute-done.5.got = f32[128,2560]{1,0:T(8,128)} collective-permute-done((f32[128,2560]{1,0:T(8,128)}, f32[128,2560]{1,0:T(8,128)}, u32[]{:S(2)}, u32[]{:S(2)}) %collective-permute-start.5) | collective-permute-done | bytes 1310752 | tf_op jit(solution)/shard_map/ppermute | solution.py:189
  103.6 3.2 %shard_map.87 = (bf16[128,2048]{1,0:T(8,128)(2,1)}, f32[64,2048]{1,0:T(8,128)}) custom-call(s32[1]{0:T(128)} %bitcast.core, f32[128,2560]{1,0:T(8,128)S(1)} %get-tuple-element.8.keep, f32[128,2560]{1,0:T(8,128)} %collective-permute-done.5.got, bf16[64,2048]{1,0:T(8,128)(2,1)S(1)} %copy.26.hidden, bf16[64,2048]{1,0:T(8,128)(2,1)S(1)} %multiply_convert_fusion.item_emb, ...), custom_call_target="tpu_custom_call" | custom-call | tf_op jit(solution)/shard_map/pallas_call | solution.py:192
  (50 shorter events, 1.6 us)
Async XLA Ops:
  7.2 13.4 %copy-start = (bf16[128,2048]{1,0:T(8,128)(2,1)S(1)}, bf16[128,2048]{1,0:T(8,128)(2,1)}, u32[]{:S(2)}) copy-start(bf16[128,2048]{1,0:T(8,128)(2,1)} %param.13) | copy-start | bytes 1572868
  7.2 14.5 %copy-start.4 = (bf16[32,2048]{1,0:T(8,128)(2,1)S(1)}, bf16[32,2048]{1,0:T(8,128)(2,1)}, u32[]{:S(2)}) copy-start(bf16[32,2048]{1,0:T(8,128)(2,1)} %param.12) | copy-start | bytes 393220
  7.2 82.6 %all-gather.2.cloned.1.call-start = ((), (), s32[]{:S(2)}) async-start(), calls=%async_computation.2 | async-start | bytes 4718592 | tf_op jit(solution)/shard_map/all_gather | solution.py:145
  7.2 14.5 %collective-permute-start.1 = (bf16[32,2048]{1,0:T(8,128)(2,1)}, bf16[32,2048]{1,0:T(8,128)(2,1)S(1)}, u32[]{:S(2)}, u32[]{:S(2)}) collective-permute-start(bf16[32,2048]{1,0:T(8,128)(2,1)} %param.12), channel_id=1, source_target_pairs={{32,0},{48,16},{0,32},{16,48},{33,1},{49,17},{1,33},{17,49},{34,2}... | collective-permute-start | bytes 393224 | tf_op jit(solution)/shard_map/ppermute | solution.py:121
  12.9 8.9 %collective-permute-start = (bf16[32,2048]{1,0:T(8,128)(2,1)}, bf16[32,2048]{1,0:T(8,128)(2,1)S(1)}, u32[]{:S(2)}, u32[]{:S(2)}) collective-permute-start(bf16[32,2048]{1,0:T(8,128)(2,1)} %param.12), channel_id=1, source_target_pairs={{16,0},{32,16},{48,32},{0,48},{17,1},{33,17},{49,33},{1,49},{18,2}... | collective-permute-start | bytes 393224 | tf_op jit(solution)/shard_map/ppermute | solution.py:121
  15.6 7.1 %collective-permute-start.2 = (bf16[32,2048]{1,0:T(8,128)(2,1)}, bf16[32,2048]{1,0:T(8,128)(2,1)S(1)}, u32[]{:S(2)}, u32[]{:S(2)}) collective-permute-start(bf16[32,2048]{1,0:T(8,128)(2,1)} %param.12), channel_id=1, source_target_pairs={{48,0},{0,16},{16,32},{32,48},{49,1},{1,17},{17,33},{33,49},{50,2}... | collective-permute-start | bytes 393224 | tf_op jit(solution)/shard_map/ppermute | solution.py:121
  22.8 15.8 %copy-start.6 = (f32[2048]{0:T(1024)S(1)}, f32[2048]{0:T(1024)}, u32[]{:S(2)}) copy-start(f32[2048]{0:T(1024)} %param.8) | copy-start | bytes 24580
  22.9 16.0 %copy-start.5 = (bf16[64,2048]{1,0:T(8,128)(2,1)S(1)}, bf16[64,2048]{1,0:T(8,128)(2,1)}, u32[]{:S(2)}) copy-start(bf16[64,2048]{1,0:T(8,128)(2,1)} %param.7) | copy-start | bytes 786436
  23.7 31.1 %all-to-all-start = ((bf16[12,8,2176]{2,1,0:T(8,128)(2,1)}), bf16[12,8,2176]{2,1,0:T(8,128)(2,1)S(1)}, u32[]{:S(2)}, u32[]{:S(2)}) async-start(bf16[12,8,2176]{2,1,0:T(8,128)(2,1)} %pad_maximum_fusion.1), calls=%async_computation | async-start | bytes 835584 | tf_op jit(solution)/shard_map/all_to_all | solution.py:146
  39.4 24.2 %copy-start.7 = (f32[2048]{0:T(1024)S(1)}, f32[2048]{0:T(1024)}, u32[]{:S(2)}) copy-start(f32[2048]{0:T(1024)} %param.11) | copy-start | bytes 24580
  55.9 26.6 %all-to-all-start.1 = ((bf16[12,8,2048]{2,1,0:T(8,128)(2,1)}), bf16[12,8,2048]{2,1,0:T(8,128)(2,1)S(1)}, u32[]{:S(2)}, u32[]{:S(2)}) async-start(bf16[12,8,2048]{2,1,0:T(8,128)(2,1)} %fusion.1), calls=%async_computation.1 | async-start | bytes 786432 | tf_op jit(solution)/shard_map/all_to_all | solution.py:155
  64.1 22.8 %collective-permute-start.4 = (bf16[128,2048]{1,0:T(8,128)(2,1)S(1)}, bf16[128,2048]{1,0:T(8,128)(2,1)S(1)}, u32[]{:S(2)}, u32[]{:S(2)}) collective-permute-start(bf16[128,2048]{1,0:T(8,128)(2,1)S(1)} %pad_maximum_fusion.grads), channel_id=1, source_target_pairs={{0,1},{1,0},{2,3},{3,2},{4,5},{5,4},{6,7},{7,6},{8,9},{9,8},{10,11... | collective-permute-start | bytes 1572872 | tf_op jit(solution)/shard_map/ppermute | solution.py:161
  83.2 4.9 %collective-permute-start.3 = (bf16[128,1024]{1,0:T(8,128)(2,1)S(1)}, bf16[128,1024]{1,0:T(8,128)(2,1)S(1)}, u32[]{:S(2)}, u32[]{:S(2)}) collective-permute-start(bf16[128,1024]{1,0:T(8,128)(2,1)S(1)} %get-tuple-element.12), channel_id=1, source_target_pairs={{0,1},{1,0},{2,3},{3,2},{4,5},{5,4},{6,7},{7,6},{8,9},{9,8},{10,11... | collective-permute-start | bytes 786440 | tf_op jit(solution)/shard_map/ppermute | solution.py:166
  86.9 0.8 copy-start.2
  89.7 2.2 %copy-start.1 = (bf16[1024,2048]{1,0:T(8,128)(2,1)S(1)}, bf16[1024,2048]{1,0:T(8,128)(2,1)}, u32[]{:S(2)}) copy-start(bf16[1024,2048]{1,0:T(8,128)(2,1)} %all-gather.2.cloned.1.call-done.weight) | copy-start | bytes 12582916
  91.9 1.0 copy-start.3
  98.0 5.5 %collective-permute-start.5 = (f32[128,2560]{1,0:T(8,128)}, f32[128,2560]{1,0:T(8,128)}, u32[]{:S(2)}, u32[]{:S(2)}) collective-permute-start(f32[128,2560]{1,0:T(8,128)} %get-tuple-element.9), channel_id=1, source_target_pairs={{0,1},{1,0},{2,3},{3,2},{4,5},{5,4},{6,7},{7,6},{8,9},{9,8},{10,11... | collective-permute-start | bytes 3932168 | tf_op jit(solution)/shard_map/ppermute | solution.py:189
Sparse Core Ops, SparseCore 0:
  23.9 65.8 all-gather.1

commit v5 on v4

--- a/solution.py
+++ b/solution.py
@@ -26,9 +26,9 @@
 
 def locate(owner_row, items):
     matches = items[:, None] == lax.broadcasted_iota(
-        jnp.int32, (items.shape[0], owner_row.shape[0]), 1
+        jnp.int32, (items.shape[0], owner_row.shape[1]), 1
     )
-    return jnp.sum(jnp.where(matches, owner_row[None, :], 0), axis=1)
+    return jnp.sum(jnp.where(matches, owner_row, 0), axis=1)
 
 
 def dot(a, b, da=1, db=0):
@@ -41,41 +41,34 @@
     return a.reshape(a.shape[0], -1)
 
 
-def products(act, act_other, grads, grads_other, weight, acc, up, up_other):
-    forward = dot(jnp.concatenate([act[...], act_other[...]], axis=0), weight[...])
-    back = dot(jnp.concatenate([grads[...], grads_other[...]], axis=0), weight[...], 1, 1)
-
-    @pl.when(pl.program_id(0) == 0)
-    def _():
-        acc[...] = forward
-
-    @pl.when(pl.program_id(0) > 0)
-    def _():
-        acc[...] += forward
-
-    rows = up.shape[0]
-    up[...] = back[:rows] + back[rows : 2 * rows]
-    up_other[...] = back[2 * rows : 3 * rows] + back[3 * rows :]
-
-
-def products_kernel(act, act_other, grads, grads_other, weight, keep, send, acc, up, up_other):
-    step, steps = pl.program_id(0), pl.num_programs(0)
-    block, width = weight.shape
-    items = up.shape[0]
-    at = pl.ds(pl.multiple_of(step * block, block), block)
-    products(
-        act, act_other, grads, grads_other, weight, acc, up.at[:, at], up_other.at[:, at]
-    )
-
-    @pl.when(step == steps - 1)
-    def _():
-        rows = act.shape[0]
-        half = up.shape[1] // 2
-        keep[:, :width] = acc[:rows]
-        send[:, :width] = acc[rows:]
-        for ref, sums in ((keep, up), (send, up_other)):
-            ref[:items, width:] = sums[:, :half]
-            ref[items:, width:] = sums[:, half:]
+def products_kernel(act, act_other, grads, grads_other, weight, keep, send, held, sems):
+    parts = sems.shape[0]
+    block = held.shape[0] // parts
+    cuts = [slice(i * block, (i + 1) * block) for i in range(parts)]
+    copies = [
+        pltpu.make_async_copy(weight.at[cut], held.at[cut], sems.at[i])
+        for i, cut in enumerate(cuts)
+    ]
+    for copy in copies:
+        copy.start()
+    rows, half = act.shape
+    width = held.shape[1]
+    items = grads.shape[0] // 2
+    both = jnp.concatenate([grads[...], grads_other[...]], axis=0)
+    for i, (copy, cut) in enumerate(zip(copies, cuts)):
+        copy.wait()
+        back = dot(both, held[cut], 1, 1)
+        row, column = divmod(i * block, half // 2)
+        row = row * items
+        at = slice(width + column, width + column + block)
+        keep[row : row + items, at] = back[:items] + back[items : 2 * items]
+        send[row : row + items, at] = back[2 * items : 3 * items] + back[3 * items :]
+    both = jnp.concatenate([act[...], act_other[...]], axis=0)
+    for i in range(parts):
+        at = slice(i * width // parts, (i + 1) * width // parts)
+        forward = dot(both, held[:, at])
+        keep[:, at] = forward[:rows]
+        send[:, at] = forward[rows:]
 
 
 def last_kernel(core, keep, got, hidden, item_emb, item_gain, user_gain, values, item_grad, up):
@@ -110,25 +103,16 @@
     groups = lax.axis_size("dp")
     item_rows, width = item_hidden.shape
     hist_rows = history.shape[0]
-    shard = value_weight.shape[0]
     half = width // 2
     core = lax.axis_index("core")
     f32, bf16 = jnp.float32, jnp.bfloat16
 
-    near = [value_weight]
-    for step in range(1, NX):
-        pairs = [((x + step) % NX, x) for x in range(NX)]
-        near.append(lax.ppermute(value_weight, "x", pairs))
-    seed = lax.dynamic_slice_in_dim(
-        jnp.concatenate(near + near, axis=0),
-        (NX - lax.axis_index("x")) % NX * shard,
-        NX * shard,
-        axis=0,
-    )
+    seed = lax.all_gather(value_weight, "x", axis=0, tiled=True)
+    history, seed = lax.optimization_barrier((history, seed))
+    weight = lax.all_gather(seed, "y", axis=0, tiled=True)
 
-    owner_row = owner_map[0]
-    pool = owner_row.shape[0]
-    stored = locate(owner_row, history)
+    pool = owner_map.shape[1]
+    stored = locate(owner_map, history)
     pick = stored[:, None] == lax.broadcasted_iota(jnp.int32, (hist_rows, pool), 1)
     wanted = jnp.any(pick, axis=0).reshape(groups, item_rows)
     slot = jnp.cumsum(wanted.astype(jnp.int32), axis=1) - 1
@@ -141,8 +125,7 @@
     slot_ids = lax.broadcasted_iota(jnp.int32, (groups, CAP, item_rows), 1)
     asked = (wanted[:, None, :] & (slot[:, None, :] == slot_ids)).astype(bf16)
     asked = jnp.pad(asked, ((0, 0), (0, 0), (0, -item_rows % 128)))
-    sent, seed = lax.optimization_barrier((jnp.concatenate([grad_sums, asked], axis=2), seed))
-    weight = lax.all_gather(seed, "y", axis=0, tiled=True)
+    sent = jnp.concatenate([grad_sums, asked], axis=2)
     arrived = lax.all_to_all(sent, "dp", split_axis=0, concat_axis=0, tiled=True)
     arrived = arrived.reshape(groups * CAP, -1)
     select = arrived[:, width : width + item_rows]
@@ -165,30 +148,20 @@
     act = jnp.where(core == 0, low, high)
     act_other = lax.ppermute(jnp.where(core == 0, high, low), "core", swap)
 
-    steps = 4
-    block = half // steps
-    piece = pl.BlockSpec((hist_rows, block), lambda i: (0, i))
-    once = pl.BlockSpec((2 * item_rows, width), lambda i: (0, 0))
+    vmem = pl.BlockSpec(memory_space=pltpu.VMEM)
     result = jax.ShapeDtypeStruct((hist_rows, width + half * item_rows // hist_rows), f32)
     keep, send = pl.pallas_call(
         products_kernel,
-        grid=(steps,),
         out_shape=[result, result],
-        in_specs=[piece, piece, once, once, pl.BlockSpec((block, width), lambda i: (i, 0))],
-        out_specs=[pl.BlockSpec(result.shape, lambda i: (0, 0))] * 2,
-        scratch_shapes=[
-            pltpu.VMEM((2 * hist_rows, width), f32),
-            pltpu.VMEM((item_rows, half), f32),
-            pltpu.VMEM((item_rows, half), f32),
-        ],
+        in_specs=[vmem] * 4 + [pl.BlockSpec(memory_space=pltpu.HBM)],
+        out_specs=[vmem] * 2,
+        scratch_shapes=[pltpu.VMEM((half, width), bf16), pltpu.SemaphoreType.DMA((4,))],
         cost_estimate=pl.CostEstimate(
             flops=8 * hist_rows * half * width, bytes_accessed=10 << 20, transcendentals=0
         ),
-        compiler_params=pltpu.CompilerParams(vmem_limit_bytes=32 << 20),
+        compiler_params=pltpu.CompilerParams(vmem_limit_bytes=52 << 20),
     )(act, act_other, grads, grads_other, weight)
     got = lax.ppermute(send, "core", swap)
-
-    vmem = pl.BlockSpec(memory_space=pltpu.VMEM)
     values, item_grad = pl.pallas_call(
         last_kernel,
         out_shape=[
@@ -198,7 +171,7 @@
         in_specs=[pl.BlockSpec(memory_space=pltpu.SMEM)] + [vmem] * 6,
         out_specs=[vmem] * 2,
         scratch_shapes=[pltpu.VMEM((item_rows, width), f32)],
-        compiler_params=pltpu.CompilerParams(vmem_limit_bytes=32 << 20),
+        compiler_params=pltpu.CompilerParams(vmem_limit_bytes=12 << 20),
     )(core.reshape(1).astype(jnp.int32), keep, got, hidden, item_emb, item_gain, user_gain)
     return (values, item_grad)
 

time: 114 us -> 111 us (0.974)
  blocking collectives: 0 us -> 13.2 us
  starting transfers between devices: 42.9 us -> 35.5 us
  waiting for transfers between devices: 36.1 us -> 30.8 us
  local copies, waits for them, and re-layouts: 6.29 us -> 2.67 us
    all_gather x0 -> x1, blocking collectives: none -> 13.2 us  [local(): seed = lax.all_gather(value_weight, 'x', axis=0, tiled=True)]
    ppermute x3 -> x0, starting transfers between devices: 10.9 us -> none  [local(): near.append(lax.ppermute(value_weight, 'x', pairs))]
    all_to_all x1, waiting for transfers between devices: 15.2 us -> 10.3 us  [local(): lax.all_to_all(outgoing, 'dp', split_axis=0, concat_axis=0, tiled=True)]
    ppermute x1, starting transfers between devices: 3.73 us -> 7.15 us  [local(): act_other = lax.ppermute(jnp.where(core == 0, high, low), 'core', swap)]
    unnamed x24 -> x11, local copies, waits for them, and re-layouts: 4.4 us -> 1.62 us
    pallas_call x1, Pallas kernels: 5.04 us -> 6.74 us  [local(): pl.pallas_call(products_kernel, out_shape=[result, result], in_specs=[vme...]
    ppermute x1, starting transfers between devices: 3.12 us -> 4.77 us  [local(): grads_other = lax.ppermute(grads, 'core', swap)]
    all_to_all x1, starting transfers between devices: 7.71 us -> 6.13 us  [local(): lax.all_to_all(outgoing, 'dp', split_axis=0, concat_axis=0, tiled=True)]
  transfers between devices with their start and end apart: 9 -> 6, of which waited for: 6 -> 5; matrix products, arithmetic and copies ran while one was open for 6% -> 6% of each run, Pallas kernels for 0% -> 0%
where the time goes in v5:
time: 111 us
  starting transfers between devices  35.5 us (32%)
  waiting for transfers between devices  30.8 us (28%)
  between operations  14.3 us (13%)
  blocking collectives  13.2 us (12%)
  Pallas kernels  8.71 us (8%)
  other arithmetic  3.6 us (3%)
  local copies, waits for them, and re-layouts  2.67 us (2%)
  matrix products  2.01 us (2%)
    all_to_all x1, waiting for transfers between devices, local(): lax.all_to_all(sent, 'dp', split_axis=0, concat_axis=0, tiled=True)  14.9 us
    all_to_all x1, starting transfers between devices, local(): lax.all_to_all(sent, 'dp', split_axis=0, concat_axis=0, tiled=True)  14.9 us
    all_gather x1, blocking collectives, local(): seed = lax.all_gather(value_weight, 'x', axis=0, tiled=True)  13.2 us
    all_to_all x1, waiting for transfers between devices, local(): lax.all_to_all(outgoing, 'dp', split_axis=0, concat_axis=0, tiled=True)  10.3 us
    ppermute x1, starting transfers between devices, local(): act_other = lax.ppermute(jnp.where(core == 0, high, low), 'core', swap)  7.15 us
    pallas_call x1, Pallas kernels, local(): pl.pallas_call(products_kernel, out_shape=[result, result], in_specs=[vme...  6.74 us
    all_to_all x1, starting transfers between devices, local(): lax.all_to_all(outgoing, 'dp', split_axis=0, concat_axis=0, tiled=True)  6.13 us
    ppermute x1, starting transfers between devices, local(): grads_other = lax.ppermute(grads, 'core', swap)  4.77 us
  transfers between devices with their start and end apart: 6, of which 5 were waited for; matrix products, arithmetic and copies ran while one was open for 6% of the time, Pallas kernels for 0%

profile of v5, /device:TPU:1, one launch (start us, length us, event | category | flops | bytes accessed | tf_op | source)
XLA Modules:
  0.0 110.8 jit_solution(6005291099041494139)
XLA Ops:
  7.2 13.2 %all_gather.6 = bf16[128,2048]{1,0:T(8,128)(2,1)} all-gather(bf16[32,2048]{1,0:T(8,128)(2,1)} %param.12), channel_id=1, replica_groups=mesh['dp'=12,'x'=4,'y'=8,'core'=2] {'x'}, dimensions={0}, use_global_device_ids=true | all-gather | bytes 655360 | tf_op jit(solution)/shard_map/all_gather | solution.py:110
  20.4 0.7 reduce.2
  21.1 0.8 select_reduce_fusion.1
  22.0 0.1 fusion.12
  22.2 0.2 reduce_window_sum.11
  22.6 0.2 select_reduce_fusion
  22.8 0.4 fusion
  23.2 0.8 pad_maximum_fusion.1
  24.0 14.9 %all-to-all-start = ((bf16[12,8,2176]{2,1,0:T(8,128)(2,1)}), bf16[12,8,2176]{2,1,0:T(8,128)(2,1)S(1)}, u32[]{:S(2)}, u32[]{:S(2)}) async-start(bf16[12,8,2176]{2,1,0:T(8,128)(2,1)} %pad_maximum_fusion.1), calls=%async_computation | async-start | bytes 835584 | tf_op jit(solution)/shard_map/all_to_all | solution.py:129
  39.1 0.3 copy.24
  39.4 0.2 copy.26.hidden
  39.6 0.3 multiply_reduce_fusion
  39.9 0.1 multiply_convert_fusion.item_emb
  40.1 14.9 %all-to-all-done = bf16[12,8,2176]{2,1,0:T(8,128)(2,1)S(1)} async-done(((bf16[12,8,2176]{2,1,0:T(8,128)(2,1)}), bf16[12,8,2176]{2,1,0:T(8,128)(2,1)S(1)}, u32[]{:S(2)}, u32[]{:S(2)}) %all-to-all-start) | async-done | bytes 417824 | tf_op jit(solution)/shard_map/all_to_all | solution.py:129
  55.0 1.0 fusion.1
  56.0 6.1 %all-to-all-start.1 = ((bf16[12,8,2048]{2,1,0:T(8,128)(2,1)}), bf16[12,8,2048]{2,1,0:T(8,128)(2,1)S(1)}, u32[]{:S(2)}, u32[]{:S(2)}) async-start(bf16[12,8,2048]{2,1,0:T(8,128)(2,1)} %fusion.1), calls=%async_computation.1 | async-start | bytes 786432 | tf_op jit(solution)/shard_map/all_to_all | solution.py:138
  62.1 0.1 reshape_reshape.7
  62.3 0.3 reduce-precision_convert_fusion
  62.6 4.8 %collective-permute-start.1 = (bf16[128,2048]{1,0:T(8,128)(2,1)S(1)}, bf16[128,2048]{1,0:T(8,128)(2,1)S(1)}, u32[]{:S(2)}, u32[]{:S(2)}) collective-permute-start(bf16[128,2048]{1,0:T(8,128)(2,1)S(1)} %pad_maximum_fusion.grads), channel_id=1, source_target_pairs={{0,1},{1,0},{2,3},{3,2},{4,5},{5,4},{6,7},{7,6},{8,9},{9,8},{10,11... | collective-permute-start | bytes 1572872 | tf_op jit(solution)/shard_map/ppermute | solution.py:144
  67.4 10.3 %all-to-all-done.1 = bf16[12,8,2048]{2,1,0:T(8,128)(2,1)S(1)} async-done(((bf16[12,8,2048]{2,1,0:T(8,128)(2,1)}), bf16[12,8,2048]{2,1,0:T(8,128)(2,1)S(1)}, u32[]{:S(2)}, u32[]{:S(2)}) %all-to-all-start.1) | async-done | bytes 393248 | tf_op jit(solution)/shard_map/all_to_all | solution.py:138
  77.7 0.2 fusion.5
  78.0 0.4 convolution_convert_fusion
  78.4 7.2 %collective-permute-start = (bf16[128,1024]{1,0:T(8,128)(2,1)S(1)}, bf16[128,1024]{1,0:T(8,128)(2,1)S(1)}, u32[]{:S(2)}, u32[]{:S(2)}) collective-permute-start(bf16[128,1024]{1,0:T(8,128)(2,1)S(1)} %get-tuple-element.12), channel_id=1, source_target_pairs={{0,1},{1,0},{2,3},{3,2},{4,5},{5,4},{6,7},{7,6},{8,9},{9,8},{10,11... | collective-permute-start | bytes 786440 | tf_op jit(solution)/shard_map/ppermute | solution.py:149
  85.6 1.1 %collective-permute-done.act_other = bf16[128,1024]{1,0:T(8,128)(2,1)S(1)} collective-permute-done((bf16[128,1024]{1,0:T(8,128)(2,1)S(1)}, bf16[128,1024]{1,0:T(8,128)(2,1)S(1)}, u32[]{:S(2)}, u32[]{:S(2)}) %collective-permute-start) | collective-permute-done | bytes 262176 | tf_op jit(solution)/shard_map/ppermute | solution.py:149
  86.7 1.7 %all-gather.2.cloned.1.call-done.weight = bf16[1024,2048]{1,0:T(8,128)(2,1)} async-done(((bf16[128,2048]{1,0:T(8,128)(2,1)}), bf16[1024,2048]{1,0:T(8,128)(2,1)}) %all-gather.2.cloned.1.call-update) | async-done | bytes 4194320 | tf_op jit(solution)/shard_map/all_gather | solution.py:112
  88.4 6.7 %shard_map.86 = (f32[128,2560]{1,0:T(8,128)}, f32[128,2560]{1,0:T(8,128)}) custom-call(bf16[128,1024]{1,0:T(8,128)(2,1)S(1)} %get-tuple-element.13.act, bf16[128,1024]{1,0:T(8,128)(2,1)S(1)} %collective-permute-done.act_other, bf16[128,2048]{1,0:T(8,128)(2,1)S(1)} %pad_maximum_fusion.grads, bf16[128,2048]{1,0:T(8,128)(2,1)S(1)} %collective-permute-done.1.grads_other, ...), custom_call_target="tpu_custom_call" | custom-call | flops 2147483648 | bytes 10485760 | tf_op jit(solution)/shard_map/pallas_call | solution.py:153
  95.2 2.6 %collective-permute-start.2 = (f32[128,2560]{1,0:T(8,128)}, f32[128,2560]{1,0:T(8,128)S(1)}, u32[]{:S(2)}, u32[]{:S(2)}) collective-permute-start(f32[128,2560]{1,0:T(8,128)} %get-tuple-element.9), channel_id=1, source_target_pairs={{0,1},{1,0},{2,3},{3,2},{4,5},{5,4},{6,7},{7,6},{8,9},{9,8},{10,11... | collective-permute-start | bytes 3932168 | tf_op jit(solution)/shard_map/ppermute | solution.py:164
  97.8 0.1 reshape.103.item_gain
  97.9 0.1 reshape.104.user_gain
  97.9 2.7 %collective-permute-done.2.got = f32[128,2560]{1,0:T(8,128)S(1)} collective-permute-done((f32[128,2560]{1,0:T(8,128)}, f32[128,2560]{1,0:T(8,128)S(1)}, u32[]{:S(2)}, u32[]{:S(2)}) %collective-permute-start.2) | collective-permute-done | bytes 1310752 | tf_op jit(solution)/shard_map/ppermute | solution.py:164
  100.6 1.3 %copy-done.1 = f32[128,2560]{1,0:T(8,128)S(1)} copy-done((f32[128,2560]{1,0:T(8,128)S(1)}, f32[128,2560]{1,0:T(8,128)}, u32[]{:S(2)}) %copy-start.1) | copy-done | bytes 1310744
  101.9 2.0 %shard_map.87 = (bf16[128,2048]{1,0:T(8,128)(2,1)}, f32[64,2048]{1,0:T(8,128)}) custom-call(s32[1]{0:T(128)} %bitcast.core, f32[128,2560]{1,0:T(8,128)S(1)} %copy-done.1, f32[128,2560]{1,0:T(8,128)S(1)} %collective-permute-done.2.got, bf16[64,2048]{1,0:T(8,128)(2,1)S(1)} %copy.26.hidden, bf16[64,2048]{1,0:T(8,128)(2,1)S(1)} %multiply_convert_fusion.item_emb, ...), custom_call_target="tpu_custom_call" | custom-call | tf_op jit(solution)/shard_map/pallas_call | solution.py:165
  (30 shorter events, 0.8 us)
Async XLA Ops:
  7.2 15.6 %copy-start = (bf16[128,2048]{1,0:T(8,128)(2,1)S(1)}, bf16[128,2048]{1,0:T(8,128)(2,1)}, u32[]{:S(2)}) copy-start(bf16[128,2048]{1,0:T(8,128)(2,1)} %param.13) | copy-start | bytes 1572868
  7.2 81.2 %all-gather.2.cloned.1.call-start = ((), (), s32[]{:S(2)}) async-start(), calls=%async_computation.2 | async-start | bytes 4718592 | tf_op jit(solution)/shard_map/all_gather | solution.py:112
  22.5 16.3 %copy-start.3 = (f32[2048]{0:T(1024)S(1)}, f32[2048]{0:T(1024)}, u32[]{:S(2)}) copy-start(f32[2048]{0:T(1024)} %param.8) | copy-start | bytes 24580
  22.8 16.3 %copy-start.2 = (bf16[64,2048]{1,0:T(8,128)(2,1)S(1)}, bf16[64,2048]{1,0:T(8,128)(2,1)}, u32[]{:S(2)}) copy-start(bf16[64,2048]{1,0:T(8,128)(2,1)} %param.7) | copy-start | bytes 786436
  24.0 31.0 %all-to-all-start = ((bf16[12,8,2176]{2,1,0:T(8,128)(2,1)}), bf16[12,8,2176]{2,1,0:T(8,128)(2,1)S(1)}, u32[]{:S(2)}, u32[]{:S(2)}) async-start(bf16[12,8,2176]{2,1,0:T(8,128)(2,1)} %pad_maximum_fusion.1), calls=%async_computation | async-start | bytes 835584 | tf_op jit(solution)/shard_map/all_to_all | solution.py:129
  39.6 22.5 %copy-start.4 = (f32[2048]{0:T(1024)S(1)}, f32[2048]{0:T(1024)}, u32[]{:S(2)}) copy-start(f32[2048]{0:T(1024)} %param.11) | copy-start | bytes 24580
  56.0 21.8 %all-to-all-start.1 = ((bf16[12,8,2048]{2,1,0:T(8,128)(2,1)}), bf16[12,8,2048]{2,1,0:T(8,128)(2,1)S(1)}, u32[]{:S(2)}, u32[]{:S(2)}) async-start(bf16[12,8,2048]{2,1,0:T(8,128)(2,1)} %fusion.1), calls=%async_computation.1 | async-start | bytes 786432 | tf_op jit(solution)/shard_map/all_to_all | solution.py:138
  62.6 23.0 %collective-permute-start.1 = (bf16[128,2048]{1,0:T(8,128)(2,1)S(1)}, bf16[128,2048]{1,0:T(8,128)(2,1)S(1)}, u32[]{:S(2)}, u32[]{:S(2)}) collective-permute-start(bf16[128,2048]{1,0:T(8,128)(2,1)S(1)} %pad_maximum_fusion.grads), channel_id=1, source_target_pairs={{0,1},{1,0},{2,3},{3,2},{4,5},{5,4},{6,7},{7,6},{8,9},{9,8},{10,11... | collective-permute-start | bytes 1572872 | tf_op jit(solution)/shard_map/ppermute | solution.py:144
  78.4 8.3 %collective-permute-start = (bf16[128,1024]{1,0:T(8,128)(2,1)S(1)}, bf16[128,1024]{1,0:T(8,128)(2,1)S(1)}, u32[]{:S(2)}, u32[]{:S(2)}) collective-permute-start(bf16[128,1024]{1,0:T(8,128)(2,1)S(1)} %get-tuple-element.12), channel_id=1, source_target_pairs={{0,1},{1,0},{2,3},{3,2},{4,5},{5,4},{6,7},{7,6},{8,9},{9,8},{10,11... | collective-permute-start | bytes 786440 | tf_op jit(solution)/shard_map/ppermute | solution.py:149
  95.2 5.4 %collective-permute-start.2 = (f32[128,2560]{1,0:T(8,128)}, f32[128,2560]{1,0:T(8,128)S(1)}, u32[]{:S(2)}, u32[]{:S(2)}) collective-permute-start(f32[128,2560]{1,0:T(8,128)} %get-tuple-element.9), channel_id=1, source_target_pairs={{0,1},{1,0},{2,3},{3,2},{4,5},{5,4},{6,7},{7,6},{8,9},{9,8},{10,11... | collective-permute-start | bytes 3932168 | tf_op jit(solution)/shard_map/ppermute | solution.py:164
  100.6 1.3 %copy-start.1 = (f32[128,2560]{1,0:T(8,128)S(1)}, f32[128,2560]{1,0:T(8,128)}, u32[]{:S(2)}) copy-start(f32[128,2560]{1,0:T(8,128)} %get-tuple-element.8.keep) | copy-start | bytes 3932164
Sparse Core Ops, SparseCore 0:
  20.6 67.8 all-gather.1

commit v6 on v5

--- a/solution.py
+++ b/solution.py
@@ -41,7 +41,7 @@
     return a.reshape(a.shape[0], -1)
 
 
-def products_kernel(act, act_other, grads, grads_other, weight, keep, send, held, sems):
+def fetch(weight, held, sems):
     parts = sems.shape[0]
     block = held.shape[0] // parts
     cuts = [slice(i * block, (i + 1) * block) for i in range(parts)]
@@ -51,37 +51,58 @@
     ]
     for copy in copies:
         copy.start()
-    rows, half = act.shape
-    width = held.shape[1]
+    return cuts, copies
+
+
+def sent_kernel(act_other, grads, grads_other, weight, up, send, held, ready, sems, out_sems):
+    cuts, copies = fetch(weight, held, sems)
+    half, width = held.shape
     items = grads.shape[0] // 2
     both = jnp.concatenate([grads[...], grads_other[...]], axis=0)
-    for i, (copy, cut) in enumerate(zip(copies, cuts)):
+    for cut, copy in zip(cuts, copies):
         copy.wait()
         back = dot(both, held[cut], 1, 1)
-        row, column = divmod(i * block, half // 2)
-        row = row * items
-        at = slice(width + column, width + column + block)
-        keep[row : row + items, at] = back[:items] + back[items : 2 * items]
-        send[row : row + items, at] = back[2 * items : 3 * items] + back[3 * items :]
-    both = jnp.concatenate([act[...], act_other[...]], axis=0)
+        row, column = divmod(cut.start, half // 2)
+        row, to = row * items, slice(column, column + cut.stop - cut.start)
+        up[row : row + items, to] = back[:items] + back[items : 2 * items]
+        to = slice(width + to.start, width + to.stop)
+        ready[row : row + items, to] = back[2 * items : 3 * items] + back[3 * items :]
+    parts = len(cuts)
+    ends = [i * width // parts for i in range(parts + 1)] + [send.shape[1]]
+    outs = [
+        pltpu.make_async_copy(ready.at[:, lo:hi], send.at[:, lo:hi], out_sems.at[i])
+        for i, (lo, hi) in enumerate(zip(ends[:-1], ends[1:]))
+    ]
+    outs[-1].start()
     for i in range(parts):
-        at = slice(i * width // parts, (i + 1) * width // parts)
-        forward = dot(both, held[:, at])
-        keep[:, at] = forward[:rows]
-        send[:, at] = forward[rows:]
-
-
-def last_kernel(core, keep, got, hidden, item_emb, item_gain, user_gain, values, item_grad, up):
+        at = slice(ends[i], ends[i + 1])
+        ready[:, at] = dot(act_other[...], held[:, at])
+        outs[i].start()
+    for out in outs:
+        out.wait()
+
+
+def kept_kernel(act, weight, keep, held, sems):
+    cuts, copies = fetch(weight, held, sems)
+    total = None
+    for cut, copy in zip(cuts, copies):
+        copy.wait()
+        part = dot(act[:, cut], held[cut])
+        total = part if total is None else total + part
+    keep[...] = total
+
+
+def last_kernel(core, keep, sums, got, hidden, item_emb, item_gain, user_gain, values, item_grad, up):
     width = values.shape[1]
     items = hidden.shape[0]
-    block = keep.shape[1] - width
+    block = sums.shape[1]
     part = width // (NX * NY * NCORE)
     tile = part * NX
-    values[...] = (keep[:, :width] + got[:, :width]).astype(jnp.bfloat16)
-    for side, ref in ((core[0], keep), (1 - core[0], got)):
+    values[...] = (keep[...] + got[:, :width]).astype(jnp.bfloat16)
+    for side, ref, skip in ((core[0], sums, 0), (1 - core[0], got, width)):
         for piece in range(2):
             at = pl.multiple_of((2 * side + piece) * block, block)
-            up[:, pl.ds(at, block)] = ref[piece * items : (piece + 1) * items, width:]
+            up[:, pl.ds(at, block)] = ref[piece * items : (piece + 1) * items, skip:]
     x = item_emb[...].astype(jnp.float32)
     scale = lax.rsqrt(jnp.mean(x * x, axis=1, keepdims=True) + eps)
     emb_grad = norm_back(x, user_gain[...], scale, up[...])
@@ -149,30 +170,48 @@
     act_other = lax.ppermute(jnp.where(core == 0, high, low), "core", swap)
 
     vmem = pl.BlockSpec(memory_space=pltpu.VMEM)
-    result = jax.ShapeDtypeStruct((hist_rows, width + half * item_rows // hist_rows), f32)
-    keep, send = pl.pallas_call(
-        products_kernel,
-        out_shape=[result, result],
-        in_specs=[vmem] * 4 + [pl.BlockSpec(memory_space=pltpu.HBM)],
-        out_specs=[vmem] * 2,
-        scratch_shapes=[pltpu.VMEM((half, width), bf16), pltpu.SemaphoreType.DMA((4,))],
-        cost_estimate=pl.CostEstimate(
-            flops=8 * hist_rows * half * width, bytes_accessed=10 << 20, transcendentals=0
-        ),
+    hbm = pl.BlockSpec(memory_space=pltpu.HBM)
+    extra = half * item_rows // hist_rows
+    held = [pltpu.VMEM((half, width), bf16)]
+    flops = 2 * hist_rows * half * width
+    sums, send = pl.pallas_call(
+        sent_kernel,
+        out_shape=[
+            jax.ShapeDtypeStruct((hist_rows, extra), f32),
+            jax.ShapeDtypeStruct((hist_rows, width + extra), f32),
+        ],
+        in_specs=[vmem] * 3 + [hbm],
+        out_specs=[vmem, hbm],
+        scratch_shapes=held
+        + [
+            pltpu.VMEM((hist_rows, width + extra), f32),
+            pltpu.SemaphoreType.DMA((4,)),
+            pltpu.SemaphoreType.DMA((5,)),
+        ],
+        cost_estimate=pl.CostEstimate(flops=3 * flops, bytes_accessed=6 << 20, transcendentals=0),
         compiler_params=pltpu.CompilerParams(vmem_limit_bytes=52 << 20),
-    )(act, act_other, grads, grads_other, weight)
+    )(act_other, grads, grads_other, weight)
     got = lax.ppermute(send, "core", swap)
+    (keep,) = pl.pallas_call(
+        kept_kernel,
+        out_shape=[jax.ShapeDtypeStruct((hist_rows, width), f32)],
+        in_specs=[vmem, hbm],
+        out_specs=[vmem],
+        scratch_shapes=held + [pltpu.SemaphoreType.DMA((4,))],
+        cost_estimate=pl.CostEstimate(flops=flops, bytes_accessed=5 << 20, transcendentals=0),
+        compiler_params=pltpu.CompilerParams(vmem_limit_bytes=52 << 20),
+    )(act, weight)
     values, item_grad = pl.pallas_call(
         last_kernel,
         out_shape=[
             jax.ShapeDtypeStruct((hist_rows, width), bf16),
             jax.ShapeDtypeStruct((item_rows, width), f32),
         ],
-        in_specs=[pl.BlockSpec(memory_space=pltpu.SMEM)] + [vmem] * 6,
+        in_specs=[pl.BlockSpec(memory_space=pltpu.SMEM)] + [vmem] * 7,
         out_specs=[vmem] * 2,
         scratch_shapes=[pltpu.VMEM((item_rows, width), f32)],
         compiler_params=pltpu.CompilerParams(vmem_limit_bytes=12 << 20),
-    )(core.reshape(1).astype(jnp.int32), keep, got, hidden, item_emb, item_gain, user_gain)
+    )(core.reshape(1).astype(jnp.int32), keep, sums, got, hidden, item_emb, item_gain, user_gain)
     return (values, item_grad)
 
 

time: 111 us -> 109 us (0.982)
  waiting for transfers between devices: 30.8 us -> 28.2 us
  local copies, waits for them, and re-layouts: 2.67 us -> 1.35 us
  Pallas kernels: 8.71 us -> 9.96 us
    ppermute x1, waiting for transfers between devices: 2.66 us -> 0.13 us  [local(): got = lax.ppermute(send, 'core', swap)]
    unnamed x11 -> x9, local copies, waits for them, and re-layouts: 1.62 us -> 0.3 us
    pallas_call x1 -> x2, Pallas kernels: 6.74 us -> 7.99 us  [the longest x1 5.46 us: local(): pl.pallas_call(sent_kernel, out_shape=[jax.ShapeDtypeStruct((hist_rows, e...]
  transfers between devices with their start and end apart: 6 -> 6, of which waited for: 5 -> 5; matrix products, arithmetic and copies ran while one was open for 6% -> 6% of each run, Pallas kernels for 0% -> 2%
where the time goes in v6:
time: 109 us; the launch traced here: 108 us
  starting transfers between devices  35.5 us (33%)
  waiting for transfers between devices  28.2 us (26%)
  between operations  14.3 us (13%)
  blocking collectives  13.2 us (12%)
  Pallas kernels  9.96 us (9%)
  other arithmetic  3.61 us (3%)
  matrix products  2 us (2%)
  local copies, waits for them, and re-layouts  1.35 us (1%)
    all_to_all x1, waiting for transfers between devices, local(): lax.all_to_all(sent, 'dp', split_axis=0, concat_axis=0, tiled=True)  14.9 us
    all_to_all x1, starting transfers between devices, local(): lax.all_to_all(sent, 'dp', split_axis=0, concat_axis=0, tiled=True)  14.9 us
    all_gather x1, blocking collectives, local(): seed = lax.all_gather(value_weight, 'x', axis=0, tiled=True)  13.2 us
    all_to_all x1, waiting for transfers between devices, local(): lax.all_to_all(outgoing, 'dp', split_axis=0, concat_axis=0, tiled=True)  10.3 us
    ppermute x1, starting transfers between devices, local(): act_other = lax.ppermute(jnp.where(core == 0, high, low), 'core', swap)  7.15 us
    all_to_all x1, starting transfers between devices, local(): lax.all_to_all(outgoing, 'dp', split_axis=0, concat_axis=0, tiled=True)  6.13 us
    pallas_call x1, Pallas kernels, local(): pl.pallas_call(sent_kernel, out_shape=[jax.ShapeDtypeStruct((hist_rows, e...  5.46 us
    ppermute x1, starting transfers between devices, local(): grads_other = lax.ppermute(grads, 'core', swap)  4.77 us
  transfers between devices with their start and end apart: 6, of which 5 were waited for; matrix products, arithmetic and copies ran while one was open for 6% of the time, Pallas kernels for 2%

profile of v6, /device:TPU:1, one launch (start us, length us, event | category | flops | bytes accessed | tf_op | source)
XLA Modules:
  0.0 108.2 jit_solution(15582663366474115566)
XLA Ops:
  7.2 13.2 %all_gather.6 = bf16[128,2048]{1,0:T(8,128)(2,1)} all-gather(bf16[32,2048]{1,0:T(8,128)(2,1)} %param.12), channel_id=1, replica_groups=mesh['dp'=12,'x'=4,'y'=8,'core'=2] {'x'}, dimensions={0}, use_global_device_ids=true | all-gather | bytes 655360 | tf_op jit(solution)/shard_map/all_gather | solution.py:131
  20.4 0.7 reduce.2
  21.1 0.8 select_reduce_fusion.1
  22.0 0.1 fusion.12
  22.2 0.2 reduce_window_sum.11
  22.6 0.2 select_reduce_fusion
  22.8 0.4 fusion
  23.2 0.8 pad_maximum_fusion.1
  24.0 14.9 %all-to-all-start = ((bf16[12,8,2176]{2,1,0:T(8,128)(2,1)}), bf16[12,8,2176]{2,1,0:T(8,128)(2,1)S(1)}, u32[]{:S(2)}, u32[]{:S(2)}) async-start(bf16[12,8,2176]{2,1,0:T(8,128)(2,1)} %pad_maximum_fusion.1), calls=%async_computation | async-start | bytes 835584 | tf_op jit(solution)/shard_map/all_to_all | solution.py:150
  39.1 0.3 copy.24
  39.4 0.2 copy.26.hidden
  39.6 0.3 multiply_reduce_fusion
  39.9 0.1 multiply_convert_fusion.item_emb
  40.1 14.9 %all-to-all-done = bf16[12,8,2176]{2,1,0:T(8,128)(2,1)S(1)} async-done(((bf16[12,8,2176]{2,1,0:T(8,128)(2,1)}), bf16[12,8,2176]{2,1,0:T(8,128)(2,1)S(1)}, u32[]{:S(2)}, u32[]{:S(2)}) %all-to-all-start) | async-done | bytes 417824 | tf_op jit(solution)/shard_map/all_to_all | solution.py:150
  55.0 1.0 fusion.1
  56.0 6.1 %all-to-all-start.1 = ((bf16[12,8,2048]{2,1,0:T(8,128)(2,1)}), bf16[12,8,2048]{2,1,0:T(8,128)(2,1)S(1)}, u32[]{:S(2)}, u32[]{:S(2)}) async-start(bf16[12,8,2048]{2,1,0:T(8,128)(2,1)} %fusion.1), calls=%async_computation.1 | async-start | bytes 786432 | tf_op jit(solution)/shard_map/all_to_all | solution.py:159
  62.1 0.1 reshape_reshape.7
  62.3 0.3 reduce-precision_convert_fusion
  62.6 4.8 %collective-permute-start.1 = (bf16[128,2048]{1,0:T(8,128)(2,1)S(1)}, bf16[128,2048]{1,0:T(8,128)(2,1)S(1)}, u32[]{:S(2)}, u32[]{:S(2)}) collective-permute-start(bf16[128,2048]{1,0:T(8,128)(2,1)S(1)} %pad_maximum_fusion.grads), channel_id=1, source_target_pairs={{0,1},{1,0},{2,3},{3,2},{4,5},{5,4},{6,7},{7,6},{8,9},{9,8},{10,11... | collective-permute-start | bytes 1572872 | tf_op jit(solution)/shard_map/ppermute | solution.py:165
  67.4 10.3 %all-to-all-done.1 = bf16[12,8,2048]{2,1,0:T(8,128)(2,1)S(1)} async-done(((bf16[12,8,2048]{2,1,0:T(8,128)(2,1)}), bf16[12,8,2048]{2,1,0:T(8,128)(2,1)S(1)}, u32[]{:S(2)}, u32[]{:S(2)}) %all-to-all-start.1) | async-done | bytes 393248 | tf_op jit(solution)/shard_map/all_to_all | solution.py:159
  77.7 0.2 fusion.5
  78.0 0.4 convolution_convert_fusion
  78.4 7.2 %collective-permute-start = (bf16[128,1024]{1,0:T(8,128)(2,1)S(1)}, bf16[128,1024]{1,0:T(8,128)(2,1)S(1)}, u32[]{:S(2)}, u32[]{:S(2)}) collective-permute-start(bf16[128,1024]{1,0:T(8,128)(2,1)S(1)} %get-tuple-element.12), channel_id=1, source_target_pairs={{0,1},{1,0},{2,3},{3,2},{4,5},{5,4},{6,7},{7,6},{8,9},{9,8},{10,11... | collective-permute-start | bytes 786440 | tf_op jit(solution)/shard_map/ppermute | solution.py:170
  85.6 1.1 %collective-permute-done.act_other = bf16[128,1024]{1,0:T(8,128)(2,1)S(1)} collective-permute-done((bf16[128,1024]{1,0:T(8,128)(2,1)S(1)}, bf16[128,1024]{1,0:T(8,128)(2,1)S(1)}, u32[]{:S(2)}, u32[]{:S(2)}) %collective-permute-start) | collective-permute-done | bytes 262176 | tf_op jit(solution)/shard_map/ppermute | solution.py:170
  86.7 1.7 %all-gather.2.cloned.1.call-done.weight = bf16[1024,2048]{1,0:T(8,128)(2,1)} async-done(((bf16[128,2048]{1,0:T(8,128)(2,1)}), bf16[1024,2048]{1,0:T(8,128)(2,1)}) %all-gather.2.cloned.1.call-update) | async-done | bytes 4194320 | tf_op jit(solution)/shard_map/all_gather | solution.py:133
  88.4 5.5 %shard_map.87 = (f32[128,512]{1,0:T(8,128)S(1)}, f32[128,2560]{1,0:T(8,128)}) custom-call(bf16[128,1024]{1,0:T(8,128)(2,1)S(1)} %collective-permute-done.act_other, bf16[128,2048]{1,0:T(8,128)(2,1)S(1)} %pad_maximum_fusion.grads, bf16[128,2048]{1,0:T(8,128)(2,1)S(1)} %collective-permute-done.1.grads_other, bf16[1024,2048]{1,0:T(8,128)(2,1)} %all-gather.2.cloned.1.call-done.weight), custom_call_target="tpu_custom_call" | custom-call | flops 1610612736 | bytes 6291456 | tf_op jit(solution)/shard_map/pallas_call | solution.py:177
  93.9 2.6 %collective-permute-start.2 = (f32[128,2560]{1,0:T(8,128)}, f32[128,2560]{1,0:T(8,128)S(1)}, u32[]{:S(2)}, u32[]{:S(2)}) collective-permute-start(f32[128,2560]{1,0:T(8,128)} %get-tuple-element.9), channel_id=1, source_target_pairs={{0,1},{1,0},{2,3},{3,2},{4,5},{5,4},{6,7},{7,6},{8,9},{9,8},{10,11... | collective-permute-start | bytes 3932168 | tf_op jit(solution)/shard_map/ppermute | solution.py:194
  96.5 0.1 reshape.103.item_gain
  96.6 0.1 reshape.104.user_gain
  96.7 2.5 %shard_map.86.keep = f32[128,2048]{1,0:T(8,128)S(1)} custom-call(bf16[128,1024]{1,0:T(8,128)(2,1)S(1)} %get-tuple-element.13.act, bf16[1024,2048]{1,0:T(8,128)(2,1)} %all-gather.2.cloned.1.call-done.weight), custom_call_target="tpu_custom_call" | custom-call | flops 536870912 | bytes 5242880 | tf_op jit(solution)/shard_map/pallas_call | solution.py:195
  99.2 0.1 collective-permute-done.2.got
  99.3 2.0 %shard_map.88 = (bf16[128,2048]{1,0:T(8,128)(2,1)}, f32[64,2048]{1,0:T(8,128)}) custom-call(s32[1]{0:T(128)} %bitcast.core, f32[128,2048]{1,0:T(8,128)S(1)} %shard_map.86.keep, f32[128,512]{1,0:T(8,128)S(1)} %get-tuple-element.8.sums, f32[128,2560]{1,0:T(8,128)S(1)} %collective-permute-done.2.got, bf16[64,2048]{1,0:T(8,128)(2,1)S(1)} %copy.26.hidden, ...), custom_call_target="tpu_custom_call" | custom-call | tf_op jit(solution)/shard_map/pallas_call | solution.py:204
  (29 shorter events, 0.8 us)
Async XLA Ops:
  7.2 15.6 %copy-start = (bf16[128,2048]{1,0:T(8,128)(2,1)S(1)}, bf16[128,2048]{1,0:T(8,128)(2,1)}, u32[]{:S(2)}) copy-start(bf16[128,2048]{1,0:T(8,128)(2,1)} %param.13) | copy-start | bytes 1572868
  7.2 81.2 %all-gather.2.cloned.1.call-start = ((), (), s32[]{:S(2)}) async-start(), calls=%async_computation.2 | async-start | bytes 4718592 | tf_op jit(solution)/shard_map/all_gather | solution.py:133
  22.5 16.3 %copy-start.2 = (f32[2048]{0:T(1024)S(1)}, f32[2048]{0:T(1024)}, u32[]{:S(2)}) copy-start(f32[2048]{0:T(1024)} %param.8) | copy-start | bytes 24580
  22.8 16.3 %copy-start.1 = (bf16[64,2048]{1,0:T(8,128)(2,1)S(1)}, bf16[64,2048]{1,0:T(8,128)(2,1)}, u32[]{:S(2)}) copy-start(bf16[64,2048]{1,0:T(8,128)(2,1)} %param.7) | copy-start | bytes 786436
  24.0 31.0 %all-to-all-start = ((bf16[12,8,2176]{2,1,0:T(8,128)(2,1)}), bf16[12,8,2176]{2,1,0:T(8,128)(2,1)S(1)}, u32[]{:S(2)}, u32[]{:S(2)}) async-start(bf16[12,8,2176]{2,1,0:T(8,128)(2,1)} %pad_maximum_fusion.1), calls=%async_computation | async-start | bytes 835584 | tf_op jit(solution)/shard_map/all_to_all | solution.py:150
  39.6 22.5 %copy-start.3 = (f32[2048]{0:T(1024)S(1)}, f32[2048]{0:T(1024)}, u32[]{:S(2)}) copy-start(f32[2048]{0:T(1024)} %param.11) | copy-start | bytes 24580
  56.0 21.8 %all-to-all-start.1 = ((bf16[12,8,2048]{2,1,0:T(8,128)(2,1)}), bf16[12,8,2048]{2,1,0:T(8,128)(2,1)S(1)}, u32[]{:S(2)}, u32[]{:S(2)}) async-start(bf16[12,8,2048]{2,1,0:T(8,128)(2,1)} %fusion.1), calls=%async_computation.1 | async-start | bytes 786432 | tf_op jit(solution)/shard_map/all_to_all | solution.py:159
  62.6 23.0 %collective-permute-start.1 = (bf16[128,2048]{1,0:T(8,128)(2,1)S(1)}, bf16[128,2048]{1,0:T(8,128)(2,1)S(1)}, u32[]{:S(2)}, u32[]{:S(2)}) collective-permute-start(bf16[128,2048]{1,0:T(8,128)(2,1)S(1)} %pad_maximum_fusion.grads), channel_id=1, source_target_pairs={{0,1},{1,0},{2,3},{3,2},{4,5},{5,4},{6,7},{7,6},{8,9},{9,8},{10,11... | collective-permute-start | bytes 1572872 | tf_op jit(solution)/shard_map/ppermute | solution.py:165
  78.4 8.3 %collective-permute-start = (bf16[128,1024]{1,0:T(8,128)(2,1)S(1)}, bf16[128,1024]{1,0:T(8,128)(2,1)S(1)}, u32[]{:S(2)}, u32[]{:S(2)}) collective-permute-start(bf16[128,1024]{1,0:T(8,128)(2,1)S(1)} %get-tuple-element.12), channel_id=1, source_target_pairs={{0,1},{1,0},{2,3},{3,2},{4,5},{5,4},{6,7},{7,6},{8,9},{9,8},{10,11... | collective-permute-start | bytes 786440 | tf_op jit(solution)/shard_map/ppermute | solution.py:170
  93.9 5.4 %collective-permute-start.2 = (f32[128,2560]{1,0:T(8,128)}, f32[128,2560]{1,0:T(8,128)S(1)}, u32[]{:S(2)}, u32[]{:S(2)}) collective-permute-start(f32[128,2560]{1,0:T(8,128)} %get-tuple-element.9), channel_id=1, source_target_pairs={{0,1},{1,0},{2,3},{3,2},{4,5},{5,4},{6,7},{7,6},{8,9},{9,8},{10,11... | collective-permute-start | bytes 3932168 | tf_op jit(solution)/shard_map/ppermute | solution.py:194
Sparse Core Ops, SparseCore 0:
  20.6 67.8 all-gather.1

commit v7 on v5

--- a/solution.py
+++ b/solution.py
@@ -41,47 +41,99 @@
     return a.reshape(a.shape[0], -1)
 
 
-def products_kernel(act, act_other, grads, grads_other, weight, keep, send, held, sems):
-    parts = sems.shape[0]
-    block = held.shape[0] // parts
-    cuts = [slice(i * block, (i + 1) * block) for i in range(parts)]
-    copies = [
-        pltpu.make_async_copy(weight.at[cut], held.at[cut], sems.at[i])
-        for i, cut in enumerate(cuts)
-    ]
-    for copy in copies:
-        copy.start()
-    rows, half = act.shape
-    width = held.shape[1]
+def lanes(place, width):
+    return pl.ds(pl.multiple_of(place * width, width), width)
+
+
+def pick_lanes(act, places, width):
+    return jnp.concatenate([act[:, lanes(p, width)] for p in places], axis=1)
+
+
+def back_products(grads, grads_other, blocks, places, up, up_other):
     items = grads.shape[0] // 2
     both = jnp.concatenate([grads[...], grads_other[...]], axis=0)
-    for i, (copy, cut) in enumerate(zip(copies, cuts)):
-        copy.wait()
-        back = dot(both, held[cut], 1, 1)
-        row, column = divmod(i * block, half // 2)
-        row = row * items
-        at = slice(width + column, width + column + block)
-        keep[row : row + items, at] = back[:items] + back[items : 2 * items]
-        send[row : row + items, at] = back[2 * items : 3 * items] + back[3 * items :]
-    both = jnp.concatenate([act[...], act_other[...]], axis=0)
-    for i in range(parts):
-        at = slice(i * width // parts, (i + 1) * width // parts)
-        forward = dot(both, held[:, at])
-        keep[:, at] = forward[:rows]
-        send[:, at] = forward[rows:]
-
-
-def last_kernel(core, keep, got, hidden, item_emb, item_gain, user_gain, values, item_grad, up):
+    weight = jnp.concatenate([b[...] for b in blocks], axis=0)
+    back = dot(both, weight, 1, 1)
+    width = weight.shape[0] // len(places)
+    per_row = NY // 2
+    for i, place in enumerate(places):
+        part = back[:, i * width : (i + 1) * width]
+        rows = pl.ds(pl.multiple_of(lax.div(place, per_row) * items, items), items)
+        at = lanes(lax.rem(place, per_row), width)
+        up[rows, at] = part[:items] + part[items : 2 * items]
+        up_other[rows, at] = part[2 * items : 3 * items] + part[3 * items :]
+
+
+def early_kernel(y, act, act_other, grads, grads_other, *refs):
+    blocks, (acc, acc_other, up, up_other) = refs[:5], refs[5:]
+    places = [lax.rem(y[0] + step, NY) for step in (0, 1, NY - 1, 2, NY - 2)]
+    up[...] = jnp.zeros_like(up)
+    up_other[...] = jnp.zeros_like(up_other)
+    back_products(grads, grads_other, blocks, places, up, up_other)
+    rows, width = acc.shape
+    block = blocks[0].shape[0]
+    both = jnp.concatenate(
+        [pick_lanes(act, places, block), pick_lanes(act_other, places, block)], axis=0
+    )
+    for lo in range(0, width, 512):
+        at = slice(lo, lo + 512)
+        forward = dot(both, jnp.concatenate([b[:, at] for b in blocks], axis=0))
+        acc[:, at] = forward[:rows]
+        acc_other[:, at] = forward[rows:]
+
+
+def late_places(y):
+    return [lax.rem(y[0] + step, NY) for step in (3, NY - 3, 4)]
+
+
+def sent_kernel(y, act_other, grads, grads_other, acc_other, up_early, up_other_early, *refs):
+    blocks, (up, send, sums) = refs[:4], refs[4:]
+    places = late_places(y)
+    up[...] = up_early[...]
+    sums[...] = up_other_early[...]
+    back_products(grads, grads_other, blocks, places, up, sums)
+    rows, width = acc_other.shape
+    send[:, width:] = sums[...]
+    both = pick_lanes(act_other, places, blocks[0].shape[0])
+    for lo in range(0, width, 512):
+        at = slice(lo, lo + 512)
+        weight = jnp.concatenate([b[:, at] for b in blocks], axis=0)
+        send[:, at] = acc_other[:, at] + dot(both, weight)
+
+
+def kept_kernel(y, act, acc, *refs):
+    blocks, keep = refs[:4], refs[4]
+    both = pick_lanes(act, late_places(y), blocks[0].shape[0])
+    for lo in range(0, acc.shape[1], 512):
+        at = slice(lo, lo + 512)
+        weight = jnp.concatenate([b[:, at] for b in blocks], axis=0)
+        keep[:, at] = acc[:, at] + dot(both, weight)
+
+
+def on_chip(kernel, scalar, *args, out, scratch=(), flops=0):
+    vmem = pl.BlockSpec(memory_space=pltpu.VMEM)
+    return pl.pallas_call(
+        kernel,
+        out_shape=[jax.ShapeDtypeStruct(shape, kind) for shape, kind in out],
+        in_specs=[pl.BlockSpec(memory_space=pltpu.SMEM)] + [vmem] * len(args),
+        out_specs=[vmem] * len(out),
+        scratch_shapes=list(scratch),
+        cost_estimate=pl.CostEstimate(flops=flops, bytes_accessed=0, transcendentals=0),
+        compiler_params=pltpu.CompilerParams(vmem_limit_bytes=16 << 20),
+    )(scalar.reshape(1).astype(jnp.int32), *args)
+
+
+def last_kernel(core, keep, sums, got, hidden, item_emb, item_gain, user_gain, values, item_grad, up):
     width = values.shape[1]
     items = hidden.shape[0]
-    block = keep.shape[1] - width
+    block = sums.shape[1]
     part = width // (NX * NY * NCORE)
     tile = part * NX
-    values[...] = (keep[:, :width] + got[:, :width]).astype(jnp.bfloat16)
-    for side, ref in ((core[0], keep), (1 - core[0], got)):
+    values[...] = (keep[...] + got[:, :width]).astype(jnp.bfloat16)
+    for side, ref, skip in ((core[0], sums, 0), (1 - core[0], got, width)):
         for piece in range(2):
             at = pl.multiple_of((2 * side + piece) * block, block)
-            up[:, pl.ds(at, block)] = ref[piece * items : (piece + 1) * items, width:]
+            up[:, pl.ds(at, block)] = ref[piece * items : (piece + 1) * items, skip:]
     x = item_emb[...].astype(jnp.float32)
     scale = lax.rsqrt(jnp.mean(x * x, axis=1, keepdims=True) + eps)
     emb_grad = norm_back(x, user_gain[...], scale, up[...])
@@ -109,7 +161,8 @@
 
     seed = lax.all_gather(value_weight, "x", axis=0, tiled=True)
     history, seed = lax.optimization_barrier((history, seed))
-    weight = lax.all_gather(seed, "y", axis=0, tiled=True)
+    around = lambda a, step: lax.ppermute(a, "y", [((i + step) % NY, i) for i in range(NY)])
+    up_one, down_one = around(seed, 1), around(seed, -1)
 
     pool = owner_map.shape[1]
     stored = locate(owner_map, history)
@@ -127,6 +180,8 @@
     asked = jnp.pad(asked, ((0, 0), (0, 0), (0, -item_rows % 128)))
     sent = jnp.concatenate([grad_sums, asked], axis=2)
     arrived = lax.all_to_all(sent, "dp", split_axis=0, concat_axis=0, tiled=True)
+    up_two, down_two = around(up_one, 1), around(down_one, -1)
+    arrived, up_two, down_two = lax.optimization_barrier((arrived, up_two, down_two))
     arrived = arrived.reshape(groups * CAP, -1)
     select = arrived[:, width : width + item_rows]
 
@@ -136,6 +191,10 @@
     item_emb = item_emb.astype(bf16)
     outgoing = dot(select, item_emb).astype(bf16).reshape(groups, CAP, width)
     incoming = lax.all_to_all(outgoing, "dp", split_axis=0, concat_axis=0, tiled=True)
+    up_three, down_three = around(up_two, 1), around(down_two, -1)
+    incoming, up_three, down_three = lax.optimization_barrier((incoming, up_three, down_three))
+    rows = seed.shape[0] // 2
+    up_four, down_four = around(up_three[:rows], 1), around(down_three[rows:], -1)
 
     swap = [(0, 1), (1, 0)]
     total = dot(select, arrived[:, :width], 0, 0)
@@ -148,31 +207,26 @@
     act = jnp.where(core == 0, low, high)
     act_other = lax.ppermute(jnp.where(core == 0, high, low), "core", swap)
 
-    vmem = pl.BlockSpec(memory_space=pltpu.VMEM)
-    result = jax.ShapeDtypeStruct((hist_rows, width + half * item_rows // hist_rows), f32)
-    keep, send = pl.pallas_call(
-        products_kernel,
-        out_shape=[result, result],
-        in_specs=[vmem] * 4 + [pl.BlockSpec(memory_space=pltpu.HBM)],
-        out_specs=[vmem] * 2,
-        scratch_shapes=[pltpu.VMEM((half, width), bf16), pltpu.SemaphoreType.DMA((4,))],
-        cost_estimate=pl.CostEstimate(
-            flops=8 * hist_rows * half * width, bytes_accessed=10 << 20, transcendentals=0
-        ),
-        compiler_params=pltpu.CompilerParams(vmem_limit_bytes=52 << 20),
-    )(act, act_other, grads, grads_other, weight)
+    early = (seed, up_one, down_one, up_two, down_two)
+    late = (up_three, down_three, up_four, down_four)
+    y = lax.axis_index("y")
+    part = ((hist_rows, half * item_rows // hist_rows), f32)
+    full = ((hist_rows, width), f32)
+    acc, acc_other, sums, sums_other = on_chip(
+        early_kernel, y, act, act_other, grads, grads_other, *early, out=[full, full, part, part]
+    )
+    sums, send = on_chip(
+        sent_kernel, y, act_other, grads, grads_other, acc_other, sums, sums_other, *late,
+        out=[part, ((hist_rows, width + part[0][1]), f32)],
+        scratch=[pltpu.VMEM(*part)],
+    )
     got = lax.ppermute(send, "core", swap)
-    values, item_grad = pl.pallas_call(
-        last_kernel,
-        out_shape=[
-            jax.ShapeDtypeStruct((hist_rows, width), bf16),
-            jax.ShapeDtypeStruct((item_rows, width), f32),
-        ],
-        in_specs=[pl.BlockSpec(memory_space=pltpu.SMEM)] + [vmem] * 6,
-        out_specs=[vmem] * 2,
-        scratch_shapes=[pltpu.VMEM((item_rows, width), f32)],
-        compiler_params=pltpu.CompilerParams(vmem_limit_bytes=12 << 20),
-    )(core.reshape(1).astype(jnp.int32), keep, got, hidden, item_emb, item_gain, user_gain)
+    (keep,) = on_chip(kept_kernel, y, act, acc, *late, out=[full])
+    values, item_grad = on_chip(
+        last_kernel, core, keep, sums, got, hidden, item_emb, item_gain, user_gain,
+        out=[((hist_rows, width), bf16), ((item_rows, width), f32)],
+        scratch=[pltpu.VMEM((item_rows, width), f32)],
+    )
     return (values, item_grad)
 
 

time: 111 us -> 123 us (1.11)
  starting transfers between devices: 35.5 us -> 68.5 us
  waiting for transfers between devices: 30.8 us -> 11.7 us
  between operations: 14.3 us -> 1.1 us
  local copies, waits for them, and re-layouts: 2.67 us -> 8.93 us
  Pallas kernels: 8.71 us -> 11.4 us
  matrix products: 2.01 us -> 4.42 us
  blocking collectives: 13.2 us -> 11.4 us
    ppermute x0 -> x8, starting transfers between devices: none -> 25.3 us  [local(): lax.ppermute(a, 'y', [((i + step) % NY, i) for i in range(NY)])]
    all_to_all x1, waiting for transfers between devices: 14.9 us -> 0.01 us  [local(): lax.all_to_all(sent, 'dp', split_axis=0, concat_axis=0, tiled=True)]
    ppermute x0 -> x8, waiting for transfers between devices: none -> 11.7 us  [local(): lax.ppermute(a, 'y', [((i + step) % NY, i) for i in range(NY)])]
    all_to_all x1, waiting for transfers between devices: 10.3 us -> 0.01 us  [local(): lax.all_to_all(outgoing, 'dp', split_axis=0, concat_axis=0, tiled=True)]
    unnamed x11 -> x35, local copies, waits for them, and re-layouts: 1.62 us -> 5.88 us
    pallas_call x2 -> x4, Pallas kernels: 8.71 us -> 11.4 us  [on_chip(): pl.pallas_call(kernel, out_shape=[jax.ShapeDtypeStruct(shape, kind) for s...]
    ppermute x1, waiting for transfers between devices: 2.66 us -> 0.02 us  [local(): got = lax.ppermute(send, 'core', swap)]
    ppermute x1, starting transfers between devices: 4.77 us -> 7.4 us  [local(): grads_other = lax.ppermute(grads, 'core', swap)]
  transfers between devices with their start and end apart: 6 -> 13, of which waited for: 5 -> 3; matrix products, arithmetic and copies ran while one was open for 6% -> 8% of each run, Pallas kernels for 0% -> 4%
where the time goes in v7:
time: 123 us; the launch traced here: 122 us
  starting transfers between devices  68.5 us (56%)
  waiting for transfers between devices  11.7 us (10%)
  blocking collectives  11.4 us (9%)
  Pallas kernels  11.4 us (9%)
  local copies, waits for them, and re-layouts  8.93 us (7%)
  matrix products  4.42 us (4%)
  other arithmetic  4.3 us (3%)
    ppermute x8, starting transfers between devices, local(): lax.ppermute(a, 'y', [((i + step) % NY, i) for i in range(NY)])  25.3 us
    all_to_all x1, starting transfers between devices, local(): lax.all_to_all(sent, 'dp', split_axis=0, concat_axis=0, tiled=True)  14.9 us
    ppermute x8, waiting for transfers between devices, local(): lax.ppermute(a, 'y', [((i + step) % NY, i) for i in range(NY)])  11.7 us
    all_gather x1, blocking collectives, local(): seed = lax.all_gather(value_weight, 'x', axis=0, tiled=True)  11.4 us
    pallas_call x4, Pallas kernels, on_chip(): pl.pallas_call(kernel, out_shape=[jax.ShapeDtypeStruct(shape, kind) for s...  11.4 us
    ppermute x1, starting transfers between devices, local(): act_other = lax.ppermute(jnp.where(core == 0, high, low), 'core', swap)  9.46 us
    all_to_all x1, starting transfers between devices, local(): lax.all_to_all(outgoing, 'dp', split_axis=0, concat_axis=0, tiled=True)  8.74 us
    ppermute x1, starting transfers between devices, local(): grads_other = lax.ppermute(grads, 'core', swap)  7.4 us
  transfers between devices with their start and end apart: 13, of which 3 were waited for; matrix products, arithmetic and copies ran while one was open for 8% of the time, Pallas kernels for 4%

profile of v7, /device:TPU:1, one launch (start us, length us, event | category | flops | bytes accessed | tf_op | source)
XLA Modules:
  0.0 121.7 jit_solution(17476766466258025616)
XLA Ops:
  0.6 11.4 %all_gather.3.refs_0_ = bf16[128,2048]{1,0:T(8,128)(2,1)S(1)} all-gather(bf16[32,2048]{1,0:T(8,128)(2,1)} %param.12), channel_id=1, replica_groups=mesh['dp'=12,'x'=4,'y'=8,'core'=2] {'x'}, dimensions={0}, use_global_device_ids=true | all-gather | bytes 655360 | tf_op jit(solution)/shard_map/all_gather | solution.py:162
  12.1 6.3 %collective-permute-start = (bf16[128,2048]{1,0:T(8,128)(2,1)S(1)}, bf16[128,2048]{1,0:T(8,128)(2,1)S(1)}, u32[]{:S(2)}, u32[]{:S(2)}) collective-permute-start(bf16[128,2048]{1,0:T(8,128)(2,1)S(1)} %all_gather.3.refs_0_), channel_id=1, source_target_pairs={{2,0},{4,2},{6,4},{8,6},{10,8},{12,10},{14,12},{0,14},{3,1},{5,3},... | collective-permute-start | bytes 1572872 | tf_op jit(solution)/shard_map/ppermute | solution.py:164
  18.4 1.9 %collective-permute-start.2 = (bf16[128,2048]{1,0:T(8,128)(2,1)S(1)}, bf16[128,2048]{1,0:T(8,128)(2,1)S(1)}, u32[]{:S(2)}, u32[]{:S(2)}) collective-permute-start(bf16[128,2048]{1,0:T(8,128)(2,1)S(1)} %all_gather.3.refs_0_), channel_id=1, source_target_pairs={{14,0},{0,2},{2,4},{4,6},{6,8},{8,10},{10,12},{12,14},{15,1},{1,3}... | collective-permute-start | bytes 1572872 | tf_op jit(solution)/shard_map/ppermute | solution.py:164
  21.0 0.8 select_reduce_fusion.1
  23.1 0.8 pad_maximum_fusion.1
  23.9 14.9 %all-to-all-start = ((bf16[12,8,2176]{2,1,0:T(8,128)(2,1)}), bf16[12,8,2176]{2,1,0:T(8,128)(2,1)}, u32[]{:S(2)}, u32[]{:S(2)}) async-start(bf16[12,8,2176]{2,1,0:T(8,128)(2,1)} %pad_maximum_fusion.1), calls=%async_computation | async-start | bytes 835584 | tf_op jit(solution)/shard_map/all_to_all | solution.py:182
  39.4 4.6 %collective-permute-start.1 = (bf16[128,2048]{1,0:T(8,128)(2,1)S(1)}, bf16[128,2048]{1,0:T(8,128)(2,1)}, u32[]{:S(2)}, u32[]{:S(2)}) collective-permute-start(bf16[128,2048]{1,0:T(8,128)(2,1)S(1)} %collective-permute-done.refs_1_), channel_id=1, source_target_pairs={{2,0},{4,2},{6,4},{8,6},{10,8},{12,10},{14,12},{0,14},{3,1},{5,3},... | collective-permute-start | bytes 1572872 | tf_op jit(solution)/shard_map/ppermute | solution.py:164
  44.0 1.9 %collective-permute-start.3 = (bf16[128,2048]{1,0:T(8,128)(2,1)S(1)}, bf16[128,2048]{1,0:T(8,128)(2,1)}, u32[]{:S(2)}, u32[]{:S(2)}) collective-permute-start(bf16[128,2048]{1,0:T(8,128)(2,1)S(1)} %collective-permute-done.2.refs_2_), channel_id=1, source_target_pairs={{14,0},{0,2},{2,4},{4,6},{6,8},{8,10},{10,12},{12,14},{15,1},{1,3}... | collective-permute-start | bytes 1572872 | tf_op jit(solution)/shard_map/ppermute | solution.py:164
  47.1 4.9 %collective-permute-done.1.refs_3_ = bf16[128,2048]{1,0:T(8,128)(2,1)} collective-permute-done((bf16[128,2048]{1,0:T(8,128)(2,1)S(1)}, bf16[128,2048]{1,0:T(8,128)(2,1)}, u32[]{:S(2)}, u32[]{:S(2)}) %collective-permute-start.1) | collective-permute-done | bytes 524320 | tf_op jit(solution)/shard_map/ppermute | solution.py:164
  52.0 5.2 %collective-permute-done.3.refs_4_ = bf16[128,2048]{1,0:T(8,128)(2,1)} collective-permute-done((bf16[128,2048]{1,0:T(8,128)(2,1)S(1)}, bf16[128,2048]{1,0:T(8,128)(2,1)}, u32[]{:S(2)}, u32[]{:S(2)}) %collective-permute-start.3) | collective-permute-done | bytes 524320 | tf_op jit(solution)/shard_map/ppermute | solution.py:164
  57.2 1.7 %fusion.1 = bf16[12,8,2048]{2,1,0:T(8,128)(2,1)} fusion(bf16[64,2048]{1,0:T(8,128)(2,1)S(1)} %multiply_convert_fusion.item_emb, bf16[96,2176]{1,0:T(8,128)(2,1)} %bitcast.3), kind=kOutput, calls=%fused_computation.4 | convolution fusion | flops 25362432 | bytes 679936 | tf_op jit(solution)/shard_map/dot_general | solution.py:35
  58.9 8.7 %all-to-all-start.1 = ((bf16[12,8,2048]{2,1,0:T(8,128)(2,1)}), bf16[12,8,2048]{2,1,0:T(8,128)(2,1)S(1)}, u32[]{:S(2)}, u32[]{:S(2)}) async-start(bf16[12,8,2048]{2,1,0:T(8,128)(2,1)} %fusion.1), calls=%async_computation.1 | async-start | bytes 786432 | tf_op jit(solution)/shard_map/all_to_all | solution.py:193
  67.7 1.9 %collective-permute-start.4 = (bf16[128,2048]{1,0:T(8,128)(2,1)}, bf16[128,2048]{1,0:T(8,128)(2,1)S(1)}, u32[]{:S(2)}, u32[]{:S(2)}) collective-permute-start(bf16[128,2048]{1,0:T(8,128)(2,1)} %collective-permute-done.1.refs_3_), channel_id=1, source_target_pairs={{2,0},{4,2},{6,4},{8,6},{10,8},{12,10},{14,12},{0,14},{3,1},{5,3},... | collective-permute-start | bytes 1572872 | tf_op jit(solution)/shard_map/ppermute | solution.py:164
  69.6 3.4 %collective-permute-start.5 = (bf16[128,2048]{1,0:T(8,128)(2,1)}, bf16[128,2048]{1,0:T(8,128)(2,1)S(1)}, u32[]{:S(2)}, u32[]{:S(2)}) collective-permute-start(bf16[128,2048]{1,0:T(8,128)(2,1)} %collective-permute-done.3.refs_4_), channel_id=1, source_target_pairs={{14,0},{0,2},{2,4},{4,6},{6,8},{8,10},{10,12},{12,14},{15,1},{1,3}... | collective-permute-start | bytes 1572872 | tf_op jit(solution)/shard_map/ppermute | solution.py:164
  73.2 1.3 %reduce-precision_convert_fusion = (bf16[64,2048]{1,0:T(8,128)(2,1)S(1)}, bf16[64,2048]{1,0:T(8,128)(2,1)S(1)}) fusion(bf16[96,2176]{1,0:T(8,128)(2,1)} %bitcast.3), kind=kOutput, calls=%fused_computation.13 | convolution fusion | flops 25690112 | bytes 942080 | tf_op jit(solution)/shard_map/dot_general | solution.py:35
  74.5 7.4 %collective-permute-start.7 = (bf16[128,2048]{1,0:T(8,128)(2,1)S(1)}, bf16[128,2048]{1,0:T(8,128)(2,1)}, u32[]{:S(2)}, u32[]{:S(2)}) collective-permute-start(bf16[128,2048]{1,0:T(8,128)(2,1)S(1)} %pad_maximum_fusion.grads), channel_id=1, source_target_pairs={{0,1},{1,0},{2,3},{3,2},{4,5},{5,4},{6,7},{7,6},{8,9},{9,8},{10,11... | collective-permute-start | bytes 1572872 | tf_op jit(solution)/shard_map/ppermute | solution.py:203
  82.8 1.0 convolution_convert_fusion
  83.8 0.7 broadcast_select_fusion
  84.6 9.5 %collective-permute-start.6 = (bf16[128,1024]{1,0:T(8,128)(2,1)}, bf16[128,1024]{1,0:T(8,128)(2,1)}, u32[]{:S(2)}, u32[]{:S(2)}) collective-permute-start(bf16[128,1024]{1,0:T(8,128)(2,1)} %get-tuple-element.32), channel_id=1, source_target_pairs={{0,1},{1,0},{2,3},{3,2},{4,5},{5,4},{6,7},{7,6},{8,9},{9,8},{10,11... | collective-permute-start | bytes 786440 | tf_op jit(solution)/shard_map/ppermute | solution.py:208
  94.0 0.7 slice.22
  94.8 1.9 %collective-permute-start.8 = (bf16[64,2048]{1,0:T(8,128)(2,1)}, bf16[64,2048]{1,0:T(8,128)(2,1)}, u32[]{:S(2)}, u32[]{:S(2)}) collective-permute-start(bf16[64,2048]{1,0:T(8,128)(2,1)} %slice.22), channel_id=1, source_target_pairs={{2,0},{4,2},{6,4},{8,6},{10,8},{12,10},{14,12},{0,14},{3,1},{5,3},... | collective-permute-start | bytes 786440 | tf_op jit(solution)/shard_map/ppermute | solution.py:164
  97.4 3.4 %collective-permute-start.9 = (bf16[64,2048]{1,0:T(8,128)(2,1)}, bf16[64,2048]{1,0:T(8,128)(2,1)}, u32[]{:S(2)}, u32[]{:S(2)}) collective-permute-start(bf16[64,2048]{1,0:T(8,128)(2,1)} %slice.23), channel_id=1, source_target_pairs={{14,0},{0,2},{2,4},{4,6},{6,8},{8,10},{10,12},{12,14},{15,1},{1,3}... | collective-permute-start | bytes 786440 | tf_op jit(solution)/shard_map/ppermute | solution.py:164
  100.8 1.0 copy-done.4
  101.8 1.0 copy-done.6
  102.9 3.3 %shard_map.86 = (f32[128,2048]{1,0:T(8,128)S(1)}, f32[128,2048]{1,0:T(8,128)S(1)}, f32[128,512]{1,0:T(8,128)S(1)}, f32[128,512]{1,0:T(8,128)S(1)}) custom-call(s32[1]{0:T(128)} %bitcast.1.y, bf16[128,1024]{1,0:T(8,128)(2,1)S(1)} %get-tuple-element.33.act, bf16[128,1024]{1,0:T(8,128)(2,1)} %collective-permute-done.6.act_other, ...), custom_call_target="tpu_custom_call" | custom-call | tf_op jit(solution)/shard_map/pallas_call | solution.py:115
  106.2 1.0 copy-done.1
  107.1 1.6 %collective-permute-done.9.refs_3_ = bf16[64,2048]{1,0:T(8,128)(2,1)} collective-permute-done((bf16[64,2048]{1,0:T(8,128)(2,1)}, bf16[64,2048]{1,0:T(8,128)(2,1)}, u32[]{:S(2)}, u32[]{:S(2)}) %collective-permute-start.9) | collective-permute-done | bytes 262176 | tf_op jit(solution)/shard_map/ppermute | solution.py:164
  108.8 3.4 %shard_map.88 = (f32[128,512]{1,0:T(8,128)S(1)}, f32[128,2560]{1,0:T(8,128)}) custom-call(s32[1]{0:T(128)} %bitcast.1.y, bf16[128,1024]{1,0:T(8,128)(2,1)} %collective-permute-done.6.act_other, bf16[128,2048]{1,0:T(8,128)(2,1)S(1)} %pad_maximum_fusion.grads, bf16[128,2048]{1,0:T(8,128)(2,1)} %collective-permute-done.7.grads_other, ...), custom_call_target="tpu_custom_call" | custom-call | tf_op jit(solution)/shard_map/pallas_call | solution.py:115
  112.8 2.7 %collective-permute-start.10 = (f32[128,2560]{1,0:T(8,128)}, f32[128,2560]{1,0:T(8,128)}, u32[]{:S(2)}, u32[]{:S(2)}) collective-permute-start(f32[128,2560]{1,0:T(8,128)} %get-tuple-element.29), channel_id=1, source_target_pairs={{0,1},{1,0},{2,3},{3,2},{4,5},{5,4},{6,7},{7,6},{8,9},{9,8},{10,11... | collective-permute-start | bytes 3932168 | tf_op jit(solution)/shard_map/ppermute | solution.py:223
  115.7 1.2 %copy-done.2 = f32[128,2048]{1,0:T(8,128)S(1)} copy-done((f32[128,2048]{1,0:T(8,128)S(1)}, f32[128,2048]{1,0:T(8,128)}, u32[]{:S(2)}) %copy-start.2) | copy-done | bytes 1048600
  116.9 1.5 %shard_map.87.keep = f32[128,2048]{1,0:T(8,128)S(1)} custom-call(s32[1]{0:T(128)} %bitcast.1.y, bf16[128,1024]{1,0:T(8,128)(2,1)S(1)} %get-tuple-element.33.act, f32[128,2048]{1,0:T(8,128)S(1)} %copy-done.2, bf16[128,2048]{1,0:T(8,128)(2,1)S(1)} %collective-permute-done.4.refs_0_, bf16[128,2048]{1,0:T(8,128)(2,1)S(1)} %collective-permute-done.5.refs_1_, ...), custom_call_target="tpu_custom_call" | custom-call | tf_op jit(solution)/shard_map/pallas_call | solution.py:115
  118.5 3.2 %shard_map.89 = (bf16[128,2048]{1,0:T(8,128)(2,1)}, f32[64,2048]{1,0:T(8,128)}) custom-call(s32[1]{0:T(128)} %bitcast.core, f32[128,2048]{1,0:T(8,128)S(1)} %shard_map.87.keep, f32[128,512]{1,0:T(8,128)S(1)} %copy-done.8, f32[128,2560]{1,0:T(8,128)} %collective-permute-done.10.got, bf16[64,2048]{1,0:T(8,128)(2,1)S(1)} %copy.26.hidden, ...), custom_call_target="tpu_custom_call" | custom-call | tf_op jit(solution)/shard_map/pallas_call | solution.py:115
  (71 shorter events, 6.3 us)
Async XLA Ops:
  0.6 22.1 %copy-start = (bf16[128,2048]{1,0:T(8,128)(2,1)S(1)}, bf16[128,2048]{1,0:T(8,128)(2,1)}, u32[]{:S(2)}) copy-start(bf16[128,2048]{1,0:T(8,128)(2,1)} %param.13) | copy-start | bytes 1572868
  12.1 27.3 %collective-permute-start = (bf16[128,2048]{1,0:T(8,128)(2,1)S(1)}, bf16[128,2048]{1,0:T(8,128)(2,1)S(1)}, u32[]{:S(2)}, u32[]{:S(2)}) collective-permute-start(bf16[128,2048]{1,0:T(8,128)(2,1)S(1)} %all_gather.3.refs_0_), channel_id=1, source_target_pairs={{2,0},{4,2},{6,4},{8,6},{10,8},{12,10},{14,12},{0,14},{3,1},{5,3},... | collective-permute-start | bytes 1572872 | tf_op jit(solution)/shard_map/ppermute | solution.py:164
  18.4 25.6 %collective-permute-start.2 = (bf16[128,2048]{1,0:T(8,128)(2,1)S(1)}, bf16[128,2048]{1,0:T(8,128)(2,1)S(1)}, u32[]{:S(2)}, u32[]{:S(2)}) collective-permute-start(bf16[128,2048]{1,0:T(8,128)(2,1)S(1)} %all_gather.3.refs_0_), channel_id=1, source_target_pairs={{14,0},{0,2},{2,4},{4,6},{6,8},{8,10},{10,12},{12,14},{15,1},{1,3}... | collective-permute-start | bytes 1572872 | tf_op jit(solution)/shard_map/ppermute | solution.py:164
  22.7 1.2 %copy-start.16 = (s32[128]{0:T(128)}, s32[128]{0:T(128)S(1)}, u32[]{:S(2)}) copy-start(s32[128]{0:T(128)S(1)} %multiply_add_fusion) | copy-start | bytes 1540
  22.7 16.1 %copy-start.13 = (bf16[64,2048]{1,0:T(8,128)(2,1)S(1)}, bf16[64,2048]{1,0:T(8,128)(2,1)}, u32[]{:S(2)}) copy-start(bf16[64,2048]{1,0:T(8,128)(2,1)} %param.7) | copy-start | bytes 786436
  23.9 33.3 %all-to-all-start = ((bf16[12,8,2176]{2,1,0:T(8,128)(2,1)}), bf16[12,8,2176]{2,1,0:T(8,128)(2,1)}, u32[]{:S(2)}, u32[]{:S(2)}) async-start(bf16[12,8,2176]{2,1,0:T(8,128)(2,1)} %pad_maximum_fusion.1), calls=%async_computation | async-start | bytes 835584 | tf_op jit(solution)/shard_map/all_to_all | solution.py:182
  39.1 7.1 %copy-start.14 = (f32[2048]{0:T(1024)S(1)}, f32[2048]{0:T(1024)}, u32[]{:S(2)}) copy-start(f32[2048]{0:T(1024)} %param.8) | copy-start | bytes 24580
  39.4 19.6 %copy-start.3 = (bf16[128,2048]{1,0:T(8,128)(2,1)}, bf16[128,2048]{1,0:T(8,128)(2,1)S(1)}, u32[]{:S(2)}) copy-start(bf16[128,2048]{1,0:T(8,128)(2,1)S(1)} %collective-permute-done.refs_1_) | copy-start | bytes 1572868
  39.4 12.6 %collective-permute-start.1 = (bf16[128,2048]{1,0:T(8,128)(2,1)S(1)}, bf16[128,2048]{1,0:T(8,128)(2,1)}, u32[]{:S(2)}, u32[]{:S(2)}) collective-permute-start(bf16[128,2048]{1,0:T(8,128)(2,1)S(1)} %collective-permute-done.refs_1_), channel_id=1, source_target_pairs={{2,0},{4,2},{6,4},{8,6},{10,8},{12,10},{14,12},{0,14},{3,1},{5,3},... | collective-permute-start | bytes 1572872 | tf_op jit(solution)/shard_map/ppermute | solution.py:164
  44.0 15.0 %copy-start.5 = (bf16[128,2048]{1,0:T(8,128)(2,1)}, bf16[128,2048]{1,0:T(8,128)(2,1)S(1)}, u32[]{:S(2)}) copy-start(bf16[128,2048]{1,0:T(8,128)(2,1)S(1)} %collective-permute-done.2.refs_2_) | copy-start | bytes 1572868
  44.0 13.2 %collective-permute-start.3 = (bf16[128,2048]{1,0:T(8,128)(2,1)S(1)}, bf16[128,2048]{1,0:T(8,128)(2,1)}, u32[]{:S(2)}, u32[]{:S(2)}) collective-permute-start(bf16[128,2048]{1,0:T(8,128)(2,1)S(1)} %collective-permute-done.2.refs_2_), channel_id=1, source_target_pairs={{14,0},{0,2},{2,4},{4,6},{6,8},{8,10},{10,12},{12,14},{15,1},{1,3}... | collective-permute-start | bytes 1572872 | tf_op jit(solution)/shard_map/ppermute | solution.py:164
  46.0 27.0 %copy-start.15 = (f32[2048]{0:T(1024)S(1)}, f32[2048]{0:T(1024)}, u32[]{:S(2)}) copy-start(f32[2048]{0:T(1024)} %param.11) | copy-start | bytes 24580
  46.3 0.6 copy-start.9
  58.9 23.0 %all-to-all-start.1 = ((bf16[12,8,2048]{2,1,0:T(8,128)(2,1)}), bf16[12,8,2048]{2,1,0:T(8,128)(2,1)S(1)}, u32[]{:S(2)}, u32[]{:S(2)}) async-start(bf16[12,8,2048]{2,1,0:T(8,128)(2,1)} %fusion.1), calls=%async_computation.1 | async-start | bytes 786432 | tf_op jit(solution)/shard_map/all_to_all | solution.py:193
  67.7 14.3 %collective-permute-start.4 = (bf16[128,2048]{1,0:T(8,128)(2,1)}, bf16[128,2048]{1,0:T(8,128)(2,1)S(1)}, u32[]{:S(2)}, u32[]{:S(2)}) collective-permute-start(bf16[128,2048]{1,0:T(8,128)(2,1)} %collective-permute-done.1.refs_3_), channel_id=1, source_target_pairs={{2,0},{4,2},{6,4},{8,6},{10,8},{12,10},{14,12},{0,14},{3,1},{5,3},... | collective-permute-start | bytes 1572872 | tf_op jit(solution)/shard_map/ppermute | solution.py:164
  69.6 12.3 %collective-permute-start.5 = (bf16[128,2048]{1,0:T(8,128)(2,1)}, bf16[128,2048]{1,0:T(8,128)(2,1)S(1)}, u32[]{:S(2)}, u32[]{:S(2)}) collective-permute-start(bf16[128,2048]{1,0:T(8,128)(2,1)} %collective-permute-done.3.refs_4_), channel_id=1, source_target_pairs={{14,0},{0,2},{2,4},{4,6},{6,8},{8,10},{10,12},{12,14},{15,1},{1,3}... | collective-permute-start | bytes 1572872 | tf_op jit(solution)/shard_map/ppermute | solution.py:164
  73.1 1.4 %copy-start.11 = (f32[1,2,8,4,32]{4,3,2,1,0:T(4,128)}, f32[1,2,8,4,32]{4,3,2,1,0:T(4,128)S(1)}, u32[]{:S(2)}) copy-start(f32[1,2,8,4,32]{4,3,2,1,0:T(4,128)S(1)} %copy.28) | copy-start | bytes 24580
  74.5 26.2 %collective-permute-start.7 = (bf16[128,2048]{1,0:T(8,128)(2,1)S(1)}, bf16[128,2048]{1,0:T(8,128)(2,1)}, u32[]{:S(2)}, u32[]{:S(2)}) collective-permute-start(bf16[128,2048]{1,0:T(8,128)(2,1)S(1)} %pad_maximum_fusion.grads), channel_id=1, source_target_pairs={{0,1},{1,0},{2,3},{3,2},{4,5},{5,4},{6,7},{7,6},{8,9},{9,8},{10,11... | collective-permute-start | bytes 1572872 | tf_op jit(solution)/shard_map/ppermute | solution.py:203
  84.6 16.2 %collective-permute-start.6 = (bf16[128,1024]{1,0:T(8,128)(2,1)}, bf16[128,1024]{1,0:T(8,128)(2,1)}, u32[]{:S(2)}, u32[]{:S(2)}) collective-permute-start(bf16[128,1024]{1,0:T(8,128)(2,1)} %get-tuple-element.32), channel_id=1, source_target_pairs={{0,1},{1,0},{2,3},{3,2},{4,5},{5,4},{6,7},{7,6},{8,9},{9,8},{10,11... | collective-permute-start | bytes 786440 | tf_op jit(solution)/shard_map/ppermute | solution.py:208
  94.8 12.4 %collective-permute-start.8 = (bf16[64,2048]{1,0:T(8,128)(2,1)}, bf16[64,2048]{1,0:T(8,128)(2,1)}, u32[]{:S(2)}, u32[]{:S(2)}) collective-permute-start(bf16[64,2048]{1,0:T(8,128)(2,1)} %slice.22), channel_id=1, source_target_pairs={{2,0},{4,2},{6,4},{8,6},{10,8},{12,10},{14,12},{0,14},{3,1},{5,3},... | collective-permute-start | bytes 786440 | tf_op jit(solution)/shard_map/ppermute | solution.py:164
  97.4 11.3 %collective-permute-start.9 = (bf16[64,2048]{1,0:T(8,128)(2,1)}, bf16[64,2048]{1,0:T(8,128)(2,1)}, u32[]{:S(2)}, u32[]{:S(2)}) collective-permute-start(bf16[64,2048]{1,0:T(8,128)(2,1)} %slice.23), channel_id=1, source_target_pairs={{14,0},{0,2},{2,4},{4,6},{6,8},{8,10},{10,12},{12,14},{15,1},{1,3}... | collective-permute-start | bytes 786440 | tf_op jit(solution)/shard_map/ppermute | solution.py:164
  100.8 1.0 copy-start.4
  101.8 1.0 copy-start.6
  106.2 1.0 copy-start.1
  108.7 6.8 %copy-start.10 = (f32[1,2,8,4,32]{4,3,2,1,0:T(4,128)S(1)}, f32[1,2,8,4,32]{4,3,2,1,0:T(4,128)}, u32[]{:S(2)}) copy-start(f32[1,2,8,4,32]{4,3,2,1,0:T(4,128)} %copy-done.9) | copy-start | bytes 24580
  108.7 6.9 %copy-start.12 = (f32[1,2,8,4,32]{4,3,2,1,0:T(4,128)S(1)}, f32[1,2,8,4,32]{4,3,2,1,0:T(4,128)}, u32[]{:S(2)}) copy-start(f32[1,2,8,4,32]{4,3,2,1,0:T(4,128)} %copy-done.11) | copy-start | bytes 24580
  112.1 0.7 copy-start.7
  112.8 5.7 %collective-permute-start.10 = (f32[128,2560]{1,0:T(8,128)}, f32[128,2560]{1,0:T(8,128)}, u32[]{:S(2)}, u32[]{:S(2)}) collective-permute-start(f32[128,2560]{1,0:T(8,128)} %get-tuple-element.29), channel_id=1, source_target_pairs={{0,1},{1,0},{2,3},{3,2},{4,5},{5,4},{6,7},{7,6},{8,9},{9,8},{10,11... | collective-permute-start | bytes 3932168 | tf_op jit(solution)/shard_map/ppermute | solution.py:223
  115.7 1.2 %copy-start.2 = (f32[128,2048]{1,0:T(8,128)S(1)}, f32[128,2048]{1,0:T(8,128)}, u32[]{:S(2)}) copy-start(f32[128,2048]{1,0:T(8,128)} %copy-done.1) | copy-start | bytes 3145732
  116.9 1.6 %copy-start.8 = (f32[128,512]{1,0:T(8,128)S(1)}, f32[128,512]{1,0:T(8,128)}, u32[]{:S(2)}) copy-start(f32[128,512]{1,0:T(8,128)} %copy-done.7) | copy-start | bytes 786436

commit v8 on v6

--- a/solution.py
+++ b/solution.py
@@ -67,7 +67,7 @@
         up[row : row + items, to] = back[:items] + back[items : 2 * items]
         to = slice(width + to.start, width + to.stop)
         ready[row : row + items, to] = back[2 * items : 3 * items] + back[3 * items :]
-    parts = len(cuts)
+    parts = out_sems.shape[0] - 1
     ends = [i * width // parts for i in range(parts + 1)] + [send.shape[1]]
     outs = [
         pltpu.make_async_copy(ready.at[:, lo:hi], send.at[:, lo:hi], out_sems.at[i])
@@ -185,7 +185,7 @@
         scratch_shapes=held
         + [
             pltpu.VMEM((hist_rows, width + extra), f32),
-            pltpu.SemaphoreType.DMA((4,)),
+            pltpu.SemaphoreType.DMA((2,)),
             pltpu.SemaphoreType.DMA((5,)),
         ],
         cost_estimate=pl.CostEstimate(flops=3 * flops, bytes_accessed=6 << 20, transcendentals=0),

time: 109 us -> 108 us (level)
  no operation moved by 1% of the time
where the time goes in v8:
time: 108 us; the launch traced here: 107 us
  starting transfers between devices  35.5 us (33%)
  waiting for transfers between devices  28.2 us (26%)
  between operations  14.3 us (13%)
  blocking collectives  13.2 us (12%)
  Pallas kernels  8.89 us (8%)
  other arithmetic  3.61 us (3%)
  matrix products  2 us (2%)
  local copies, waits for them, and re-layouts  1.35 us (1%)
    all_to_all x1, waiting for transfers between devices, local(): lax.all_to_all(sent, 'dp', split_axis=0, concat_axis=0, tiled=True)  14.9 us
    all_to_all x1, starting transfers between devices, local(): lax.all_to_all(sent, 'dp', split_axis=0, concat_axis=0, tiled=True)  14.9 us
    all_gather x1, blocking collectives, local(): seed = lax.all_gather(value_weight, 'x', axis=0, tiled=True)  13.2 us
    all_to_all x1, waiting for transfers between devices, local(): lax.all_to_all(outgoing, 'dp', split_axis=0, concat_axis=0, tiled=True)  10.3 us
    ppermute x1, starting transfers between devices, local(): act_other = lax.ppermute(jnp.where(core == 0, high, low), 'core', swap)  7.15 us
    all_to_all x1, starting transfers between devices, local(): lax.all_to_all(outgoing, 'dp', split_axis=0, concat_axis=0, tiled=True)  6.13 us
    ppermute x1, starting transfers between devices, local(): grads_other = lax.ppermute(grads, 'core', swap)  4.77 us
    pallas_call x1, Pallas kernels, local(): pl.pallas_call(sent_kernel, out_shape=[jax.ShapeDtypeStruct((hist_rows, e...  4.4 us
  transfers between devices with their start and end apart: 6, of which 5 were waited for; matrix products, arithmetic and copies ran while one was open for 6% of the time, Pallas kernels for 2%

profile of v8, /device:TPU:1, one launch (start us, length us, event | category | flops | bytes accessed | tf_op | source)
XLA Modules:
  0.0 107.1 jit_solution(1065827376211260439)
XLA Ops:
  7.2 13.2 %all_gather.6 = bf16[128,2048]{1,0:T(8,128)(2,1)} all-gather(bf16[32,2048]{1,0:T(8,128)(2,1)} %param.12), channel_id=1, replica_groups=mesh['dp'=12,'x'=4,'y'=8,'core'=2] {'x'}, dimensions={0}, use_global_device_ids=true | all-gather | bytes 655360 | tf_op jit(solution)/shard_map/all_gather | solution.py:131
  20.4 0.7 reduce.2
  21.1 0.8 select_reduce_fusion.1
  22.0 0.1 fusion.12
  22.2 0.2 reduce_window_sum.11
  22.6 0.2 select_reduce_fusion
  22.8 0.4 fusion
  23.2 0.8 pad_maximum_fusion.1
  24.0 14.9 %all-to-all-start = ((bf16[12,8,2176]{2,1,0:T(8,128)(2,1)}), bf16[12,8,2176]{2,1,0:T(8,128)(2,1)S(1)}, u32[]{:S(2)}, u32[]{:S(2)}) async-start(bf16[12,8,2176]{2,1,0:T(8,128)(2,1)} %pad_maximum_fusion.1), calls=%async_computation | async-start | bytes 835584 | tf_op jit(solution)/shard_map/all_to_all | solution.py:150
  38.9 0.1 reshape_reshape.6
  39.1 0.3 copy.24
  39.4 0.2 copy.26.hidden
  39.6 0.3 multiply_reduce_fusion
  39.9 0.1 multiply_convert_fusion.item_emb
  40.1 14.9 %all-to-all-done = bf16[12,8,2176]{2,1,0:T(8,128)(2,1)S(1)} async-done(((bf16[12,8,2176]{2,1,0:T(8,128)(2,1)}), bf16[12,8,2176]{2,1,0:T(8,128)(2,1)S(1)}, u32[]{:S(2)}, u32[]{:S(2)}) %all-to-all-start) | async-done | bytes 417824 | tf_op jit(solution)/shard_map/all_to_all | solution.py:150
  55.0 1.0 fusion.1
  56.0 6.1 %all-to-all-start.1 = ((bf16[12,8,2048]{2,1,0:T(8,128)(2,1)}), bf16[12,8,2048]{2,1,0:T(8,128)(2,1)S(1)}, u32[]{:S(2)}, u32[]{:S(2)}) async-start(bf16[12,8,2048]{2,1,0:T(8,128)(2,1)} %fusion.1), calls=%async_computation.1 | async-start | bytes 786432 | tf_op jit(solution)/shard_map/all_to_all | solution.py:159
  62.3 0.3 reduce-precision_convert_fusion
  62.6 4.8 %collective-permute-start.1 = (bf16[128,2048]{1,0:T(8,128)(2,1)S(1)}, bf16[128,2048]{1,0:T(8,128)(2,1)S(1)}, u32[]{:S(2)}, u32[]{:S(2)}) collective-permute-start(bf16[128,2048]{1,0:T(8,128)(2,1)S(1)} %pad_maximum_fusion.grads), channel_id=1, source_target_pairs={{0,1},{1,0},{2,3},{3,2},{4,5},{5,4},{6,7},{7,6},{8,9},{9,8},{10,11... | collective-permute-start | bytes 1572872 | tf_op jit(solution)/shard_map/ppermute | solution.py:165
  67.4 10.3 %all-to-all-done.1 = bf16[12,8,2048]{2,1,0:T(8,128)(2,1)S(1)} async-done(((bf16[12,8,2048]{2,1,0:T(8,128)(2,1)}), bf16[12,8,2048]{2,1,0:T(8,128)(2,1)S(1)}, u32[]{:S(2)}, u32[]{:S(2)}) %all-to-all-start.1) | async-done | bytes 393248 | tf_op jit(solution)/shard_map/all_to_all | solution.py:159
  77.7 0.2 fusion.5
  78.0 0.4 convolution_convert_fusion
  78.4 7.2 %collective-permute-start = (bf16[128,1024]{1,0:T(8,128)(2,1)S(1)}, bf16[128,1024]{1,0:T(8,128)(2,1)S(1)}, u32[]{:S(2)}, u32[]{:S(2)}) collective-permute-start(bf16[128,1024]{1,0:T(8,128)(2,1)S(1)} %get-tuple-element.12), channel_id=1, source_target_pairs={{0,1},{1,0},{2,3},{3,2},{4,5},{5,4},{6,7},{7,6},{8,9},{9,8},{10,11... | collective-permute-start | bytes 786440 | tf_op jit(solution)/shard_map/ppermute | solution.py:170
  85.6 1.1 %collective-permute-done.act_other = bf16[128,1024]{1,0:T(8,128)(2,1)S(1)} collective-permute-done((bf16[128,1024]{1,0:T(8,128)(2,1)S(1)}, bf16[128,1024]{1,0:T(8,128)(2,1)S(1)}, u32[]{:S(2)}, u32[]{:S(2)}) %collective-permute-start) | collective-permute-done | bytes 262176 | tf_op jit(solution)/shard_map/ppermute | solution.py:170
  86.7 1.7 %all-gather.2.cloned.1.call-done.weight = bf16[1024,2048]{1,0:T(8,128)(2,1)} async-done(((bf16[128,2048]{1,0:T(8,128)(2,1)}), bf16[1024,2048]{1,0:T(8,128)(2,1)}) %all-gather.2.cloned.1.call-update) | async-done | bytes 4194320 | tf_op jit(solution)/shard_map/all_gather | solution.py:133
  88.4 4.4 %shard_map.87 = (f32[128,512]{1,0:T(8,128)S(1)}, f32[128,2560]{1,0:T(8,128)}) custom-call(bf16[128,1024]{1,0:T(8,128)(2,1)S(1)} %collective-permute-done.act_other, bf16[128,2048]{1,0:T(8,128)(2,1)S(1)} %pad_maximum_fusion.grads, bf16[128,2048]{1,0:T(8,128)(2,1)S(1)} %collective-permute-done.1.grads_other, bf16[1024,2048]{1,0:T(8,128)(2,1)} %all-gather.2.cloned.1.call-done.weight), custom_call_target="tpu_custom_call" | custom-call | flops 1610612736 | bytes 6291456 | tf_op jit(solution)/shard_map/pallas_call | solution.py:177
  92.8 2.6 %collective-permute-start.2 = (f32[128,2560]{1,0:T(8,128)}, f32[128,2560]{1,0:T(8,128)S(1)}, u32[]{:S(2)}, u32[]{:S(2)}) collective-permute-start(f32[128,2560]{1,0:T(8,128)} %get-tuple-element.9), channel_id=1, source_target_pairs={{0,1},{1,0},{2,3},{3,2},{4,5},{5,4},{6,7},{7,6},{8,9},{9,8},{10,11... | collective-permute-start | bytes 3932168 | tf_op jit(solution)/shard_map/ppermute | solution.py:194
  95.4 0.1 reshape.103.item_gain
  95.5 0.1 reshape.104.user_gain
  95.6 2.5 %shard_map.86.keep = f32[128,2048]{1,0:T(8,128)S(1)} custom-call(bf16[128,1024]{1,0:T(8,128)(2,1)S(1)} %get-tuple-element.13.act, bf16[1024,2048]{1,0:T(8,128)(2,1)} %all-gather.2.cloned.1.call-done.weight), custom_call_target="tpu_custom_call" | custom-call | flops 536870912 | bytes 5242880 | tf_op jit(solution)/shard_map/pallas_call | solution.py:195
  98.1 0.1 collective-permute-done.2.got
  98.3 2.0 %shard_map.88 = (bf16[128,2048]{1,0:T(8,128)(2,1)}, f32[64,2048]{1,0:T(8,128)}) custom-call(s32[1]{0:T(128)} %bitcast.core, f32[128,2048]{1,0:T(8,128)S(1)} %shard_map.86.keep, f32[128,512]{1,0:T(8,128)S(1)} %get-tuple-element.8.sums, f32[128,2560]{1,0:T(8,128)S(1)} %collective-permute-done.2.got, bf16[64,2048]{1,0:T(8,128)(2,1)S(1)} %copy.26.hidden, ...), custom_call_target="tpu_custom_call" | custom-call | tf_op jit(solution)/shard_map/pallas_call | solution.py:204
  (29 shorter events, 0.8 us)
Async XLA Ops:
  7.2 15.6 %copy-start = (bf16[128,2048]{1,0:T(8,128)(2,1)S(1)}, bf16[128,2048]{1,0:T(8,128)(2,1)}, u32[]{:S(2)}) copy-start(bf16[128,2048]{1,0:T(8,128)(2,1)} %param.13) | copy-start | bytes 1572868
  7.2 81.2 %all-gather.2.cloned.1.call-start = ((), (), s32[]{:S(2)}) async-start(), calls=%async_computation.2 | async-start | bytes 4718592 | tf_op jit(solution)/shard_map/all_gather | solution.py:133
  22.5 16.3 %copy-start.2 = (f32[2048]{0:T(1024)S(1)}, f32[2048]{0:T(1024)}, u32[]{:S(2)}) copy-start(f32[2048]{0:T(1024)} %param.8) | copy-start | bytes 24580
  22.8 16.3 %copy-start.1 = (bf16[64,2048]{1,0:T(8,128)(2,1)S(1)}, bf16[64,2048]{1,0:T(8,128)(2,1)}, u32[]{:S(2)}) copy-start(bf16[64,2048]{1,0:T(8,128)(2,1)} %param.7) | copy-start | bytes 786436
  24.0 31.0 %all-to-all-start = ((bf16[12,8,2176]{2,1,0:T(8,128)(2,1)}), bf16[12,8,2176]{2,1,0:T(8,128)(2,1)S(1)}, u32[]{:S(2)}, u32[]{:S(2)}) async-start(bf16[12,8,2176]{2,1,0:T(8,128)(2,1)} %pad_maximum_fusion.1), calls=%async_computation | async-start | bytes 835584 | tf_op jit(solution)/shard_map/all_to_all | solution.py:150
  39.6 22.5 %copy-start.3 = (f32[2048]{0:T(1024)S(1)}, f32[2048]{0:T(1024)}, u32[]{:S(2)}) copy-start(f32[2048]{0:T(1024)} %param.11) | copy-start | bytes 24580
  56.0 21.8 %all-to-all-start.1 = ((bf16[12,8,2048]{2,1,0:T(8,128)(2,1)}), bf16[12,8,2048]{2,1,0:T(8,128)(2,1)S(1)}, u32[]{:S(2)}, u32[]{:S(2)}) async-start(bf16[12,8,2048]{2,1,0:T(8,128)(2,1)} %fusion.1), calls=%async_computation.1 | async-start | bytes 786432 | tf_op jit(solution)/shard_map/all_to_all | solution.py:159
  62.6 23.0 %collective-permute-start.1 = (bf16[128,2048]{1,0:T(8,128)(2,1)S(1)}, bf16[128,2048]{1,0:T(8,128)(2,1)S(1)}, u32[]{:S(2)}, u32[]{:S(2)}) collective-permute-start(bf16[128,2048]{1,0:T(8,128)(2,1)S(1)} %pad_maximum_fusion.grads), channel_id=1, source_target_pairs={{0,1},{1,0},{2,3},{3,2},{4,5},{5,4},{6,7},{7,6},{8,9},{9,8},{10,11... | collective-permute-start | bytes 1572872 | tf_op jit(solution)/shard_map/ppermute | solution.py:165
  78.4 8.3 %collective-permute-start = (bf16[128,1024]{1,0:T(8,128)(2,1)S(1)}, bf16[128,1024]{1,0:T(8,128)(2,1)S(1)}, u32[]{:S(2)}, u32[]{:S(2)}) collective-permute-start(bf16[128,1024]{1,0:T(8,128)(2,1)S(1)} %get-tuple-element.12), channel_id=1, source_target_pairs={{0,1},{1,0},{2,3},{3,2},{4,5},{5,4},{6,7},{7,6},{8,9},{9,8},{10,11... | collective-permute-start | bytes 786440 | tf_op jit(solution)/shard_map/ppermute | solution.py:170
  92.8 5.4 %collective-permute-start.2 = (f32[128,2560]{1,0:T(8,128)}, f32[128,2560]{1,0:T(8,128)S(1)}, u32[]{:S(2)}, u32[]{:S(2)}) collective-permute-start(f32[128,2560]{1,0:T(8,128)} %get-tuple-element.9), channel_id=1, source_target_pairs={{0,1},{1,0},{2,3},{3,2},{4,5},{5,4},{6,7},{7,6},{8,9},{9,8},{10,11... | collective-permute-start | bytes 3932168 | tf_op jit(solution)/shard_map/ppermute | solution.py:194
Sparse Core Ops, SparseCore 0:
  20.6 67.8 all-gather.1

commit v9 on v8

--- a/solution.py
+++ b/solution.py
@@ -92,32 +92,43 @@
     keep[...] = total
 
 
-def last_kernel(core, keep, sums, got, hidden, item_emb, item_gain, user_gain, values, item_grad, up):
-    width = values.shape[1]
-    items = hidden.shape[0]
+def last_kernel(
+    core, keep, sums, got, hidden, item_emb, item_scale, scale, item_gain, user_gain,
+    values, item_grad, ready, up, placed, sems,
+):
+    items, width = placed.shape
     block = sums.shape[1]
     part = width // (NX * NY * NCORE)
     tile = part * NX
-    values[...] = (keep[...] + got[:, :width]).astype(jnp.bfloat16)
+    ready[...] = (keep[...] + got[:, :width]).astype(jnp.bfloat16)
+    copies = [pltpu.make_async_copy(ready, values, sems.at[0])]
+    copies[0].start()
     for side, ref, skip in ((core[0], sums, 0), (1 - core[0], got, width)):
         for piece in range(2):
             at = pl.multiple_of((2 * side + piece) * block, block)
             up[:, pl.ds(at, block)] = ref[piece * items : (piece + 1) * items, skip:]
-    x = item_emb[...].astype(jnp.float32)
-    scale = lax.rsqrt(jnp.mean(x * x, axis=1, keepdims=True) + eps)
-    emb_grad = norm_back(x, user_gain[...], scale, up[...])
-    hid = hidden[...].astype(jnp.float32)
-    scale = lax.rsqrt(jnp.mean(hid * hid, axis=1, keepdims=True) + eps)
-    up[...] = norm_back(hid, item_gain[...], scale, emb_grad)
+    emb_grad = norm_back(item_emb[...].astype(jnp.float32), user_gain[...], scale[...], up[...])
+    up[...] = norm_back(hidden[...].astype(jnp.float32), item_gain[...], item_scale[...], emb_grad)
     group = lax.broadcasted_iota(jnp.int32, (items, tile), 1) // part
-    for out in range(width // tile):
+    outs = width // tile
+    for out in range(outs):
         at_x, y = out // (NY // 2), 2 * (out % (NY // 2))
         total = None
         for to, (side, at_y) in enumerate(((0, y), (1, y), (0, y + 1), (1, y + 1))):
             piece = up[:, (side * NY + at_y) * tile : (side * NY + at_y + 1) * tile]
             piece = pltpu.roll(piece, (to - at_x) % NX * part, 1)
             total = piece if total is None else jnp.where(group == to, piece, total)
-        item_grad[:, out * tile : (out + 1) * tile] = total
+        placed[:, out * tile : (out + 1) * tile] = total
+        if out % (outs // 2) == outs // 2 - 1:
+            half = slice(out // (outs // 2) * (width // 2), (out + 1) * tile)
+            copies.append(
+                pltpu.make_async_copy(
+                    placed.at[:, half], item_grad.at[:, half], sems.at[len(copies)]
+                )
+            )
+            copies[-1].start()
+    for copy in copies:
+        copy.wait()
 
 
 def local(item_hidden, item_gain, history, owner_map, user_gain, value_weight, value_grad):
@@ -153,8 +164,9 @@
 
     hidden = split(item_hidden)
     item_gain, user_gain = split(item_gain.reshape(1, width)), split(user_gain.reshape(1, width))
-    item_emb, _ = norm_rows(hidden.astype(f32), item_gain)
+    item_emb, item_scale = norm_rows(hidden.astype(f32), item_gain)
     item_emb = item_emb.astype(bf16)
+    _, scale = norm_rows(item_emb.astype(f32), user_gain)
     outgoing = dot(select, item_emb).astype(bf16).reshape(groups, CAP, width)
     incoming = lax.all_to_all(outgoing, "dp", split_axis=0, concat_axis=0, tiled=True)
 
@@ -207,11 +219,19 @@
             jax.ShapeDtypeStruct((hist_rows, width), bf16),
             jax.ShapeDtypeStruct((item_rows, width), f32),
         ],
-        in_specs=[pl.BlockSpec(memory_space=pltpu.SMEM)] + [vmem] * 7,
-        out_specs=[vmem] * 2,
-        scratch_shapes=[pltpu.VMEM((item_rows, width), f32)],
+        in_specs=[pl.BlockSpec(memory_space=pltpu.SMEM)] + [vmem] * 9,
+        out_specs=[hbm] * 2,
+        scratch_shapes=[
+            pltpu.VMEM((hist_rows, width), bf16),
+            pltpu.VMEM((item_rows, width), f32),
+            pltpu.VMEM((item_rows, width), f32),
+            pltpu.SemaphoreType.DMA((3,)),
+        ],
         compiler_params=pltpu.CompilerParams(vmem_limit_bytes=12 << 20),
-    )(core.reshape(1).astype(jnp.int32), keep, sums, got, hidden, item_emb, item_gain, user_gain)
+    )(
+        core.reshape(1).astype(jnp.int32), keep, sums, got, hidden, item_emb, item_scale, scale,
+        item_gain, user_gain,
+    )
     return (values, item_grad)
 
 

time: 108 us -> 109 us (level)
  waiting for transfers between devices: 28.2 us -> 25.9 us
  other arithmetic: 3.61 us -> 4.97 us
  matrix products: 2 us -> 3.19 us
    all_gather x1, waiting for transfers between devices: 1.69 us -> 0.03 us  [local(): weight = lax.all_gather(seed, 'y', axis=0, tiled=True)]
    dot_general x4, matrix products: 2 us -> 3.19 us  [dot(): lax.dot_general(a, b, (((da,), (db,)), ((), ())), preferred_element_type=...]
  transfers between devices with their start and end apart: 6 -> 6, of which waited for: 5 -> 3; matrix products, arithmetic and copies ran while one was open for 6% -> 10% of each run, Pallas kernels for 2% -> 2%
where the time goes in v9:
time: 109 us; the launch traced here: 108 us
  starting transfers between devices  35.5 us (33%)
  waiting for transfers between devices  25.9 us (24%)
  between operations  14.3 us (13%)
  blocking collectives  13.2 us (12%)
  Pallas kernels  8.68 us (8%)
  other arithmetic  4.97 us (5%)
  matrix products  3.19 us (3%)
  local copies, waits for them, and re-layouts  2.21 us (2%)
    all_to_all x1, starting transfers between devices, local(): lax.all_to_all(sent, 'dp', split_axis=0, concat_axis=0, tiled=True)  14.9 us
    all_to_all x1, waiting for transfers between devices, local(): lax.all_to_all(sent, 'dp', split_axis=0, concat_axis=0, tiled=True)  14.4 us
    all_gather x1, blocking collectives, local(): seed = lax.all_gather(value_weight, 'x', axis=0, tiled=True)  13.2 us
    all_to_all x1, waiting for transfers between devices, local(): lax.all_to_all(outgoing, 'dp', split_axis=0, concat_axis=0, tiled=True)  10.3 us
    ppermute x1, starting transfers between devices, local(): act_other = lax.ppermute(jnp.where(core == 0, high, low), 'core', swap)  7.15 us
    all_to_all x1, starting transfers between devices, local(): lax.all_to_all(outgoing, 'dp', split_axis=0, concat_axis=0, tiled=True)  6.13 us
    ppermute x1, starting transfers between devices, local(): grads_other = lax.ppermute(grads, 'core', swap)  4.77 us
    pallas_call x1, Pallas kernels, local(): pl.pallas_call(sent_kernel, out_shape=[jax.ShapeDtypeStruct((hist_rows, e...  4.4 us
  transfers between devices with their start and end apart: 6, of which 3 were waited for; matrix products, arithmetic and copies ran while one was open for 10% of the time, Pallas kernels for 2%

profile of v9, /device:TPU:1, one launch (start us, length us, event | category | flops | bytes accessed | tf_op | source)
XLA Modules:
  0.0 108.0 jit_solution(11082871363911620140)
XLA Ops:
  7.2 13.2 %all_gather.6 = bf16[128,2048]{1,0:T(8,128)(2,1)} all-gather(bf16[32,2048]{1,0:T(8,128)(2,1)} %param.12), channel_id=1, replica_groups=mesh['dp'=12,'x'=4,'y'=8,'core'=2] {'x'}, dimensions={0}, use_global_device_ids=true | all-gather | bytes 655360 | tf_op jit(solution)/shard_map/all_gather | solution.py:142
  20.4 0.7 reduce.3
  21.1 0.8 select_reduce_fusion.1
  22.0 0.1 fusion.15
  22.2 0.2 reduce_window_sum.11
  22.6 0.2 select_reduce_fusion
  22.8 0.5 multiply_add_fusion
  23.3 1.0 fusion
  24.3 0.8 pad_maximum_fusion.1
  25.1 14.9 %all-to-all-start = ((bf16[12,8,2176]{2,1,0:T(8,128)(2,1)}), bf16[12,8,2176]{2,1,0:T(8,128)(2,1)S(1)}, u32[]{:S(2)}, u32[]{:S(2)}) async-start(bf16[12,8,2176]{2,1,0:T(8,128)(2,1)} %pad_maximum_fusion.1), calls=%async_computation | async-start | bytes 835584 | tf_op jit(solution)/shard_map/all_to_all | solution.py:161
  40.1 0.3 copy.30
  40.5 0.2 copy.32.hidden
  40.7 0.3 fusion.2
  41.0 0.5 fusion.21
  41.5 0.1 multiply_convert_fusion.item_emb
  41.6 14.4 %all-to-all-done = bf16[12,8,2176]{2,1,0:T(8,128)(2,1)S(1)} async-done(((bf16[12,8,2176]{2,1,0:T(8,128)(2,1)}), bf16[12,8,2176]{2,1,0:T(8,128)(2,1)S(1)}, u32[]{:S(2)}, u32[]{:S(2)}) %all-to-all-start) | async-done | bytes 417824 | tf_op jit(solution)/shard_map/all_to_all | solution.py:161
  56.1 1.0 fusion.1
  57.1 6.1 %all-to-all-start.1 = ((bf16[12,8,2048]{2,1,0:T(8,128)(2,1)}), bf16[12,8,2048]{2,1,0:T(8,128)(2,1)S(1)}, u32[]{:S(2)}, u32[]{:S(2)}) async-start(bf16[12,8,2048]{2,1,0:T(8,128)(2,1)} %fusion.1), calls=%async_computation.1 | async-start | bytes 786432 | tf_op jit(solution)/shard_map/all_to_all | solution.py:171
  63.4 0.3 reduce-precision_convert_fusion
  63.7 4.8 %collective-permute-start.1 = (bf16[128,2048]{1,0:T(8,128)(2,1)S(1)}, bf16[128,2048]{1,0:T(8,128)(2,1)S(1)}, u32[]{:S(2)}, u32[]{:S(2)}) collective-permute-start(bf16[128,2048]{1,0:T(8,128)(2,1)S(1)} %pad_maximum_fusion.grads), channel_id=1, source_target_pairs={{0,1},{1,0},{2,3},{3,2},{4,5},{5,4},{6,7},{7,6},{8,9},{9,8},{10,11... | collective-permute-start | bytes 1572872 | tf_op jit(solution)/shard_map/ppermute | solution.py:177
  68.5 10.3 %all-to-all-done.1 = bf16[12,8,2048]{2,1,0:T(8,128)(2,1)S(1)} async-done(((bf16[12,8,2048]{2,1,0:T(8,128)(2,1)}), bf16[12,8,2048]{2,1,0:T(8,128)(2,1)S(1)}, u32[]{:S(2)}, u32[]{:S(2)}) %all-to-all-start.1) | async-done | bytes 393248 | tf_op jit(solution)/shard_map/all_to_all | solution.py:171
  78.8 0.2 fusion.8
  79.1 0.9 convolution_convert_fusion
  80.1 7.2 %collective-permute-start = (bf16[128,1024]{1,0:T(8,128)(2,1)S(1)}, bf16[128,1024]{1,0:T(8,128)(2,1)S(1)}, u32[]{:S(2)}, u32[]{:S(2)}) collective-permute-start(bf16[128,1024]{1,0:T(8,128)(2,1)S(1)} %get-tuple-element.12), channel_id=1, source_target_pairs={{0,1},{1,0},{2,3},{3,2},{4,5},{5,4},{6,7},{7,6},{8,9},{9,8},{10,11... | collective-permute-start | bytes 786440 | tf_op jit(solution)/shard_map/ppermute | solution.py:182
  87.3 1.1 %collective-permute-done.act_other = bf16[128,1024]{1,0:T(8,128)(2,1)S(1)} collective-permute-done((bf16[128,1024]{1,0:T(8,128)(2,1)S(1)}, bf16[128,1024]{1,0:T(8,128)(2,1)S(1)}, u32[]{:S(2)}, u32[]{:S(2)}) %collective-permute-start) | collective-permute-done | bytes 262176 | tf_op jit(solution)/shard_map/ppermute | solution.py:182
  88.4 4.4 %shard_map.87 = (f32[128,512]{1,0:T(8,128)S(1)}, f32[128,2560]{1,0:T(8,128)}) custom-call(bf16[128,1024]{1,0:T(8,128)(2,1)S(1)} %collective-permute-done.act_other, bf16[128,2048]{1,0:T(8,128)(2,1)S(1)} %pad_maximum_fusion.grads, bf16[128,2048]{1,0:T(8,128)(2,1)S(1)} %collective-permute-done.1.grads_other, bf16[1024,2048]{1,0:T(8,128)(2,1)} %all-gather.2.cloned.1.call-done.weight), custom_call_target="tpu_custom_call" | custom-call | flops 1610612736 | bytes 6291456 | tf_op jit(solution)/shard_map/pallas_call | solution.py:189
  92.8 2.6 %collective-permute-start.2 = (f32[128,2560]{1,0:T(8,128)}, f32[128,2560]{1,0:T(8,128)S(1)}, u32[]{:S(2)}, u32[]{:S(2)}) collective-permute-start(f32[128,2560]{1,0:T(8,128)} %get-tuple-element.9), channel_id=1, source_target_pairs={{0,1},{1,0},{2,3},{3,2},{4,5},{5,4},{6,7},{7,6},{8,9},{9,8},{10,11... | collective-permute-start | bytes 3932168 | tf_op jit(solution)/shard_map/ppermute | solution.py:206
  95.6 0.4 multiply_reduce_fusion
  96.0 0.1 copy.39.scale
  96.1 0.8 copy.38.item_scale
  96.8 2.5 %shard_map.86.keep = f32[128,2048]{1,0:T(8,128)S(1)} custom-call(bf16[128,1024]{1,0:T(8,128)(2,1)S(1)} %get-tuple-element.13.act, bf16[1024,2048]{1,0:T(8,128)(2,1)} %all-gather.2.cloned.1.call-done.weight), custom_call_target="tpu_custom_call" | custom-call | flops 536870912 | bytes 5242880 | tf_op jit(solution)/shard_map/pallas_call | solution.py:207
  99.4 1.8 %shard_map.88 = (bf16[128,2048]{1,0:T(8,128)(2,1)}, f32[64,2048]{1,0:T(8,128)}) custom-call(s32[1]{0:T(128)} %bitcast.core, f32[128,2048]{1,0:T(8,128)S(1)} %shard_map.86.keep, f32[128,512]{1,0:T(8,128)S(1)} %get-tuple-element.8.sums, f32[128,2560]{1,0:T(8,128)S(1)} %collective-permute-done.2.got, bf16[64,2048]{1,0:T(8,128)(2,1)S(1)} %copy.32.hidden, ...), custom_call_target="tpu_custom_call" | custom-call | tf_op jit(solution)/shard_map/pallas_call | solution.py:216
  (37 shorter events, 1.1 us)
Async XLA Ops:
  7.2 16.1 %copy-start = (bf16[128,2048]{1,0:T(8,128)(2,1)S(1)}, bf16[128,2048]{1,0:T(8,128)(2,1)}, u32[]{:S(2)}) copy-start(bf16[128,2048]{1,0:T(8,128)(2,1)} %param.13) | copy-start | bytes 1572868
  7.2 81.3 %all-gather.2.cloned.1.call-start = ((), (), s32[]{:S(2)}) async-start(), calls=%async_computation.2 | async-start | bytes 4718592 | tf_op jit(solution)/shard_map/all_gather | solution.py:144
  22.5 17.4 %copy-start.2 = (f32[2048]{0:T(1024)S(1)}, f32[2048]{0:T(1024)}, u32[]{:S(2)}) copy-start(f32[2048]{0:T(1024)} %param.8) | copy-start | bytes 24580
  23.3 16.9 %copy-start.1 = (bf16[64,2048]{1,0:T(8,128)(2,1)S(1)}, bf16[64,2048]{1,0:T(8,128)(2,1)}, u32[]{:S(2)}) copy-start(bf16[64,2048]{1,0:T(8,128)(2,1)} %param.7) | copy-start | bytes 786436
  25.1 31.0 %all-to-all-start = ((bf16[12,8,2176]{2,1,0:T(8,128)(2,1)}), bf16[12,8,2176]{2,1,0:T(8,128)(2,1)S(1)}, u32[]{:S(2)}, u32[]{:S(2)}) async-start(bf16[12,8,2176]{2,1,0:T(8,128)(2,1)} %pad_maximum_fusion.1), calls=%async_computation | async-start | bytes 835584 | tf_op jit(solution)/shard_map/all_to_all | solution.py:161
  40.7 22.5 %copy-start.3 = (f32[2048]{0:T(1024)S(1)}, f32[2048]{0:T(1024)}, u32[]{:S(2)}) copy-start(f32[2048]{0:T(1024)} %param.11) | copy-start | bytes 24580
  41.5 22.2 %copy-start.4 = (f32[64]{0:T(128)}, f32[64]{0:T(128)S(1)}, u32[]{:S(2)}) copy-start(f32[64]{0:T(128)S(1)} %get-tuple-element.15) | copy-start | bytes 772
  57.1 21.8 %all-to-all-start.1 = ((bf16[12,8,2048]{2,1,0:T(8,128)(2,1)}), bf16[12,8,2048]{2,1,0:T(8,128)(2,1)S(1)}, u32[]{:S(2)}, u32[]{:S(2)}) async-start(bf16[12,8,2048]{2,1,0:T(8,128)(2,1)} %fusion.1), calls=%async_computation.1 | async-start | bytes 786432 | tf_op jit(solution)/shard_map/all_to_all | solution.py:171
  63.7 23.5 %collective-permute-start.1 = (bf16[128,2048]{1,0:T(8,128)(2,1)S(1)}, bf16[128,2048]{1,0:T(8,128)(2,1)S(1)}, u32[]{:S(2)}, u32[]{:S(2)}) collective-permute-start(bf16[128,2048]{1,0:T(8,128)(2,1)S(1)} %pad_maximum_fusion.grads), channel_id=1, source_target_pairs={{0,1},{1,0},{2,3},{3,2},{4,5},{5,4},{6,7},{7,6},{8,9},{9,8},{10,11... | collective-permute-start | bytes 1572872 | tf_op jit(solution)/shard_map/ppermute | solution.py:177
  80.1 15.5 %copy-start.5 = (f32[64]{0:T(128)S(1)}, f32[64]{0:T(128)}, u32[]{:S(2)}) copy-start(f32[64]{0:T(128)} %copy-done.4) | copy-start | bytes 772
  80.1 8.3 %collective-permute-start = (bf16[128,1024]{1,0:T(8,128)(2,1)S(1)}, bf16[128,1024]{1,0:T(8,128)(2,1)S(1)}, u32[]{:S(2)}, u32[]{:S(2)}) collective-permute-start(bf16[128,1024]{1,0:T(8,128)(2,1)S(1)} %get-tuple-element.12), channel_id=1, source_target_pairs={{0,1},{1,0},{2,3},{3,2},{4,5},{5,4},{6,7},{7,6},{8,9},{9,8},{10,11... | collective-permute-start | bytes 786440 | tf_op jit(solution)/shard_map/ppermute | solution.py:182
  92.8 6.5 %collective-permute-start.2 = (f32[128,2560]{1,0:T(8,128)}, f32[128,2560]{1,0:T(8,128)S(1)}, u32[]{:S(2)}, u32[]{:S(2)}) collective-permute-start(f32[128,2560]{1,0:T(8,128)} %get-tuple-element.9), channel_id=1, source_target_pairs={{0,1},{1,0},{2,3},{3,2},{4,5},{5,4},{6,7},{7,6},{8,9},{9,8},{10,11... | collective-permute-start | bytes 3932168 | tf_op jit(solution)/shard_map/ppermute | solution.py:206
Sparse Core Ops, SparseCore 0:
  20.6 67.8 all-gather.1

commit v10 on v8

--- a/solution.py
+++ b/solution.py
@@ -57,16 +57,16 @@
 def sent_kernel(act_other, grads, grads_other, weight, up, send, held, ready, sems, out_sems):
     cuts, copies = fetch(weight, held, sems)
     half, width = held.shape
-    items = grads.shape[0] // 2
+    items = grads.shape[0]
     both = jnp.concatenate([grads[...], grads_other[...]], axis=0)
     for cut, copy in zip(cuts, copies):
         copy.wait()
         back = dot(both, held[cut], 1, 1)
         row, column = divmod(cut.start, half // 2)
         row, to = row * items, slice(column, column + cut.stop - cut.start)
-        up[row : row + items, to] = back[:items] + back[items : 2 * items]
+        up[row : row + items, to] = back[:items]
         to = slice(width + to.start, width + to.stop)
-        ready[row : row + items, to] = back[2 * items : 3 * items] + back[3 * items :]
+        ready[row : row + items, to] = back[items:]
     parts = out_sems.shape[0] - 1
     ends = [i * width // parts for i in range(parts + 1)] + [send.shape[1]]
     outs = [
@@ -160,8 +160,7 @@
 
     swap = [(0, 1), (1, 0)]
     total = dot(select, arrived[:, :width], 0, 0)
-    high = lax.reduce_precision(total, 8, 7)
-    grads = jnp.concatenate([high, total - high], axis=0).astype(bf16)
+    grads = total.astype(bf16)
     grads_other = lax.ppermute(grads, "core", swap)
     normed, _ = norm_rows(incoming.reshape(groups * CAP, width).astype(f32), user_gain)
     normed = dot(one_hot, normed.astype(bf16)).astype(bf16)

time: 108 us -> 108 us (level)
  no operation moved by 1% of the time
where the time goes in v10:
time: 108 us; the launch traced here: 107 us
  starting transfers between devices  35.6 us (33%)
  waiting for transfers between devices  28.3 us (26%)
  between operations  14.3 us (13%)
  blocking collectives  13.2 us (12%)
  Pallas kernels  9.05 us (8%)
  other arithmetic  3.57 us (3%)
  matrix products  1.99 us (2%)
  local copies, waits for them, and re-layouts  1.35 us (1%)
    all_to_all x1, waiting for transfers between devices, local(): lax.all_to_all(sent, 'dp', split_axis=0, concat_axis=0, tiled=True)  14.9 us
    all_to_all x1, starting transfers between devices, local(): lax.all_to_all(sent, 'dp', split_axis=0, concat_axis=0, tiled=True)  14.9 us
    all_gather x1, blocking collectives, local(): seed = lax.all_gather(value_weight, 'x', axis=0, tiled=True)  13.2 us
    all_to_all x1, waiting for transfers between devices, local(): lax.all_to_all(outgoing, 'dp', split_axis=0, concat_axis=0, tiled=True)  10.4 us
    ppermute x1, starting transfers between devices, local(): act_other = lax.ppermute(jnp.where(core == 0, high, low), 'core', swap)  7.15 us
    all_to_all x1, starting transfers between devices, local(): lax.all_to_all(outgoing, 'dp', split_axis=0, concat_axis=0, tiled=True)  6.13 us
    ppermute x1, starting transfers between devices, local(): grads_other = lax.ppermute(grads, 'core', swap)  4.77 us
    pallas_call x1, Pallas kernels, local(): pl.pallas_call(sent_kernel, out_shape=[jax.ShapeDtypeStruct((hist_rows, e...  4.56 us
  transfers between devices with their start and end apart: 6, of which 5 were waited for; matrix products, arithmetic and copies ran while one was open for 6% of the time, Pallas kernels for 2%

profile of v10, /device:TPU:1, one launch (start us, length us, event | category | flops | bytes accessed | tf_op | source)
XLA Modules:
  0.0 107.3 jit_solution(1077976549985161204)
XLA Ops:
  7.2 13.2 %all_gather.6 = bf16[128,2048]{1,0:T(8,128)(2,1)} all-gather(bf16[32,2048]{1,0:T(8,128)(2,1)} %param.12), channel_id=1, replica_groups=mesh['dp'=12,'x'=4,'y'=8,'core'=2] {'x'}, dimensions={0}, use_global_device_ids=true | all-gather | bytes 655360 | tf_op jit(solution)/shard_map/all_gather | solution.py:131
  20.4 0.7 reduce.2
  21.1 0.8 select_reduce_fusion.1
  22.0 0.1 fusion.10
  22.2 0.2 reduce_window_sum.11
  22.6 0.2 select_reduce_fusion
  22.8 0.4 fusion
  23.2 0.8 pad_maximum_fusion
  24.0 14.9 %all-to-all-start = ((bf16[12,8,2176]{2,1,0:T(8,128)(2,1)}), bf16[12,8,2176]{2,1,0:T(8,128)(2,1)S(1)}, u32[]{:S(2)}, u32[]{:S(2)}) async-start(bf16[12,8,2176]{2,1,0:T(8,128)(2,1)} %pad_maximum_fusion), calls=%async_computation | async-start | bytes 835584 | tf_op jit(solution)/shard_map/all_to_all | solution.py:150
  38.9 0.1 reshape_reshape.6
  39.1 0.3 copy.24
  39.4 0.2 copy.26.hidden
  39.6 0.3 multiply_reduce_fusion
  39.9 0.1 multiply_convert_fusion.item_emb
  40.1 14.9 %all-to-all-done = bf16[12,8,2176]{2,1,0:T(8,128)(2,1)S(1)} async-done(((bf16[12,8,2176]{2,1,0:T(8,128)(2,1)}), bf16[12,8,2176]{2,1,0:T(8,128)(2,1)S(1)}, u32[]{:S(2)}, u32[]{:S(2)}) %all-to-all-start) | async-done | bytes 417824 | tf_op jit(solution)/shard_map/all_to_all | solution.py:150
  55.0 1.0 fusion.1
  56.0 6.1 %all-to-all-start.1 = ((bf16[12,8,2048]{2,1,0:T(8,128)(2,1)}), bf16[12,8,2048]{2,1,0:T(8,128)(2,1)S(1)}, u32[]{:S(2)}, u32[]{:S(2)}) async-start(bf16[12,8,2048]{2,1,0:T(8,128)(2,1)} %fusion.1), calls=%async_computation.1 | async-start | bytes 786432 | tf_op jit(solution)/shard_map/all_to_all | solution.py:159
  62.3 0.2 convolution_convert_fusion.3.grads
  62.6 4.8 %collective-permute-start.1 = (bf16[64,2048]{1,0:T(8,128)(2,1)S(1)}, bf16[64,2048]{1,0:T(8,128)(2,1)S(1)}, u32[]{:S(2)}, u32[]{:S(2)}) collective-permute-start(bf16[64,2048]{1,0:T(8,128)(2,1)S(1)} %convolution_convert_fusion.3.grads), channel_id=1, source_target_pairs={{0,1},{1,0},{2,3},{3,2},{4,5},{5,4},{6,7},{7,6},{8,9},{9,8},{10,11... | collective-permute-start | bytes 786440 | tf_op jit(solution)/shard_map/ppermute | solution.py:164
  67.4 10.4 %all-to-all-done.1 = bf16[12,8,2048]{2,1,0:T(8,128)(2,1)S(1)} async-done(((bf16[12,8,2048]{2,1,0:T(8,128)(2,1)}), bf16[12,8,2048]{2,1,0:T(8,128)(2,1)S(1)}, u32[]{:S(2)}, u32[]{:S(2)}) %all-to-all-start.1) | async-done | bytes 393248 | tf_op jit(solution)/shard_map/all_to_all | solution.py:159
  77.7 0.2 fusion.5
  78.0 0.4 convolution_convert_fusion
  78.4 7.2 %collective-permute-start = (bf16[128,1024]{1,0:T(8,128)(2,1)S(1)}, bf16[128,1024]{1,0:T(8,128)(2,1)S(1)}, u32[]{:S(2)}, u32[]{:S(2)}) collective-permute-start(bf16[128,1024]{1,0:T(8,128)(2,1)S(1)} %get-tuple-element.10), channel_id=1, source_target_pairs={{0,1},{1,0},{2,3},{3,2},{4,5},{5,4},{6,7},{7,6},{8,9},{9,8},{10,11... | collective-permute-start | bytes 786440 | tf_op jit(solution)/shard_map/ppermute | solution.py:169
  85.6 1.1 %collective-permute-done.act_other = bf16[128,1024]{1,0:T(8,128)(2,1)S(1)} collective-permute-done((bf16[128,1024]{1,0:T(8,128)(2,1)S(1)}, bf16[128,1024]{1,0:T(8,128)(2,1)S(1)}, u32[]{:S(2)}, u32[]{:S(2)}) %collective-permute-start) | collective-permute-done | bytes 262176 | tf_op jit(solution)/shard_map/ppermute | solution.py:169
  86.7 1.7 %all-gather.2.cloned.1.call-done.weight = bf16[1024,2048]{1,0:T(8,128)(2,1)} async-done(((bf16[128,2048]{1,0:T(8,128)(2,1)}), bf16[1024,2048]{1,0:T(8,128)(2,1)}) %all-gather.2.cloned.1.call-update) | async-done | bytes 4194320 | tf_op jit(solution)/shard_map/all_gather | solution.py:133
  88.4 4.6 %shard_map.87 = (f32[128,512]{1,0:T(8,128)S(1)}, f32[128,2560]{1,0:T(8,128)}) custom-call(bf16[128,1024]{1,0:T(8,128)(2,1)S(1)} %collective-permute-done.act_other, bf16[64,2048]{1,0:T(8,128)(2,1)S(1)} %convolution_convert_fusion.3.grads, bf16[64,2048]{1,0:T(8,128)(2,1)S(1)} %collective-permute-done.1.grads_other, ...), custom_call_target="tpu_custom_call" | custom-call | flops 1610612736 | bytes 6291456 | tf_op jit(solution)/shard_map/pallas_call | solution.py:176
  93.0 2.6 %collective-permute-start.2 = (f32[128,2560]{1,0:T(8,128)}, f32[128,2560]{1,0:T(8,128)S(1)}, u32[]{:S(2)}, u32[]{:S(2)}) collective-permute-start(f32[128,2560]{1,0:T(8,128)} %get-tuple-element.9), channel_id=1, source_target_pairs={{0,1},{1,0},{2,3},{3,2},{4,5},{5,4},{6,7},{7,6},{8,9},{9,8},{10,11... | collective-permute-start | bytes 3932168 | tf_op jit(solution)/shard_map/ppermute | solution.py:193
  95.6 0.1 reshape.103.item_gain
  95.7 0.1 reshape.104.user_gain
  95.8 2.5 %shard_map.86.keep = f32[128,2048]{1,0:T(8,128)S(1)} custom-call(bf16[128,1024]{1,0:T(8,128)(2,1)S(1)} %get-tuple-element.11.act, bf16[1024,2048]{1,0:T(8,128)(2,1)} %all-gather.2.cloned.1.call-done.weight), custom_call_target="tpu_custom_call" | custom-call | flops 536870912 | bytes 5242880 | tf_op jit(solution)/shard_map/pallas_call | solution.py:194
  98.3 0.1 collective-permute-done.2.got
  98.4 2.0 %shard_map.88 = (bf16[128,2048]{1,0:T(8,128)(2,1)}, f32[64,2048]{1,0:T(8,128)}) custom-call(s32[1]{0:T(128)} %bitcast.core, f32[128,2048]{1,0:T(8,128)S(1)} %shard_map.86.keep, f32[128,512]{1,0:T(8,128)S(1)} %get-tuple-element.8.sums, f32[128,2560]{1,0:T(8,128)S(1)} %collective-permute-done.2.got, bf16[64,2048]{1,0:T(8,128)(2,1)S(1)} %copy.26.hidden, ...), custom_call_target="tpu_custom_call" | custom-call | tf_op jit(solution)/shard_map/pallas_call | solution.py:203
  (28 shorter events, 0.8 us)
Async XLA Ops:
  7.2 15.6 %copy-start = (bf16[128,2048]{1,0:T(8,128)(2,1)S(1)}, bf16[128,2048]{1,0:T(8,128)(2,1)}, u32[]{:S(2)}) copy-start(bf16[128,2048]{1,0:T(8,128)(2,1)} %param.13) | copy-start | bytes 1572868
  7.2 81.2 %all-gather.2.cloned.1.call-start = ((), (), s32[]{:S(2)}) async-start(), calls=%async_computation.2 | async-start | bytes 4718592 | tf_op jit(solution)/shard_map/all_gather | solution.py:133
  22.5 16.3 %copy-start.2 = (f32[2048]{0:T(1024)S(1)}, f32[2048]{0:T(1024)}, u32[]{:S(2)}) copy-start(f32[2048]{0:T(1024)} %param.8) | copy-start | bytes 24580
  22.8 16.3 %copy-start.1 = (bf16[64,2048]{1,0:T(8,128)(2,1)S(1)}, bf16[64,2048]{1,0:T(8,128)(2,1)}, u32[]{:S(2)}) copy-start(bf16[64,2048]{1,0:T(8,128)(2,1)} %param.7) | copy-start | bytes 786436
  24.0 31.0 %all-to-all-start = ((bf16[12,8,2176]{2,1,0:T(8,128)(2,1)}), bf16[12,8,2176]{2,1,0:T(8,128)(2,1)S(1)}, u32[]{:S(2)}, u32[]{:S(2)}) async-start(bf16[12,8,2176]{2,1,0:T(8,128)(2,1)} %pad_maximum_fusion), calls=%async_computation | async-start | bytes 835584 | tf_op jit(solution)/shard_map/all_to_all | solution.py:150
  39.6 22.5 %copy-start.3 = (f32[2048]{0:T(1024)S(1)}, f32[2048]{0:T(1024)}, u32[]{:S(2)}) copy-start(f32[2048]{0:T(1024)} %param.11) | copy-start | bytes 24580
  56.0 21.8 %all-to-all-start.1 = ((bf16[12,8,2048]{2,1,0:T(8,128)(2,1)}), bf16[12,8,2048]{2,1,0:T(8,128)(2,1)S(1)}, u32[]{:S(2)}, u32[]{:S(2)}) async-start(bf16[12,8,2048]{2,1,0:T(8,128)(2,1)} %fusion.1), calls=%async_computation.1 | async-start | bytes 786432 | tf_op jit(solution)/shard_map/all_to_all | solution.py:159
  62.6 23.0 %collective-permute-start.1 = (bf16[64,2048]{1,0:T(8,128)(2,1)S(1)}, bf16[64,2048]{1,0:T(8,128)(2,1)S(1)}, u32[]{:S(2)}, u32[]{:S(2)}) collective-permute-start(bf16[64,2048]{1,0:T(8,128)(2,1)S(1)} %convolution_convert_fusion.3.grads), channel_id=1, source_target_pairs={{0,1},{1,0},{2,3},{3,2},{4,5},{5,4},{6,7},{7,6},{8,9},{9,8},{10,11... | collective-permute-start | bytes 786440 | tf_op jit(solution)/shard_map/ppermute | solution.py:164
  78.4 8.3 %collective-permute-start = (bf16[128,1024]{1,0:T(8,128)(2,1)S(1)}, bf16[128,1024]{1,0:T(8,128)(2,1)S(1)}, u32[]{:S(2)}, u32[]{:S(2)}) collective-permute-start(bf16[128,1024]{1,0:T(8,128)(2,1)S(1)} %get-tuple-element.10), channel_id=1, source_target_pairs={{0,1},{1,0},{2,3},{3,2},{4,5},{5,4},{6,7},{7,6},{8,9},{9,8},{10,11... | collective-permute-start | bytes 786440 | tf_op jit(solution)/shard_map/ppermute | solution.py:169
  93.0 5.4 %collective-permute-start.2 = (f32[128,2560]{1,0:T(8,128)}, f32[128,2560]{1,0:T(8,128)S(1)}, u32[]{:S(2)}, u32[]{:S(2)}) collective-permute-start(f32[128,2560]{1,0:T(8,128)} %get-tuple-element.9), channel_id=1, source_target_pairs={{0,1},{1,0},{2,3},{3,2},{4,5},{5,4},{6,7},{7,6},{8,9},{9,8},{10,11... | collective-permute-start | bytes 3932168 | tf_op jit(solution)/shard_map/ppermute | solution.py:193
Sparse Core Ops, SparseCore 0:
  20.6 67.8 all-gather.1
